TPU v7x, 128 devices: a whole 4x4x4 slice. The times are simulated.
128 devices in a mesh: ctx: 16 (over z_lo, y, core), fsdp: 8 (over x, z_hi).
Axes of the slice: x: 4, y: 4, z: 4 (z_hi: 2, z_lo: 2; z = z_hi * 2 + z_lo), core: 2. Of those that a mesh axis runs over, the one named last changes fastest.
Arguments:
- tokens_in: bfloat16 [8, 16, 2, 64, 1024], P('fsdp', 'ctx'), may hold values from -6 to 6
- positions: int32 [8, 2048], P('fsdp'), may hold values from 0 to 6141, as said below
- block_pairs: int32 [16, 2], replicated, may hold values from 0 to 31, as said below
- first_gain: float32 [1024], replicated, may hold values from 0.5 to 1.5
- first_bias: float32 [1024], replicated, may hold values from -1.25 to 1.25
- second_gain: float32 [1024], replicated, may hold values from 0.5 to 1.5
- second_bias: float32 [1024], replicated, may hold values from -1.25 to 1.25
- triple_weight: bfloat16 [1024, 3072], P('fsdp'), may hold values from -0.1875 to 0.1875
- triple_bias: float32 [3072], replicated, may hold values from -1.25 to 1.25
- output_weight: bfloat16 [1024, 1024], P(None, 'fsdp'), may hold values from -0.75 to 0.75
- output_bias: float32 [1024], replicated, may hold values from -1.25 to 1.25
- expand_weight: bfloat16 [1024, 4096], P('fsdp'), may hold values from -0.1875 to 0.1875
- expand_bias: float32 [4096], replicated, may hold values from -1.25 to 1.25
- shrink_weight: bfloat16 [4096, 1024], P(None, 'fsdp'), may hold values from -0.09375 to 0.09375
- shrink_bias: float32 [1024], replicated, may hold values from -1.25 to 1.25
- cotangent: bfloat16 [8, 16, 2, 64, 1024], P('fsdp', 'ctx'), may hold values from -6 to 6
Outputs:
- activations: bfloat16 [8, 16, 2, 64, 1024], P('fsdp', 'ctx')
- grad_tokens: float32 [8, 16, 2, 64, 1024], P('fsdp', 'ctx')
- grad_first_gain: float32 [1024], P(('ctx', 'fsdp'))
- grad_first_bias: float32 [1024], P(('ctx', 'fsdp'))
- grad_second_gain: float32 [1024], P(('ctx', 'fsdp'))
- grad_second_bias: float32 [1024], P(('ctx', 'fsdp'))
- grad_triple_weight: float32 [1024, 3072], P(('ctx', 'fsdp'))
- grad_triple_bias: float32 [2048], P(('ctx', 'fsdp'))
- grad_value_bias: float32 [1024], P(('ctx', 'fsdp'))
- grad_output_weight: float32 [1024, 1024], P(('ctx', 'fsdp'))
- grad_output_bias: float32 [1024], P(('ctx', 'fsdp'))
- grad_expand_weight: float32 [1024, 4096], P(('ctx', 'fsdp'))
- grad_expand_bias: float32 [4096], P(('ctx', 'fsdp'))
- grad_shrink_weight: float32 [4096, 1024], P(('ctx', 'fsdp'))
- grad_shrink_bias: float32 [1024], P(('ctx', 'fsdp'))
Inputs may be any that keep to these rules, and one draw needn't show every extreme that they name: `block_pairs`: row c holds a block p below 16 and its mirror 2 * 16 - 1 - p; every block of a sequence is named once. In each sequence's token order positions begin at 0 and rise by 1 to 3 from one token to the next, except that the last token of every sequence stands at 6141.
All inputs are finite; a program needn't handle non-finite values.
Results may differ from a plain program's by a relative error of at most 0.011.
Values may be sent and summed in bfloat16 or wider, within the bound.
A program may use at most 256 MiB of HBM per device.

v0:
```python
import math

import jax
import jax.numpy as jnp
from jax import lax
from jax.sharding import PartitionSpec as P

HEADS = 16


eps_norm = 1e-05
rotary_base = 10000.0


def in_one_piece(arrays, axis, dim, along):
    ends, at = ([], 0)
    for a in arrays[:-1]:
        at += a.shape[along]
        ends.append(at)
    both = jnp.concatenate(arrays, axis=along)
    return tuple(jnp.split(lax.all_gather(both, axis, axis=dim, tiled=True), ends, axis=along))


def in_blocks(shard, dim, length):
    before, after = (shard.shape[:dim], shard.shape[dim + 1 :])
    return jnp.moveaxis(shard.reshape(*before, length, -1, *after), dim, 0)


def scatter_lines(shard, axis, dim):
    length = lax.axis_size(axis)
    tiles = in_blocks(shard, dim, length)
    lines = tiles.reshape(length, -1)
    width = max(16, -(-lines.shape[1] // 1024) * 8)
    lines = jnp.pad(lines, ((0, 0), (0, width * 128 - lines.shape[1]))).reshape(-1, 128)
    own = lax.psum_scatter(lines, axis, scatter_dimension=0, tiled=True)
    return own.reshape(-1)[: tiles[0].size].reshape(tiles.shape[1:])


def rotate(values, angles, rot_width):
    half = rot_width // 2
    first = values[..., :half]
    second = values[..., half:rot_width]
    cosine = jnp.cos(angles)
    sine = jnp.sin(angles)
    return jnp.concatenate(
        [first * cosine - second * sine, second * cosine + first * sine, values[..., rot_width:]],
        axis=-1,
    )


def frequency(rot_width):
    return 1.0 / rotary_base ** (jnp.arange(0, rot_width, 2, dtype=jnp.float32) / rot_width)


def times_t(left, right):
    return lax.dot_general(
        left, right, (((1,), (1,)), ((), ())), preferred_element_type=jnp.float32
    )


def t_times(left, right):
    return lax.dot_general(
        left, right, (((0,), (0,)), ((), ())), preferred_element_type=jnp.float32
    )


def shards(
    tokens_in,
    positions,
    block_pairs,
    first_gain,
    first_bias,
    second_gain,
    second_bias,
    triple_weight,
    triple_bias,
    output_weight,
    output_bias,
    expand_weight,
    expand_bias,
    shrink_weight,
    shrink_bias,
    cotangent,
):
    seq_dev = tokens_in.shape[0]
    block = tokens_in.shape[3]
    width = tokens_in.shape[4]
    hidden_width = expand_weight.shape[1]
    n_ctx = lax.axis_size("ctx")
    head_dim = width // HEADS
    rot_width = head_dim // 4
    local_len = 2 * block
    whole_len = n_ctx * local_len
    rows = seq_dev * local_len
    scale = 1.0 / math.sqrt(head_dim)
    arange_blk = jnp.arange(block, dtype=jnp.int32)
    all_index = (block_pairs[:, :, None] * block + arange_blk[None, None, :]).reshape(whole_len)
    own_pairs = lax.dynamic_index_in_dim(block_pairs, lax.axis_index("ctx"), 0, keepdims=False)
    own_index = (own_pairs[:, None] * block + arange_blk[None, :]).reshape(local_len)
    own_pos = jnp.take(positions, own_index, axis=1).astype(jnp.float32)
    angles = (own_pos[..., None] * frequency(rot_width))[:, :, None, :]
    allowed = all_index[None, :] <= own_index[:, None]
    x_flat = tokens_in.reshape(rows, width).astype(jnp.float32)
    row_mean = jnp.mean(x_flat, axis=1, keepdims=True)
    centred = x_flat - row_mean
    inv_std = lax.rsqrt(jnp.mean(centred * centred, axis=1, keepdims=True) + eps_norm)
    x_hat = centred * inv_std
    first_low = (x_hat * first_gain + first_bias).astype(jnp.bfloat16)
    second_low = (x_hat * second_gain + second_bias).astype(jnp.bfloat16)
    pieces = (
        lax.all_gather(triple_weight, "fsdp", axis=0, tiled=True),
        lax.all_gather(expand_weight, "fsdp", axis=0, tiled=True),
    )
    left = first_low
    right = second_low
    triple_pre = jnp.dot(left, pieces[0], preferred_element_type=jnp.float32)
    expand_pre = jnp.dot(right, pieces[1], preferred_element_type=jnp.float32)
    triple = triple_pre + triple_bias
    expand = expand_pre + expand_bias
    hidden_low = jax.nn.gelu(expand, approximate=False).astype(jnp.bfloat16)
    parts = triple.reshape(seq_dev, local_len, 3, HEADS, head_dim)
    query_pre = parts[:, :, 0]
    key_pre = parts[:, :, 1]
    query_low = rotate(query_pre, angles, rot_width).astype(jnp.bfloat16)
    key_low = rotate(key_pre, angles, rot_width).astype(jnp.bfloat16)
    value_low = parts[:, :, 2].astype(jnp.bfloat16)
    key_pack = key_low.reshape(seq_dev, 1, local_len, width)
    value_pack = value_low.reshape(seq_dev, 1, local_len, width)
    keys_all, values_all = (
        lax.all_gather(key_pack, "ctx", axis=1, tiled=True),
        lax.all_gather(value_pack, "ctx", axis=1, tiled=True),
    )
    keys_all = keys_all.reshape(seq_dev, whole_len, HEADS, head_dim)
    values_all = values_all.reshape(seq_dev, whole_len, HEADS, head_dim)

    def masked_scores(query_s, keys_s):
        raw = (
            jnp.einsum("qhd,khd->hqk", query_s, keys_s, preferred_element_type=jnp.float32) * scale
        )
        return jnp.where(allowed[None], raw, -jnp.inf)

    def attend(inputs):
        query_s, keys_s, values_s = inputs
        masked = masked_scores(query_s, keys_s)
        peak = jnp.max(masked, axis=2, keepdims=True)
        total = jnp.sum(jnp.exp(masked - peak), axis=2, keepdims=True)
        log_total = peak + jnp.log(total)
        weights = jnp.exp(masked - log_total).astype(jnp.bfloat16)
        mixed = jnp.einsum("hqk,khd->qhd", weights, values_s, preferred_element_type=jnp.float32)
        return (mixed, log_total)

    mixed, log_totals = lax.map(attend, (query_low, keys_all, values_all))
    attn_low = mixed.reshape(rows, width).astype(jnp.bfloat16)
    grad_low = cotangent.reshape(rows, width)
    grad_seq = grad_low.astype(jnp.float32)
    pieces = in_one_piece((output_weight, shrink_weight), "fsdp", 1, 0)
    part = jnp.dot(attn_low, pieces[0], preferred_element_type=jnp.float32) + jnp.dot(
        hidden_low, pieces[1], preferred_element_type=jnp.float32
    )
    pieces = in_one_piece((output_weight, shrink_weight), "fsdp", 1, 0)
    d_attn = times_t(grad_low, pieces[0])
    d_hidden = times_t(grad_low, pieces[1])
    activations = (
        (x_flat + part + output_bias + shrink_bias).astype(jnp.bfloat16).reshape(tokens_in.shape)
    )
    d_attn_low = d_attn.astype(jnp.bfloat16)
    gelu_back = jax.vjp(lambda inner: jax.nn.gelu(inner, approximate=False), expand)[1]
    d_expand_low = gelu_back(d_hidden)[0].astype(jnp.bfloat16)

    def attend_back(inputs):
        query_s, keys_s, values_s, dmix_s, log_total = inputs
        probs = jnp.exp(masked_scores(query_s, keys_s) - log_total)
        probs_low = probs.astype(jnp.bfloat16)
        d_value = jnp.einsum("hqk,qhd->khd", probs_low, dmix_s, preferred_element_type=jnp.float32)
        d_probs = jnp.einsum("qhd,khd->hqk", dmix_s, values_s, preferred_element_type=jnp.float32)
        inner = jnp.sum(probs * d_probs, axis=2, keepdims=True)
        d_scores = (probs * (d_probs - inner)).astype(jnp.bfloat16)
        d_query = (
            jnp.einsum("hqk,khd->qhd", d_scores, keys_s, preferred_element_type=jnp.float32) * scale
        )
        d_key = (
            jnp.einsum("hqk,qhd->khd", d_scores, query_s, preferred_element_type=jnp.float32)
            * scale
        )
        return (d_query, d_key, d_value)

    dmix = d_attn_low.reshape(seq_dev, local_len, HEADS, head_dim)
    d_query, d_key_all, d_value_all = lax.map(
        attend_back, (query_low, keys_all, values_all, dmix, log_totals)
    )
    d_key_own, d_value_own = (
        lax.psum_scatter(
            d_key_all.reshape(seq_dev, n_ctx, local_len, width),
            "ctx",
            scatter_dimension=1,
            tiled=True,
        ),
        lax.psum_scatter(
            d_value_all.reshape(seq_dev, n_ctx, local_len, width),
            "ctx",
            scatter_dimension=1,
            tiled=True,
        ),
    )
    rotate_back = jax.vjp(lambda values: rotate(values, angles, rot_width), query_pre)[1]
    d_query_pre = rotate_back(d_query)[0]
    d_key_pre = rotate_back(d_key_own.reshape(seq_dev, local_len, HEADS, head_dim))[0]
    d_value_pre = d_value_own.reshape(seq_dev, local_len, HEADS, head_dim)
    d_triple_low = (
        jnp.stack([d_query_pre, d_key_pre, d_value_pre], axis=2)
        .reshape(rows, 3 * width)
        .astype(jnp.bfloat16)
    )
    pieces = (
        lax.all_gather(triple_weight, "fsdp", axis=0, tiled=True),
        lax.all_gather(expand_weight, "fsdp", axis=0, tiled=True),
    )
    part_first = times_t(d_triple_low, pieces[0])
    part_second = times_t(d_expand_low, pieces[1])
    d_hat = part_first * first_gain + part_second * second_gain
    d_norm = inv_std * (
        d_hat
        - jnp.mean(d_hat, axis=1, keepdims=True)
        - x_hat * jnp.mean(d_hat * x_hat, axis=1, keepdims=True)
    )
    grad_tokens = (grad_seq + d_norm).reshape(tokens_in.shape)
    triple_sums = jnp.sum(d_triple_low.astype(jnp.float32), axis=0)
    small = (
        lax.psum_scatter(
            jnp.sum(part_first * x_hat, axis=0), ("ctx", "fsdp"), scatter_dimension=0, tiled=True
        ),
        lax.psum_scatter(
            jnp.sum(part_first, axis=0), ("ctx", "fsdp"), scatter_dimension=0, tiled=True
        ),
        lax.psum_scatter(
            jnp.sum(part_second * x_hat, axis=0), ("ctx", "fsdp"), scatter_dimension=0, tiled=True
        ),
        lax.psum_scatter(
            jnp.sum(part_second, axis=0), ("ctx", "fsdp"), scatter_dimension=0, tiled=True
        ),
        lax.psum_scatter(
            triple_sums[: 2 * width], ("ctx", "fsdp"), scatter_dimension=0, tiled=True
        ),
        lax.psum_scatter(
            triple_sums[2 * width :], ("ctx", "fsdp"), scatter_dimension=0, tiled=True
        ),
        lax.psum_scatter(
            jnp.sum(d_expand_low.astype(jnp.float32), axis=0),
            ("ctx", "fsdp"),
            scatter_dimension=0,
            tiled=True,
        ),
        lax.psum_scatter(
            jnp.sum(grad_seq, axis=0), ("ctx", "fsdp"), scatter_dimension=0, tiled=True
        ),
    )
    n_all = lax.axis_size(("ctx", "fsdp"))
    left = first_low
    right = second_low
    in_grads = scatter_lines(
        jnp.concatenate([t_times(left, d_triple_low), t_times(right, d_expand_low)], axis=1),
        ("ctx", "fsdp"),
        0,
    )
    rows_out = width // n_all
    rows_down = hidden_width // n_all
    per_owner = rows_out + rows_down
    owners = per_owner * lax.axis_size(("ctx", "fsdp")) // per_owner
    left = attn_low
    right = hidden_low
    part_out = t_times(left, grad_low).reshape(owners, rows_out, width)
    part_down = t_times(right, grad_low).reshape(owners, rows_down, width)
    out_grads = lax.psum_scatter(
        jnp.concatenate([part_out, part_down], axis=1).reshape(
            per_owner * lax.axis_size(("ctx", "fsdp")), width
        ),
        ("ctx", "fsdp"),
        scatter_dimension=0,
        tiled=True,
    )
    return (
        activations,
        grad_tokens,
        small[0],
        small[1],
        small[2],
        small[3],
        in_grads[:, : 3 * width],
        small[4],
        small[5],
        out_grads[:rows_out],
        small[7],
        in_grads[:, 3 * width :],
        small[6],
        out_grads[rows_out:],
        small[7],
    )


def solution(mesh):
    return jax.shard_map(
        shards,
        mesh=mesh,
        in_specs=(
            P("fsdp", "ctx", None, None, None),
            P("fsdp", None),
            P(),
            P(),
            P(),
            P(),
            P(),
            P("fsdp", None),
            P(),
            P(None, "fsdp"),
            P(),
            P("fsdp", None),
            P(),
            P(None, "fsdp"),
            P(),
            P("fsdp", "ctx", None, None, None),
        ),
        out_specs=(
            P("fsdp", "ctx", None, None, None),
            P("fsdp", "ctx", None, None, None),
            P(("ctx", "fsdp")),
            P(("ctx", "fsdp")),
            P(("ctx", "fsdp")),
            P(("ctx", "fsdp")),
            P(("ctx", "fsdp"), None),
            P(("ctx", "fsdp")),
            P(("ctx", "fsdp")),
            P(("ctx", "fsdp"), None),
            P(("ctx", "fsdp")),
            P(("ctx", "fsdp"), None),
            P(("ctx", "fsdp")),
            P(("ctx", "fsdp"), None),
            P(("ctx", "fsdp")),
        ),
        check_vma=False,
    )
```

profile of v0, /device:TPU:0, one launch (start us, length us, event | category | flops | bytes accessed | tf_op | source)
XLA Modules:
  0.0 2028.8 jit_solution(6970761060675879354)
XLA Ops:
  8.0 2.5 pad_maximum_fusion.2
  11.4 91.1 %all-gather.6.cloned.1.call-done = bf16[1024,3072]{1,0:T(8,128)(2,1)} async-done(((bf16[128,3072]{1,0:T(8,128)(2,1)}), bf16[1024,3072]{1,0:T(8,128)(2,1)}) %all-gather.6.cloned.1.call-update) | async-done | bytes 6291472 | tf_op jit(solution)/shard_map/all_gather | solution.py:111
  102.5 3.8 convolution_add_fusion.1
  111.9 132.6 %all-gather.12.cloned.1.call-done = bf16[5120,1024]{1,0:T(8,128)(2,1)} async-done(((bf16[5120,128]{1,0:T(8,128)(2,1)}), bf16[5120,1024]{1,0:T(8,128)(2,1)}) %all-gather.12.cloned.1.call-update) | async-done | bytes 10485776 | tf_op jit(solution)/shard_map/all_gather | solution.py:21
  244.5 2.3 fusion.54
  246.8 36.1 %all-gather.8.cloned.1.call-done = bf16[1,16,128,1024]{3,2,0,1:T(8,128)(2,1)} async-done(((bf16[1,1,128,1024]{3,2,0,1:T(8,128)(2,1)}), bf16[1,16,128,1024]{3,2,0,1:T(8,128)(2,1)}) %all-gather.8.cloned.1.call-update) | async-done | bytes 4194320 | tf_op jit(solution)/shard_map/all_gather | solution.py:131
  282.9 6.9 copy.51
  289.7 7.4 squeeze.34
  297.2 25.3 %all-gather.10.cloned.1.call-done = bf16[1,16,128,1024]{3,2,0,1:T(8,128)(2,1)} async-done(((bf16[1,1,128,1024]{3,2,0,1:T(8,128)(2,1)}), bf16[1,16,128,1024]{3,2,0,1:T(8,128)(2,1)}) %all-gather.10.cloned.1.call-update) | async-done | bytes 4194320 | tf_op jit(solution)/shard_map/all_gather | solution.py:130
  322.5 6.9 copy.54
  329.4 7.5 squeeze.37
  336.8 4.8 fusion
  341.7 4.4 exponential_reduce_fusion
  346.1 2.7 copy-done.2
  348.8 12.9 multiply_reduce_fusion
  361.7 13.4 multiply_convert_fusion
  375.1 1.4 convolution_multiply_fusion
  376.5 1.8 copy-done.3
  378.3 2.0 copy.61
  380.3 5.9 copy.55
  386.3 8.2 fusion.65
  394.5 2.0 copy.62
  396.5 5.9 copy.56
  402.4 31.2 %all-gather.14.cloned.1.call-done = bf16[1024,4096]{1,0:T(8,128)(2,1)} async-done(((bf16[128,4096]{1,0:T(8,128)(2,1)}), bf16[1024,4096]{1,0:T(8,128)(2,1)}) %all-gather.14.cloned.1.call-update) | async-done | bytes 8388624 | tf_op jit(solution)/shard_map/all_gather | solution.py:112
  433.7 9.3 fusion.12
  442.9 1.6 copy.58
  444.6 8.3 fusion.57
  452.9 8.2 convolution_convert_fusion
  461.8 7.2 pad_maximum_fusion.1
  469.0 14.3 copy.60
  484.5 10.1 convert_reduce_fusion
  494.6 8.3 fusion.85
  502.9 6.4 fusion.38
  512.1 72.2 %reduce-scatter.7.cloned.1.call-done = f32[1,1,128,1024]{2,3,1,0:T(8,128)} async-done(((f32[1,16,128,1024]{2,3,1,0:T(8,128)}), f32[1,1,128,1024]{2,3,1,0:T(8,128)}) %reduce-scatter.7.cloned.1.call-update) | async-done | bytes 524304 | tf_op jit(solution)/shard_map/reduce_scatter | solution.py:198
  584.4 1.6 convert_reduce_fusion.1
  586.0 1.8 fusion.84
  587.8 3.9 copy-done.4
  591.7 10.1 pad_maximum_fusion
  601.8 30.5 %reshape.497 = f32[57344,128]{1,0:T(8,128)} reshape(f32[1024,7168]{1,0:T(8,128)} %pad_maximum_fusion) | data formatting | bytes 58720256 | tf_op jit(solution)/shard_map/reshape | solution.py:34
  632.5 8.4 fusion.4
  640.9 2.8 fusion.51
  643.9 5.1 fusion.83
  649.0 6.6 fusion.80
  655.6 80.5 %all-reduce.14 = (f32[1024]{0:T(1024)S(1)}, f32[1024]{0:T(1024)S(1)}, f32[1024]{0:T(1024)S(1)}, f32[1024]{0:T(1024)S(1)}, f32[2048]{0:T(1024)S(1)}, /*index=5*/f...) all-reduce(f32[1024]{0:T(1024)S(1)} %get-tuple-element.88, ...), channel_id=4, replica_groups=mesh['ctx'=16,'fsdp'=8] {'ctx','fsdp'}, use_global_device_ids=true, to_apply=%region_10.11.clone | all-reduce | flops 12288 | bytes 98304
  741.3 547.3 %reduce-scatter.11.cloned.1.call-done = f32[40,1024]{1,0:T(8,128)} async-done(((f32[5120,1024]{1,0:T(8,128)}), f32[40,1024]{1,0:T(8,128)}) %reduce-scatter.11.cloned.1.call-update) | async-done | bytes 163856 | tf_op jit(solution)/shard_map/reduce_scatter | solution.py:273
  1288.6 1.4 slice.85
  1289.9 1.6 slice.87
  1291.5 727.5 %reduce-scatter.9.cloned.1.call-done = f32[448,128]{1,0:T(8,128)} async-done(((f32[57344,128]{1,0:T(8,128)}), f32[448,128]{1,0:T(8,128)}) %reduce-scatter.9.cloned.1.call-update) | async-done | bytes 229392 | tf_op jit(solution)/shard_map/reduce_scatter | solution.py:35
  (150 shorter events, 20.0 us)
Async XLA Ops:
  7.2 101.1 %copy-start = (s32[1,2048]{1,0:T(1,128)S(1)}, s32[1,2048]{1,0:T(1,128)}, u32[]{:S(2)}) copy-start(s32[1,2048]{1,0:T(1,128)} %param.17) | copy-start | bytes 24580
  7.2 95.3 %all-gather.6.cloned.1.call-start = ((), (), s32[]{:S(2)}) async-start(), calls=%async_computation.4 | async-start | bytes 7077888 | tf_op jit(solution)/shard_map/all_gather | solution.py:111
  7.9 2.7 copy-start.8
  7.9 3.2 copy-start.13
  8.0 3.2 copy-start.19
  8.0 3.2 copy-start.21
  8.0 3.2 copy-start.30
  8.0 94.5 %copy-start.23 = (f32[3072]{0:T(1024)S(1)}, f32[3072]{0:T(1024)}, u32[]{:S(2)}) copy-start(f32[3072]{0:T(1024)} %param.24) | copy-start | bytes 36868
  8.0 236.5 %all-gather.12.cloned.1.call-start = ((), (), s32[]{:S(2)}) async-start(), calls=%async_computation.7 | async-start | bytes 11796480 | tf_op jit(solution)/shard_map/all_gather | solution.py:21
  10.5 272.3 %all-gather.8.cloned.1.call-start = ((), (), s32[]{:S(2)}) async-start(), calls=%async_computation.5 | async-start | bytes 4456448 | tf_op jit(solution)/shard_map/all_gather | solution.py:131
  10.7 91.8 %copy-start.24 = (f32[2,64]{1,0:T(2,128)}, f32[2,64]{1,0:T(2,128)S(1)}, u32[]{:S(2)}) copy-start(f32[2,64]{1,0:T(2,128)S(1)} %broadcast_multiply_fusion.1) | copy-start | bytes 1540
  10.8 91.7 %copy-start.26 = (f32[128]{0:T(128)}, f32[128]{0:T(128)S(1)}, u32[]{:S(2)}) copy-start(f32[128]{0:T(128)S(1)} %div.21) | copy-start | bytes 1540
  11.0 91.5 %copy-start.33 = (f32[2,64]{1,0:T(2,128)}, f32[2,64]{1,0:T(2,128)S(1)}, u32[]{:S(2)}) copy-start(f32[2,64]{1,0:T(2,128)S(1)} %add_rsqrt_fusion) | copy-start | bytes 1540
  11.2 91.4 %copy-start.28 = (f32[128]{0:T(128)}, f32[128]{0:T(128)S(1)}, u32[]{:S(2)}) copy-start(f32[128]{0:T(128)S(1)} %rsqrt.13) | copy-start | bytes 1540
  106.3 1.5 copy-start.35
  107.7 214.8 %all-gather.10.cloned.1.call-start = ((), (), s32[]{:S(2)}) async-start(), calls=%async_computation.6 | async-start | bytes 4456448 | tf_op jit(solution)/shard_map/all_gather | solution.py:130
  109.5 1.1 copy-start.15
  109.6 1.1 copy-start.17
  109.7 134.8 %copy-start.10 = (bf16[1,1,2,64,1024]{4,3,2,1,0:T(8,128)(2,1)S(1)}, bf16[1,1,2,64,1024]{4,3,2,1,0:T(8,128)(2,1)}, u32[]{:S(2)}) copy-start(bf16[1,1,2,64,1024]{4,3,2,1,0:T(8,128)(2,1)} %param.31) | copy-start | bytes 786436
  110.7 323.0 %all-gather.14.cloned.1.call-start = ((), (), s32[]{:S(2)}) async-start(), calls=%async_computation.8 | async-start | bytes 9437184 | tf_op jit(solution)/shard_map/all_gather | solution.py:112
  111.3 398.1 %reduce-scatter.5.cloned.1.call-start = ((), (), s32[]{:S(2)}) async-start(), calls=%async_computation.9 | async-start | bytes 8912896 | tf_op jit(solution)/shard_map/reduce_scatter | solution.py:192
  341.7 7.1 copy-start.2
  341.7 7.1 copy-start.6
  375.1 3.2 copy-start.3
  386.2 198.1 %reduce-scatter.7.cloned.1.call-start = ((), (), s32[]{:S(2)}) async-start(), calls=%async_computation.10 | async-start | bytes 8912896 | tf_op jit(solution)/shard_map/reduce_scatter | solution.py:198
  402.3 31.3 %copy-start.36 = (f32[4096]{0:T(1024)S(1)}, f32[4096]{0:T(1024)}, u32[]{:S(2)}) copy-start(f32[4096]{0:T(1024)} %param.28) | copy-start | bytes 49156
  402.4 886.2 %reduce-scatter.11.cloned.1.call-start = ((), (), s32[]{:S(2)}) async-start(), calls=%async_computation.12 | async-start | bytes 21135360 | tf_op jit(solution)/shard_map/reduce_scatter | solution.py:273
  444.6 8.3 copy-start.7
  461.1 0.7 copy-start.11
  483.3 1.0 copy-start.9
  483.3 1.0 copy-start.14
  483.3 1.0 copy-start.22
  483.3 1.0 copy-start.25
  483.3 1.0 copy-start.34
  483.3 1535.6 %reduce-scatter.9.cloned.1.call-start = ((), (), s32[]{:S(2)}) async-start(), calls=%async_computation.11 | async-start | bytes 29589504 | tf_op jit(solution)/shard_map/reduce_scatter | solution.py:35
  494.6 8.3 copy-start.5
  502.9 7.5 copy-start.16
  502.9 7.5 copy-start.18
  586.0 5.8 copy-start.4
  632.5 8.4 copy-start.12
  632.5 8.4 copy-start.31
  632.5 8.4 copy-start.32
  643.9 5.1 copy-start.20
  643.9 5.1 copy-start.27
  643.9 5.1 copy-start.29
  649.0 1372.8 %copy-start.1 = (s32[1,2048]{1,0:T(1,128)S(1)}, s32[1,2048]{1,0:T(1,128)}, u32[]{:S(2)}) copy-start(s32[1,2048]{1,0:T(1,128)} %param.17) | copy-start | bytes 24580
  739.1 1282.7 %copy-start.37 = (f32[8]{0:T(128)}, f32[8]{0:T(128)S(1)}, u32[]{:S(2)}) copy-start(f32[8]{0:T(128)S(1)} %dynamic-slice.7) | copy-start | bytes 100
Sparse Core Ops, SparseCore 0:
  10.3 92.1 all-gather.5
  104.7 139.7 all-gather.11
  246.8 36.0 all-gather.7
  285.0 37.4 all-gather.9
  324.7 108.9 all-gather.13
  435.9 72.5 reduce-scatter.4
  511.0 73.3 reduce-scatter.6
  586.8 701.7 reduce-scatter.10
  1291.0 727.9 reduce-scatter.8
where the time goes:
time: 2040 us; the launch traced here: 2030 us
  waiting for transfers between devices  1660 us (81%)
  local copies, waits for them, and re-layouts  115 us (6%)
  matrix products  109 us (5%)
  blocking collectives  80.5 us (4%)
  other arithmetic  43.5 us (2%)
    reduce_scatter x1, waiting for transfers between devices, scatter_lines(): own = lax.psum_scatter(lines, axis, scatter_dimension=0, tiled=True)  727 us
    reduce_scatter x1, waiting for transfers between devices, shards(): lax.psum_scatter(jnp.concatenate([part_out, part_down], axis=1).reshape(p...  547 us
    all_gather x1, waiting for transfers between devices, in_one_piece(): lax.all_gather(both, axis, axis=dim, tiled=True)  133 us
    all_gather x1, waiting for transfers between devices, shards(): lax.all_gather(triple_weight, 'fsdp', axis=0, tiled=True)  91.1 us
    unnamed x1, blocking collectives  80.5 us
    reduce_scatter x1, waiting for transfers between devices, shards(): lax.psum_scatter(d_value_all.reshape(seq_dev, n_ctx, local_len, width), '...  72.2 us
  transfers between devices with their start and end apart: 9, of which 8 were waited for; matrix products, arithmetic and copies ran while one was open for 13% of the time, Pallas kernels for 0%

commit v1 on v0

v1 whole, which is shorter than its diff:
```python
import math

import jax
import jax.numpy as jnp
from jax import lax
from jax.experimental import pallas as pl
from jax.experimental.pallas import tpu as pltpu
from jax.sharding import PartitionSpec as P

MESH = pl.DeviceIdType.MESH
BF, F32 = jnp.bfloat16, jnp.float32
EPS = 1e-05
BASE = 10000.0
MIB = 1 << 20
SCALE = 0.125

ZL, KC, ZH = (1, 0, 0, 0, 0), (0, 0, 1, 0, 0), (0, 0, 0, 0, 1)
YS = {i: (0, i, 0, 0, 0) for i in (1, 2, 3)}
XS = {i: (0, 0, 0, i, 0) for i in (1, 2, 3)}
ZYS = {i: (1, i, 0, 0, 0) for i in (1, 2, 3)}
NEAR_FIRST = (1, 3, 2)


def coords():
    c, f = lax.axis_index("ctx"), lax.axis_index("fsdp")
    return lax.div(c, 8), lax.rem(lax.div(c, 2), 4), lax.rem(c, 2), lax.div(f, 2), lax.rem(f, 2)


def device_at(me, off):
    a, b, k, x, h = (lax.rem(p + o, n) for p, o, n in zip(me, off, (2, 4, 2, 4, 2)))
    return ((a * 4 + b) * 2 + k, x * 2 + h)


def barrier(me, offs):
    sem = pltpu.get_barrier_semaphore()
    for off in offs:
        pl.semaphore_signal(sem, inc=1, device_id=device_at(me, off), device_id_type=MESH)
    pl.semaphore_wait(sem, len(offs))


class Sender:
    def __init__(self, me, send_sems, recv_sems):
        self.me, self.send_sems, self.recv_sems, self.copies = me, send_sems, recv_sems, []

    def __call__(self, src, dst, off):
        i = len(self.copies)
        copy = pltpu.make_async_remote_copy(
            src_ref=src,
            dst_ref=dst,
            send_sem=self.send_sems.at[i],
            recv_sem=self.recv_sems.at[i],
            device_id=device_at(self.me, off),
            device_id_type=MESH,
        )
        copy.start()
        self.copies.append(copy)
        return copy

    def finish(self):
        for copy in self.copies:
            copy.wait_send()


def nt(left, right):
    return lax.dot_general(left, right, (((1,), (1,)), ((), ())), preferred_element_type=F32)


def tn(left, right):
    return lax.dot_general(left, right, (((0,), (0,)), ((), ())), preferred_element_type=F32)


def nn(left, right):
    return jnp.dot(left, right, preferred_element_type=F32)


ANY = pl.BlockSpec(memory_space=pl.ANY)
VM = pl.BlockSpec(memory_space=pltpu.VMEM)


GATHER_COPIES = 2 * (1 + 3 + 3 + 0) + 2 * (1 + 3 + 3 + 8)


def gather_kernel(x, g, wa, wb, xo, go, wao, wbo, ss, rs, ls):
    me = coords()
    a, b, k, xx, h = me
    t, f = a * 4 + b, xx * 2 + h
    barrier(me, [ZL, *YS.values(), *XS.values(), ZH, KC])
    send = Sender(me, ss, rs)

    def wa_at(ff):
        return wao.at[pl.ds(pl.multiple_of(ff * 128 + k * 64, 64), 64)]

    def wb_at(ff):
        return wbo.at[
            pl.ds(pl.multiple_of(k * 320, 64), 320), pl.ds(pl.multiple_of(ff * 128, 128), 128)
        ]

    own_wa = wa.at[pl.ds(pl.multiple_of(k * 64, 64), 64)]
    own_wb = wb.at[pl.ds(pl.multiple_of(k * 320, 64), 320)]
    gz = send(g, go.at[t], ZL)
    wz = (send(own_wa, wa_at(f), ZH), send(own_wb, wb_at(f), ZH))
    gy = [send(g, go.at[t], YS[i]) for i in NEAR_FIRST]
    wx = [
        (send(own_wa, wa_at(f), XS[i]), send(own_wb, wb_at(f), XS[i])) for i in NEAR_FIRST
    ]
    xy = [send(x, xo.at[t], YS[i]) for i in NEAR_FIRST]
    rest = list(gy)
    rest.append(send(x, xo.at[t], ZL))
    rest += [send(own_wa, wa_at(f), KC), send(own_wb, wb_at(f), KC)]
    local = [
        pltpu.make_async_copy(src, dst, ls.at[i])
        for i, (src, dst) in enumerate(
            ((x, xo.at[t]), (g, go.at[t]), (own_wa, wa_at(f)), (own_wb, wb_at(f)))
        )
    ]
    for copy in local:
        copy.start()
    tz = (1 - a) * 4 + b
    gz.wait_recv()
    rest += [send(go.at[tz], go.at[tz], YS[i]) for i in NEAR_FIRST]
    fz = xx * 2 + (1 - h)
    for copy in wz:
        copy.wait_recv()
    wxz = [
        (send(wa_at(fz), wa_at(fz), XS[i]), send(wb_at(fz), wb_at(fz), XS[i]))
        for i in NEAR_FIRST
    ]
    rest += [send(wa_at(fz), wa_at(fz), KC), send(wb_at(fz), wb_at(fz), KC)]
    for j, i in enumerate(NEAR_FIRST):
        xy[j].wait_recv()
        ts = a * 4 + lax.rem(b + 4 - i, 4)
        rest.append(send(xo.at[ts], xo.at[ts], ZL))
        for copy in wx[j]:
            copy.wait_recv()
        fs = lax.rem(xx + 4 - i, 4) * 2 + h
        rest += [send(wa_at(fs), wa_at(fs), KC), send(wb_at(fs), wb_at(fs), KC)]
    for j, i in enumerate(NEAR_FIRST):
        for copy in wxz[j]:
            copy.wait_recv()
        fs = lax.rem(xx + 4 - i, 4) * 2 + (1 - h)
        rest += [send(wa_at(fs), wa_at(fs), KC), send(wb_at(fs), wb_at(fs), KC)]
    for copy in rest:
        copy.wait_recv()
    send.finish()
    for copy in local:
        copy.wait()


def gather(x, g, wa, wb):
    return pl.pallas_call(
        gather_kernel,
        out_shape=(
            jax.ShapeDtypeStruct((8, 128, 1024), BF),
            jax.ShapeDtypeStruct((8, 128, 1024), BF),
            jax.ShapeDtypeStruct((1024, 896), BF),
            jax.ShapeDtypeStruct((640, 1024), BF),
        ),
        in_specs=[ANY] * 4,
        out_specs=(ANY,) * 4,
        scratch_shapes=[
            pltpu.SemaphoreType.DMA((GATHER_COPIES,)),
            pltpu.SemaphoreType.DMA((GATHER_COPIES,)),
            pltpu.SemaphoreType.DMA((4,)),
        ],
        compiler_params=pltpu.CompilerParams(collective_id=0, has_side_effects=True),
        name="gather",
    )(x, g, wa, wb)


def normalised(x):
    mean = jnp.mean(x, axis=1, keepdims=True)
    centred = x - mean
    inv = lax.rsqrt(jnp.mean(centred * centred, axis=1, keepdims=True) + EPS)
    return centred * inv, inv


def lanes(shape):
    return lax.broadcasted_iota(jnp.int32, shape, 1)


def left_half(shape):
    return lanes(shape) < 64


def roll(v, shift):
    return pltpu.roll(v, shift, 1)


def tokens_kernel(
    x, g, wa, wb, tb, eb, g1, b1, g2, b2, cs, first, second, pack, hidden, dexp, ge, gs
):
    step = pl.program_id(0)
    n = 256
    x_hat, _ = normalised(x[...].reshape(n, 1024).astype(F32))
    first_low = (x_hat * g1[...] + b1[...]).astype(BF)
    second_low = (x_hat * g2[...] + b2[...]).astype(BF)
    first[...] = first_low
    second[...] = second_low
    grad = g[...].reshape(n, 1024)
    cos, sin = cs[0:8, :], cs[8:16, :]
    one, zero = jnp.ones((48, n), F32), jnp.zeros((48, n), F32)
    tc = jnp.concatenate([cos, cos, one, cos, cos, one], axis=0).T
    ts = jnp.concatenate([-sin, sin, zero, -sin, sin, zero], axis=0).T
    early = (lanes((n, 128)) & 63) < 8

    def turn(v):
        return v * tc + jnp.where(early, roll(v, 120), roll(v, 8)) * ts

    triple = nn(first_low, wa[:, 0:384]) + tb[...]
    query, key, value = turn(triple[:, 0:128]), turn(triple[:, 128:256]), triple[:, 256:384]
    dmix = nt(grad, wb[0:128, :])
    low = left_half((n, 128))
    pack[0, :, 0:128] = jnp.where(low, query, roll(key, 64)).astype(BF)
    pack[0, :, 128:256] = jnp.where(low, value, roll(dmix, 64)).astype(BF)
    pack[1, :, 0:128] = jnp.where(low, roll(query, 64), key).astype(BF)
    pack[1, :, 128:256] = jnp.where(low, roll(value, 64), dmix).astype(BF)
    u = nn(second_low, wa[:, 384:896]) + eb[...]
    cdf = 0.5 * (1.0 + lax.erf(u * math.sqrt(0.5)))
    pdf = jnp.exp(-0.5 * u * u) * (1.0 / math.sqrt(2.0 * math.pi))
    hidden_low = (u * cdf).astype(BF)
    hidden[...] = hidden_low
    dexp_low = (nt(grad, wb[128:640, :]) * (cdf + u * pdf)).astype(BF)
    dexp[...] = dexp_low

    @pl.when(step == 0)
    def _():
        ge[...] = jnp.zeros_like(ge)
        gs[...] = jnp.zeros_like(gs)

    ge[...] += tn(second_low, dexp_low)
    gs[...] += tn(hidden_low, grad)


def tokens_part(x, g, wa, wb, tb, eb, g1, b1, g2, b2, cs):
    def whole(*shape):
        return pl.BlockSpec(shape, lambda i: (0,) * len(shape))

    return pl.pallas_call(
        tokens_kernel,
        grid=(4,),
        out_shape=(
            jax.ShapeDtypeStruct((1024, 1024), BF),
            jax.ShapeDtypeStruct((1024, 1024), BF),
            jax.ShapeDtypeStruct((2, 1024, 256), BF),
            jax.ShapeDtypeStruct((1024, 512), BF),
            jax.ShapeDtypeStruct((1024, 512), BF),
            jax.ShapeDtypeStruct((1024, 512), F32),
            jax.ShapeDtypeStruct((512, 1024), F32),
        ),
        in_specs=[
            pl.BlockSpec((2, 128, 1024), lambda i: (i, 0, 0)),
            pl.BlockSpec((2, 128, 1024), lambda i: (i, 0, 0)),
            whole(1024, 896),
            whole(640, 1024),
            whole(1, 384),
            whole(1, 512),
            whole(1, 1024),
            whole(1, 1024),
            whole(1, 1024),
            whole(1, 1024),
            pl.BlockSpec((16, 256), lambda i: (0, i)),
        ],
        out_specs=(
            pl.BlockSpec((256, 1024), lambda i: (i, 0)),
            pl.BlockSpec((256, 1024), lambda i: (i, 0)),
            pl.BlockSpec((2, 256, 256), lambda i: (0, i, 0)),
            pl.BlockSpec((256, 512), lambda i: (i, 0)),
            pl.BlockSpec((256, 512), lambda i: (i, 0)),
            whole(1024, 512),
            whole(512, 1024),
        ),
        compiler_params=pltpu.CompilerParams(
            dimension_semantics=("arbitrary",), vmem_limit_bytes=56 * MIB
        ),
        name="tokens_part",
    )(x, g, wa, wb, tb, eb, g1, b1, g2, b2, cs)


def swap(src, name, ident):
    def kernel(src, dst, ss, rs, ls):
        me = coords()
        k = me[2]
        keep = pltpu.make_async_copy(src.at[k], dst.at[k], ls.at[0])
        keep.start()
        barrier(me, [KC])
        send = Sender(me, ss, rs)
        away = send(src.at[1 - k], dst.at[k], KC)
        away.wait_recv()
        send.finish()
        keep.wait()

    return pl.pallas_call(
        kernel,
        out_shape=jax.ShapeDtypeStruct(src.shape, src.dtype),
        in_specs=[ANY],
        out_specs=ANY,
        scratch_shapes=[pltpu.SemaphoreType.DMA((1,))] * 3,
        compiler_params=pltpu.CompilerParams(collective_id=ident, has_side_effects=True),
        name=name,
    )(src)


TILE = 256


def attention_kernel(
    order, pack, cs, out, t0, t1, t0r, t1r, qz, dz, t0t, t1t, sc, acc, left, right
):
    def place(n, _):
        at = pl.ds(pl.multiple_of(order[n] * 64, 64), 64)
        v0, v1 = pack[n, :, 0:128].astype(F32), pack[n, :, 128:256].astype(F32)
        low = left_half((64, 128))
        v0 = jnp.where(low, v0 * SCALE, v0)
        t0[at, :] = v0.astype(BF)
        t1[at, :] = v1.astype(BF)
        t0r[at, :] = roll(v0, 64).astype(BF)
        t1r[at, :] = roll(v1, 64).astype(BF)
        qz[at, :] = jnp.where(low, v0, 0.0).astype(BF)
        dz[at, :] = jnp.where(low, 0.0, v1).astype(BF)
        return 0

    lax.fori_loop(0, 32, place, 0)
    acc[...] = jnp.zeros_like(acc)
    for i in range(8):
        rows = pl.ds(i * TILE, TILE)
        t0t[:, rows] = t0[rows, :].astype(F32).T.astype(BF)
        t1t[:, rows] = t1[rows, :].astype(F32).T.astype(BF)

    key_row = lax.broadcasted_iota(jnp.int32, (TILE, TILE), 0)
    query_col = lax.broadcasted_iota(jnp.int32, (TILE, TILE), 1)
    seen = key_row <= query_col
    low = left_half((TILE, 128))

    def folded(v, op):
        parts = [v[j * 8 : j * 8 + 8] for j in range(TILE // 8)]
        while len(parts) > 1:
            parts = [op(parts[j], parts[j + 1]) for j in range(0, len(parts), 2)]
        return parts[0]

    for i in range(8):
        cols = pl.ds(i * TILE, TILE)
        q_i, d_i = qz[cols, :], dz[cols, :]

        def scores(j, peak):
            rows = pl.ds(pl.multiple_of(j * TILE, TILE), TILE)
            s = nt(t0r[rows, :], q_i)
            sc[rows, :] = s
            return jnp.maximum(peak, folded(s, jnp.maximum))

        s = jnp.where(seen, nt(t0r[cols, :], q_i), -jnp.inf)
        sc[cols, :] = s
        peak = lax.fori_loop(0, i, scores, folded(s, jnp.maximum))
        peak = jnp.max(peak, axis=0, keepdims=True)

        def weigh(j, carry):
            total, mix = carry
            rows = pl.ds(pl.multiple_of(j * TILE, TILE), TILE)
            e = jnp.exp(sc[rows, :] - peak)
            sc[rows, :] = e
            return total + folded(e, jnp.add), mix + nn(t1t[:, rows], e.astype(BF))

        total, mix = lax.fori_loop(
            0, i + 1, weigh, (jnp.zeros((8, TILE), F32), jnp.zeros((128, TILE), F32))
        )
        inv = 1.0 / jnp.sum(total, axis=0, keepdims=True)
        mix = mix[0:64] * inv
        inner = jnp.sum(mix * t1t[64:128, cols].astype(F32), axis=0, keepdims=True)

        def back(j, dq):
            rows = pl.ds(pl.multiple_of(j * TILE, TILE), TILE)
            p = sc[rows, :] * inv
            ds = (p * (nt(t1r[rows, :], d_i) - inner)).astype(BF)
            acc[rows, :] += jnp.where(low, nn(ds, t0[cols, :]), nn(p.astype(BF), t1[cols, :]))
            return dq + nn(t0t[:, rows], ds)

        dq = lax.fori_loop(0, i + 1, back, jnp.zeros((128, TILE), F32))[64:128] * SCALE
        cos, sin = cs[0:8, cols], cs[8:16, cols]
        f1, f2 = dq[0:8], dq[8:16]
        both = jnp.concatenate(
            [mix, f1 * cos + f2 * sin, f2 * cos - f1 * sin, dq[16:64]], axis=0
        )
        left[cols, :] = both.T.astype(BF)

    for i in range(8):
        cols = pl.ds(i * TILE, TILE)
        dk = acc[cols, :].T
        cos, sin = cs[0:8, cols], cs[8:16, cols]
        f1, f2 = dk[0:8], dk[8:16]
        both = jnp.concatenate([f1 * cos + f2 * sin, f2 * cos - f1 * sin, dk[16:128]], axis=0)
        right[cols, :] = both.T.astype(BF)

    def give(n, _):
        at = pl.ds(pl.multiple_of(order[n] * 64, 64), 64)
        out[n, :, 0:128] = left[at, :]
        out[n, :, 128:256] = right[at, :]
        return 0

    lax.fori_loop(0, 32, give, 0)


def attention(order, pack, cs):
    return pl.pallas_call(
        attention_kernel,
        out_shape=jax.ShapeDtypeStruct((32, 64, 256), BF),
        in_specs=[pl.BlockSpec(memory_space=pltpu.SMEM), VM, VM],
        out_specs=VM,
        scratch_shapes=[pltpu.VMEM((2048, 128), BF)] * 6
        + [pltpu.VMEM((128, 2048), BF)] * 2
        + [
            pltpu.VMEM((2048, TILE), F32),
            pltpu.VMEM((2048, 128), F32),
            pltpu.VMEM((2048, 128), BF),
            pltpu.VMEM((2048, 128), BF),
        ],
        compiler_params=pltpu.CompilerParams(vmem_limit_bytes=56 * MIB),
        name="attention",
    )(order, pack, cs)


def partials_kernel(
    x, g, e, hidden, dexp, first, wa, wb, g1, g2, ge, gs, act, dhat, grads, sums, gt, go
):
    step = pl.program_id(0)
    n = 256

    @pl.when(step == 0)
    def _():
        gt[...] = jnp.zeros_like(gt)
        go[...] = jnp.zeros_like(go)
        sums[...] = jnp.zeros_like(sums)

    low = left_half((n, 128))
    p0, p1 = e[0, :, 0:128].astype(F32), e[1, :, 0:128].astype(F32)
    r0, r1 = e[0, :, 128:256].astype(F32), e[1, :, 128:256].astype(F32)
    attn = jnp.where(low, p0, roll(p1, 64)).astype(BF)
    dtr = jnp.concatenate(
        [
            jnp.where(low, roll(p0, 64), p1),
            jnp.where(low, r0, roll(r1, 64)),
            jnp.where(low, roll(r0, 64), r1),
        ],
        axis=1,
    )
    dtr_low = dtr.astype(BF)
    grad = g[...].reshape(n, 1024)
    out = nn(attn, wb[0:128, :]) + nn(hidden[...], wb[128:640, :])
    act[...] = out.astype(BF).reshape(2, 128, 1024)
    x_hat, _ = normalised(x[...].reshape(n, 1024).astype(F32))
    d_first = nt(dtr_low, wa[:, 0:384])
    d_second = nt(dexp[...], wa[:, 384:896])
    both = d_first * g1[...] + d_second * g2[...]
    dhat[...] = both.astype(BF).reshape(2, 128, 1024)

    def down(v):
        return jnp.sum(v, axis=0, keepdims=True)

    sums[0:1, :] += down(d_first * x_hat)
    sums[1:2, :] += down(d_first)
    sums[2:3, :] += down(d_second * x_hat)
    sums[3:4, :] += down(d_second)
    sums[4:5, :] += down(grad.astype(F32))
    sums[5:6, 0:384] += down(dtr)
    sums[5:6, 384:896] += down(dexp[...].astype(F32))
    gt[...] += tn(first[...], dtr_low)
    go[...] += tn(attn, grad)

    @pl.when(step == 3)
    def _():
        for kk in range(2):
            for ff in range(8):
                at = [(tt * 2 + kk) * 64 + ff * 8 for tt in range(8)]
                own = kk * 8 + ff
                grads[kk, ff, 0:64, 0:384] = jnp.concatenate(
                    [gt[r : r + 8, :] for r in at], axis=0
                ).astype(BF)
                grads[kk, ff, 0:64, 384:896] = jnp.concatenate(
                    [ge[r : r + 8, :] for r in at], axis=0
                ).astype(BF)
                grads[kk, ff, 0:64, 896:1024] = jnp.concatenate(
                    [go[own * 8 : own * 8 + 8, j * 128 : j * 128 + 128] for j in range(8)], axis=0
                ).astype(BF)
                grads[kk, ff, 64:96, :] = gs[own * 32 : own * 32 + 32, :].astype(BF)


def partials(x, g, e, hidden, dexp, first, wa, wb, g1, g2, ge, gs):
    def whole(*shape):
        return pl.BlockSpec(shape, lambda i: (0,) * len(shape))

    tok = pl.BlockSpec((2, 128, 1024), lambda i: (i, 0, 0))
    return pl.pallas_call(
        partials_kernel,
        grid=(4,),
        out_shape=(
            jax.ShapeDtypeStruct((8, 128, 1024), BF),
            jax.ShapeDtypeStruct((8, 128, 1024), BF),
            jax.ShapeDtypeStruct((2, 8, 96, 1024), BF),
            jax.ShapeDtypeStruct((8, 1024), F32),
        ),
        in_specs=[
            tok,
            tok,
            pl.BlockSpec((2, 256, 256), lambda i: (0, i, 0)),
            pl.BlockSpec((256, 512), lambda i: (i, 0)),
            pl.BlockSpec((256, 512), lambda i: (i, 0)),
            pl.BlockSpec((256, 1024), lambda i: (i, 0)),
            whole(1024, 896),
            whole(640, 1024),
            whole(1, 1024),
            whole(1, 1024),
            whole(1024, 512),
            whole(512, 1024),
        ],
        out_specs=(tok, tok, whole(2, 8, 96, 1024), whole(8, 1024)),
        scratch_shapes=[pltpu.VMEM((1024, 384), F32), pltpu.VMEM((128, 1024), F32)],
        compiler_params=pltpu.CompilerParams(
            dimension_semantics=("arbitrary",), vmem_limit_bytes=56 * MIB
        ),
        name="partials",
    )(x, g, e, hidden, dexp, first, wa, wb, g1, g2, ge, gs)


SUM_COPIES = 2 + 1 + 3 + 6 + 3 + 2 + 1 + 14


def sums_kernel(
    act, dhat, grads, small, x, g, bias,
    act_o, tok_o, gtw_o, gew_o, gow_o, gsw_o, small_o,
    rb, rm, ra, rd, u, um, ru, rum, ta, rta, v, vm, rv, rvm, w, rw, fin, finm, rg, rgm,
    ss, rs,
):
    me = coords()
    a, b, k, xx, h = me
    t = a * 4 + b
    barrier(me, [ZL, *YS.values(), *ZYS.values(), *XS.values(), ZH, KC])
    send = Sender(me, ss, rs)
    to_core = (send(grads.at[1 - k], rb, KC), send(small.at[1 - k], rm, KC))
    act_z = send(act.at[1 - a], ra, ZL)
    dhat_y = [
        send(dhat.at[:, lax.rem(b + i, 4)], rd.at[j], YS[i]) for j, i in enumerate(NEAR_FIRST)
    ]
    for copy in to_core:
        copy.wait_recv()

    def pair(ff, _):
        u[ff] = (grads[k, ff].astype(F32) + rb[ff].astype(F32)).astype(BF)
        um[ff] = small[k, ff] + rm[ff]
        return 0

    lax.fori_loop(0, 8, pair, 0)
    to_x = []
    for j, i in enumerate(NEAR_FIRST):
        there = pl.ds(lax.rem(xx + i, 4) * 2, 2)
        to_x += [send(u.at[there], ru.at[j], XS[i]), send(um.at[there], rum.at[j], XS[i])]
    act_z.wait_recv()

    def pair_act(bb, _):
        ta[bb] = (act[a, bb].astype(F32) + ra[bb].astype(F32)).astype(BF)
        return 0

    lax.fori_loop(0, 4, pair_act, 0)
    act_y = [send(ta.at[lax.rem(b + i, 4)], rta.at[j], YS[i]) for j, i in enumerate(NEAR_FIRST)]
    for copy in to_x:
        copy.wait_recv()
    for hh in range(2):
        total, total_m = u[xx * 2 + hh].astype(F32), um[xx * 2 + hh]
        for j in range(3):
            total += ru[j, hh].astype(F32)
            total_m += rum[j, hh]
        v[hh] = total.astype(BF)
        vm[hh] = total_m
    to_zh = (send(v.at[1 - h], rv, ZH), send(vm.at[1 - h], rvm, ZH))
    for copy in dhat_y:
        copy.wait_recv()
    for aa in range(2):
        total = dhat[aa, b].astype(F32)
        for j in range(3):
            total += rd[j, aa].astype(F32)
        w[aa] = total.astype(BF)
    dhat_z = send(w.at[1 - a], rw, ZL)
    for copy in to_zh:
        copy.wait_recv()
    total = v[h].astype(F32) + rv[...].astype(F32)
    gsw_o[...] = total[64:96, :]
    for j in range(8):
        gow_o[:, j * 128 : j * 128 + 128] = total[j * 8 : j * 8 + 8, 896:1024]
        fin[j] = total[j * 8 : j * 8 + 8, 0:896]
    finm[...] = vm[h] + rvm[...]
    peers = [(ZL, 1, 0)] + [(YS[i], 0, i) for i in NEAR_FIRST] + [(ZYS[i], 1, i) for i in NEAR_FIRST]
    owners = []
    for off, da, db in peers:
        there = lax.rem(a + da, 2) * 4 + lax.rem(b + db, 4)
        owners += [send(fin.at[there], rg.at[t], off), send(finm, rgm.at[t], off)]
    rg[t] = fin[t]
    rgm[t] = finm[...]
    for copy in act_y:
        copy.wait_recv()
    total = x[...].astype(F32) + bias[...] + ta[b].astype(F32)
    for j in range(3):
        total += rta[j].astype(F32)
    act_o[...] = total.astype(BF)
    dhat_z.wait_recv()
    d_hat = w[a].astype(F32) + rw[...].astype(F32)
    x_hat, inv = normalised(x[...].astype(F32))
    tok_o[...] = g[...].astype(F32) + inv * (
        d_hat
        - jnp.mean(d_hat, axis=1, keepdims=True)
        - x_hat * jnp.mean(d_hat * x_hat, axis=1, keepdims=True)
    )
    for copy in owners:
        copy.wait_recv()
    for s in range(8):
        for o in range(3):
            at = o * 1024 + s * 128
            gtw_o[:, at : at + 128] = rg[s, :, o * 128 : o * 128 + 128]
        gew_o[:, s * 512 : s * 512 + 512] = rg[s, :, 384:896]
    total = rgm[0]
    for s in range(1, 8):
        total += rgm[s]
    small_o[...] = total
    send.finish()


def sums(act, dhat, grads, small, x, g, bias):
    shapes = [
        ((8, 96, 1024), BF),
        ((8, 8, 128), F32),
        ((4, 128, 1024), BF),
        ((3, 2, 128, 1024), BF),
        ((8, 96, 1024), BF),
        ((8, 8, 128), F32),
        ((3, 2, 96, 1024), BF),
        ((3, 2, 8, 128), F32),
        ((4, 128, 1024), BF),
        ((3, 128, 1024), BF),
        ((2, 96, 1024), BF),
        ((2, 8, 128), F32),
        ((96, 1024), BF),
        ((8, 128), F32),
        ((2, 128, 1024), BF),
        ((128, 1024), BF),
        ((8, 8, 896), F32),
        ((8, 128), F32),
        ((8, 8, 896), F32),
        ((8, 8, 128), F32),
    ]
    return pl.pallas_call(
        sums_kernel,
        out_shape=(
            jax.ShapeDtypeStruct((128, 1024), BF),
            jax.ShapeDtypeStruct((128, 1024), F32),
            jax.ShapeDtypeStruct((8, 3072), F32),
            jax.ShapeDtypeStruct((8, 4096), F32),
            jax.ShapeDtypeStruct((8, 1024), F32),
            jax.ShapeDtypeStruct((32, 1024), F32),
            jax.ShapeDtypeStruct((8, 128), F32),
        ),
        in_specs=[VM] * 7,
        out_specs=(VM,) * 7,
        scratch_shapes=[pltpu.VMEM(shape, kind) for shape, kind in shapes]
        + [pltpu.SemaphoreType.DMA((SUM_COPIES,))] * 2,
        compiler_params=pltpu.CompilerParams(
            collective_id=3, has_side_effects=True, vmem_limit_bytes=56 * MIB
        ),
        name="sums",
    )(act, dhat, grads, small, x, g, bias)


def shards(
    tokens_in,
    positions,
    block_pairs,
    first_gain,
    first_bias,
    second_gain,
    second_bias,
    triple_weight,
    triple_bias,
    output_weight,
    output_bias,
    expand_weight,
    expand_bias,
    shrink_weight,
    shrink_bias,
    cotangent,
):
    c = lax.axis_index("ctx")
    t, k = c // 2, c % 2
    x, g = tokens_in.reshape(128, 1024), cotangent.reshape(128, 1024)

    def cut(v, at, size, dim):
        return lax.dynamic_slice_in_dim(v, at, size, dim)

    wa = jnp.concatenate(
        [cut(triple_weight, o * 1024 + t * 128, 128, 1) for o in range(3)]
        + [cut(expand_weight, t * 512, 512, 1)],
        axis=1,
    )
    wb = jnp.concatenate(
        [cut(output_weight, t * 128, 128, 0), cut(shrink_weight, t * 512, 512, 0)], axis=0
    )
    tb = cut(triple_bias.reshape(3, 1024), t * 128, 128, 1).reshape(1, 384)
    eb = cut(expand_bias, t * 512, 512, 0).reshape(1, 512)
    order = block_pairs.reshape(8, 2, 2).transpose(1, 0, 2)
    rates = 1.0 / BASE ** (jnp.arange(0, 16, 2, dtype=F32) / 16)

    def turns(pos):
        angles = rates[:, None] * pos.astype(F32)[None, :]
        return jnp.concatenate([jnp.cos(angles), jnp.sin(angles)], axis=0)

    own_blocks = lax.dynamic_index_in_dim(order, k, 0, keepdims=False).reshape(16)
    cs_own = turns(jnp.take(positions.reshape(32, 64), own_blocks, axis=0).reshape(1024))
    cs_all = turns(positions.reshape(2048))
    g1, b1 = first_gain.reshape(1, 1024), first_bias.reshape(1, 1024)
    g2, b2 = second_gain.reshape(1, 1024), second_bias.reshape(1, 1024)

    xs, gs, was, wbs = gather(x, g, wa, wb)
    first, second, pack, hidden, dexp, grad_e, grad_s = tokens_part(
        xs, gs, was, wbs, tb, eb, g1, b1, g2, b2, cs_own
    )
    del second
    pack = swap(pack, "swap_in", 1)
    mixed = attention(order.reshape(32), pack.reshape(32, 64, 256), cs_all)
    mixed = swap(mixed.reshape(2, 1024, 256), "swap_out", 2)
    act, dhat, grads, sm = partials(
        xs, gs, mixed, hidden, dexp, first, was, wbs, g1, g2, grad_e, grad_s
    )

    here = (jnp.arange(8) == t).astype(F32)[:, None]

    def by_owner(v, n):
        return v.reshape(8, 2, 8, n).transpose(1, 2, 0, 3)

    def spread(v):
        return (here * v[None, :]).reshape(-1)

    dq, dk, dv, de = sm[5, 0:128], sm[5, 128:256], sm[5, 256:384], sm[5, 384:896]
    pieces = [by_owner(sm[i], 8) for i in range(4)]
    pieces.append(by_owner(jnp.concatenate([spread(dq), spread(dk)]), 16))
    pieces.append(by_owner(spread(dv), 8))
    pieces.append(by_owner(spread(de), 32))
    pieces.append(by_owner(sm[4] * jnp.repeat(here[:, 0], 128), 8))
    small = jnp.pad(jnp.concatenate(pieces, axis=3), ((0, 0),) * 3 + ((0, 32),))

    bias = (output_bias + shrink_bias).reshape(1, 1024)
    act, tok, gtw, gew, gow, gsw, small = sums(
        act.reshape(2, 4, 128, 1024), dhat.reshape(2, 4, 128, 1024), grads, small, x, g, bias
    )
    own = lax.dynamic_index_in_dim(small, t, 0, keepdims=False)
    return (
        act.reshape(tokens_in.shape),
        tok.reshape(tokens_in.shape),
        own[0:8],
        own[8:16],
        own[16:24],
        own[24:32],
        gtw,
        own[32:48],
        own[48:56],
        gow,
        own[88:96],
        gew,
        own[56:88],
        gsw,
        own[88:96],
    )


def solution(mesh):
    return jax.shard_map(
        shards,
        mesh=mesh,
        in_specs=(
            P("fsdp", "ctx", None, None, None),
            P("fsdp", None),
            P(),
            P(),
            P(),
            P(),
            P(),
            P("fsdp", None),
            P(),
            P(None, "fsdp"),
            P(),
            P("fsdp", None),
            P(),
            P(None, "fsdp"),
            P(),
            P("fsdp", "ctx", None, None, None),
        ),
        out_specs=(
            P("fsdp", "ctx", None, None, None),
            P("fsdp", "ctx", None, None, None),
            P(("ctx", "fsdp")),
            P(("ctx", "fsdp")),
            P(("ctx", "fsdp")),
            P(("ctx", "fsdp")),
            P(("ctx", "fsdp"), None),
            P(("ctx", "fsdp")),
            P(("ctx", "fsdp")),
            P(("ctx", "fsdp"), None),
            P(("ctx", "fsdp")),
            P(("ctx", "fsdp"), None),
            P(("ctx", "fsdp")),
            P(("ctx", "fsdp"), None),
            P(("ctx", "fsdp")),
        ),
        check_vma=False,
    )
```

time: 2040 us -> 217 us (0.11)
  waiting for transfers between devices: 1660 us -> 0 us
  Pallas kernels: 0 us -> 186 us
  matrix products: 109 us -> 0 us
  local copies, waits for them, and re-layouts: 115 us -> 23 us
  blocking collectives: 80.5 us -> 0 us
  other arithmetic: 43.5 us -> 4.94 us
    reduce_scatter x4 -> x0, waiting for transfers between devices: 1350 us -> none  [the longest x1 727 us: scatter_lines(): own = lax.psum_scatter(lines, axis, scatter_dimension=0, tiled=True)]
    all_gather x5 -> x0, waiting for transfers between devices: 316 us -> none  [the longest x1 133 us: in_one_piece(): lax.all_gather(both, axis, axis=dim, tiled=True)]
    pallas_call x0 -> x7, Pallas kernels: none -> 186 us  [the longest x1 45.4 us: sums(): pl.pallas_call(sums_kernel, out_shape=(jax.ShapeDtypeStruct((128, 1024),...]
    dot_general x18 -> x0, matrix products: 109 us -> none  [the longest x4 24 us: times_t(): lax.dot_general(left, right, (((1,), (1,)), ((), ())), preferred_element_...]
    unnamed x1 -> x0, blocking collectives: 80.5 us -> none
    reshape x3 -> x6, local copies, waits for them, and re-layouts: 42.3 us -> 0.92 us  [the longest x1 0.6 us: shards(): mixed = attention(order.reshape(32), pack.reshape(32, 64, 256), cs_all)]
  transfers between devices with their start and end apart: 9 -> 0, of which waited for: 8 -> 0; matrix products, arithmetic and copies ran while one was open for 13% -> 0% of each run, Pallas kernels for 0% -> 0%
where the time goes in v1:
time: 217 us; the launch traced here: 215 us
  Pallas kernels  186 us (86%)
  local copies, waits for them, and re-layouts  23 us (11%)
  other arithmetic  4.94 us (2%)
    pallas_call x1, Pallas kernels, sums(): pl.pallas_call(sums_kernel, out_shape=(jax.ShapeDtypeStruct((128, 1024),...  45.4 us
    pallas_call x1, Pallas kernels, gather(): pl.pallas_call(gather_kernel, out_shape=(jax.ShapeDtypeStruct((8, 128, 10...  43.8 us
    pallas_call x1, Pallas kernels, attention(): pl.pallas_call(attention_kernel, out_shape=jax.ShapeDtypeStruct((32, 64,...  34.2 us
    pallas_call x2, Pallas kernels, swap(): pl.pallas_call(kernel, out_shape=jax.ShapeDtypeStruct(src.shape, src.dtyp...  34.1 us
    pallas_call x1, Pallas kernels, tokens_part(): pl.pallas_call(tokens_kernel, grid=(4,), out_shape=(jax.ShapeDtypeStruct(...  14.9 us
    pallas_call x1, Pallas kernels, partials(): pl.pallas_call(partials_kernel, grid=(4,), out_shape=(jax.ShapeDtypeStruc...  13.6 us
    unnamed x26, local copies, waits for them, and re-layouts  10.6 us

profile of v1, /device:TPU:0, one launch (start us, length us, event | category | flops | bytes accessed | tf_op | source)
XLA Modules:
  0.0 214.9 jit_solution(16435099835257183365)
XLA Ops:
  0.7 0.9 constant_dynamic-slice_fusion.8
  1.6 0.3 copy-done
  1.9 0.7 pad_maximum_fusion.wa
  2.7 0.9 constant_dynamic-slice_fusion.3
  3.6 0.8 constant_dynamic-slice_fusion.4
  4.3 0.7 pad_maximum_fusion.1.wb
  5.0 43.8 %gather.8 = (bf16[8,128,1024]{2,1,0:T(8,128)(2,1)}, bf16[8,128,1024]{2,1,0:T(8,128)(2,1)}, bf16[1024,896]{1,0:T(8,128)(2,1)}, bf16[640,1024]{1,0:T(8,128)(2,1)}) custom-call(bf16[128,1024]{1,0:T(8,128)(2,1)} %bitcast.63, bf16[128,1024]{1,0:T(8,128)(2,1)} %bitcast.65, bf16[128,896]{1,0:T(8,128)(2,1)} %pad_maximum_fusion.wa, bf16[640,128]{1,0:T(8,128)(2,1)} %pad_maximum_fusion.1.wb), custom_call_target="tpu_custom_call" | custom-call | tf_op jit(solution)/shard_map/gather/pallas_call | solution.py:150
  49.0 0.1 copy.35
  49.1 0.1 reshape.238
  49.3 0.5 broadcast.150
  49.8 0.7 fusion.3
  50.5 0.6 gather_fusion
  51.3 0.2 multiply_cosine_fusion.1
  51.5 0.6 pad_maximum_fusion.3.cs
  52.2 0.6 copy.52
  52.8 1.3 dynamic_slice.37
  54.1 14.9 %tokens_part.1 = (bf16[1024,1024]{1,0:T(8,128)(2,1)}, bf16[1024,1024]{1,0:T(8,128)(2,1)}, bf16[2,1024,256]{2,1,0:T(8,128)(2,1)}, bf16[1024,512]{1,0:T(8,128)(2,1...) custom-call(bf16[8,128,1024]{2,1,0:T(8,128)(2,1)} %get-tuple-element.36.x, ...), custom_call_target="tpu_custom_call" | custom-call | tf_op jit(solution)/shard_map/tokens_part/pallas_call | solution.py:238
  69.0 17.1 %swap_in.1 = bf16[2,1024,256]{2,1,0:T(8,128)(2,1)} custom-call(bf16[2,1024,256]{2,1,0:T(8,128)(2,1)} %get-tuple-element.40.src), custom_call_target="tpu_custom_call" | custom-call | tf_op jit(solution)/shard_map/swap_in/pallas_call | solution.py:292
  86.1 0.3 multiply_cosine_fusion
  86.4 0.7 pad_maximum_fusion.2.cs
  87.1 0.1 copy.34
  87.2 0.6 reshape.228.order
  87.8 34.2 %attention.1 = bf16[32,64,256]{2,1,0:T(8,128)(2,1)} custom-call(s32[32]{0:T(128)} %reshape.228.order, bf16[32,64,256]{2,1,0:T(8,128)(2,1)} %bitcast.59, f32[16,2048]{1,0:T(8,128)} %pad_maximum_fusion.2.cs), custom_call_target="tpu_custom_call" | custom-call | tf_op jit(solution)/shard_map/attention/pallas_call | solution.py:402
  122.0 17.0 %swap_out.1.e = bf16[2,1024,256]{2,1,0:T(8,128)(2,1)} custom-call(bf16[2,1024,256]{2,1,0:T(8,128)(2,1)} %bitcast.60), custom_call_target="tpu_custom_call" | custom-call | tf_op jit(solution)/shard_map/swap_out/pallas_call | solution.py:292
  139.1 13.6 %partials.1 = (bf16[8,128,1024]{2,1,0:T(8,128)(2,1)}, bf16[8,128,1024]{2,1,0:T(8,128)(2,1)}, bf16[2,8,96,1024]{3,2,1,0:T(8,128)(2,1)}, f32[8,1024]{1,0:T(8,128)}) custom-call(bf16[8,128,1024]{2,1,0:T(8,128)(2,1)} %get-tuple-element.36.x, bf16[8,128,1024]{2,1,0:T(8,128)(2,1)} %get-tuple-element.37.g, bf16[2,1024,256]{2,1,0:T(8,128)(2,1)} %swap_out.1.e, ...), custom_call_target="tpu_custom_call" | custom-call | tf_op jit(solution)/shard_map/partials/pallas_call | solution.py:490
  152.7 0.7 slice_reduce_fusion.6
  153.6 0.1 broadcast_multiply_fusion.3
  153.7 1.0 slice_reduce_fusion
  154.7 0.1 reshape_squeeze.15
  154.8 0.1 squeeze.7
  155.1 0.1 reshape_squeeze.14
  155.2 0.1 reshape_squeeze.12
  155.3 0.7 slice_reduce_fusion.5
  156.4 0.2 concatenate.24
  156.6 0.6 pad.4.small
  157.2 0.6 add.66
  157.8 45.4 %sums.1 = (bf16[128,1024]{1,0:T(8,128)(2,1)}, f32[128,1024]{1,0:T(8,128)}, f32[8,3072]{1,0:T(8,128)}, f32[8,4096]{1,0:T(8,128)}, f32[8,1024]{1,0:T(8,128)}, /*index=5*/f32[32,1024]{1,0:T(8,128)}, f32[8,128]{1,0:T(8,128)}) custom-call(bf16[2,4,128,1024]{3,2,1,0:T(8,128)(2,1)} %bitcast.61, bf16[2,4,128,1024]{3,2,1,0:T(8,128)(2,1)} %bitcast.62, ...), custom_call_target="tpu_custom_call" | custom-call | tf_op jit(solution)/shard_map/sums/pallas_call | solution.py:646
  203.3 0.7 constant_dynamic-slice_fusion
  204.0 0.6 slice_bitcast_fusion.1
  204.6 0.6 slice_bitcast_fusion
  205.2 0.6 slice_bitcast_fusion.3
  205.7 0.5 copy.60
  206.2 1.7 copy.61
  207.9 1.9 copy.62
  209.8 1.5 copy.63
  211.3 1.4 copy.64
  212.7 1.6 copy.65
  214.3 0.7 copy.66
  (41 shorter events, 1.3 us)
Async XLA Ops:
  0.6 1.3 copy-start
  0.7 48.2 %copy-start.6 = (s32[16,2]{0,1:T(2,128)S(1)}, s32[16,2]{0,1:T(2,128)}, u32[]{:S(2)}) copy-start(s32[16,2]{0,1:T(2,128)} %param.18) | copy-start | bytes 388
  0.7 49.1 %copy-start.3 = (s32[1,2048]{1,0:T(1,128)S(1)}, s32[1,2048]{1,0:T(1,128)}, u32[]{:S(2)}) copy-start(s32[1,2048]{1,0:T(1,128)} %param.17) | copy-start | bytes 24580
  0.7 51.5 %copy-start.2 = (f32[3072]{0:T(1024)S(1)}, f32[3072]{0:T(1024)}, u32[]{:S(2)}) copy-start(f32[3072]{0:T(1024)} %param.24) | copy-start | bytes 36868
  152.6 4.6 %copy-start.4 = (f32[1024]{0:T(1024)S(1)}, f32[1024]{0:T(1024)}, u32[]{:S(2)}) copy-start(f32[1024]{0:T(1024)} %param.26) | copy-start | bytes 12292
  152.7 4.6 %copy-start.5 = (f32[1024]{0:T(1024)S(1)}, f32[1024]{0:T(1024)}, u32[]{:S(2)}) copy-start(f32[1024]{0:T(1024)} %param.30) | copy-start | bytes 12292
  203.2 11.0 %copy-start.1 = (f32[32,1024]{1,0:T(8,128)S(1)}, f32[32,1024]{1,0:T(8,128)}, u32[]{:S(2)}) copy-start(f32[32,1024]{1,0:T(8,128)} %get-tuple-element.144) | copy-start | bytes 393220
  204.6 10.4 %copy-start.7 = (f32[8]{0:T(128)}, f32[8]{0:T(128)S(1)}, u32[]{:S(2)}) copy-start(f32[8]{0:T(128)S(1)} %get-tuple-element.141) | copy-start | bytes 100

commit v2 on v1

v2 whole, which is shorter than its diff:
```python
import math

import jax
import jax.numpy as jnp
from jax import lax
from jax.experimental import pallas as pl
from jax.experimental.pallas import tpu as pltpu
from jax.sharding import PartitionSpec as P

MESH = pl.DeviceIdType.MESH
BF, F32 = jnp.bfloat16, jnp.float32
EPS = 1e-05
BASE = 10000.0
MIB = 1 << 20
SCALE = 0.125

ZL, KC, ZH = (1, 0, 0, 0, 0), (0, 0, 1, 0, 0), (0, 0, 0, 0, 1)
YS = {i: (0, i, 0, 0, 0) for i in (1, 2, 3)}
XS = {i: (0, 0, 0, i, 0) for i in (1, 2, 3)}
NEAR_FIRST = (1, 3, 2)
OFFS = ((0, 0), (0, 1), (0, 3), (0, 2), (1, 0), (1, 1), (1, 3), (1, 2))
SLOT = {off: n for n, off in enumerate(OFFS)}


def origin(da, i):
    return SLOT[(da, (4 - i) % 4)]


def chips(n):
    return (*OFFS[n], 0, 0, 0)


def coords():
    c, f = lax.axis_index("ctx"), lax.axis_index("fsdp")
    return lax.div(c, 8), lax.rem(lax.div(c, 2), 4), lax.rem(c, 2), lax.div(f, 2), lax.rem(f, 2)


def device_at(me, off):
    a, b, k, x, h = (lax.rem(p + o, n) for p, o, n in zip(me, off, (2, 4, 2, 4, 2)))
    return ((a * 4 + b) * 2 + k, x * 2 + h)


def barrier(me, offs):
    sem = pltpu.get_barrier_semaphore()
    for off in offs:
        pl.semaphore_signal(sem, inc=1, device_id=device_at(me, off), device_id_type=MESH)
    pl.semaphore_wait(sem, len(offs))


class Sender:
    def __init__(self, me, send_sems, recv_sems):
        self.me, self.send_sems, self.recv_sems, self.copies = me, send_sems, recv_sems, []

    def __call__(self, src, dst, off):
        i = len(self.copies)
        copy = pltpu.make_async_remote_copy(
            src_ref=src,
            dst_ref=dst,
            send_sem=self.send_sems.at[i],
            recv_sem=self.recv_sems.at[i],
            device_id=device_at(self.me, off),
            device_id_type=MESH,
        )
        copy.start()
        self.copies.append(copy)
        return copy

    def finish(self):
        for copy in self.copies:
            copy.wait_send()


def nt(left, right):
    return lax.dot_general(left, right, (((1,), (1,)), ((), ())), preferred_element_type=F32)


def tn(left, right):
    return lax.dot_general(left, right, (((0,), (0,)), ((), ())), preferred_element_type=F32)


def nn(left, right):
    return jnp.dot(left, right, preferred_element_type=F32)


ANY = pl.BlockSpec(memory_space=pl.ANY)
VM = pl.BlockSpec(memory_space=pltpu.VMEM)


GATHER_COPIES = 2 * 7 + 2 * 15 + 8
KEEP = 4 + 6 * 8 + 2


def gather_kernel(
    x, g, wa, wb, tb, eb, g1, b1, g2, b2, cs,
    pack_o, x_o, g_o, first_o, p1_o, p2_o, waq_o, wbo_o, grads_o, sums_o,
    xs, gs, was, wbs, first, second, hidden, dexp, p1, p2, mine, theirs, ge, gsh,
    ss, rs, ls,
):
    me = coords()
    a, b, k, xx, h = me
    f = xx * 2 + h
    barrier(me, [ZL, *YS.values(), *XS.values(), ZH, KC])
    send = Sender(me, ss, rs)
    local = []

    def keep(src, dst):
        copy = pltpu.make_async_copy(src, dst, ls.at[len(local)])
        copy.start()
        local.append(copy)
        return copy

    def wa_at(ff):
        return was.at[pl.ds(pl.multiple_of(ff * 128 + k * 64, 64), 64)]

    def wb_at(ff):
        return wbs.at[
            pl.ds(pl.multiple_of(k * 320, 64), 320), pl.ds(pl.multiple_of(ff * 128, 128), 128)
        ]

    own_wa = wa.at[pl.ds(pl.multiple_of(k * 64, 64), 64)]
    own_wb = wb.at[pl.ds(pl.multiple_of(k * 320, 64), 320)]
    wz = (send(own_wa, wa_at(f), ZH), send(own_wb, wb_at(f), ZH))
    gz = send(g, gs.at[SLOT[(1, 0)]], ZL)
    wx = [(send(own_wa, wa_at(f), XS[i]), send(own_wb, wb_at(f), XS[i])) for i in NEAR_FIRST]
    gy = {i: send(g, gs.at[origin(0, i)], YS[i]) for i in NEAR_FIRST}
    xy = {i: send(x, xs.at[origin(0, i)], YS[i]) for i in NEAR_FIRST}
    xz = send(x, xs.at[SLOT[(1, 0)]], ZL)
    weights = [send(own_wa, wa_at(f), KC), send(own_wb, wb_at(f), KC)]
    own = [keep(x, xs.at[0]), keep(g, gs.at[0]), keep(own_wa, wa_at(f)), keep(own_wb, wb_at(f))]
    fz = xx * 2 + (1 - h)
    for copy in wz:
        copy.wait_recv()
    wxz = [
        (send(wa_at(fz), wa_at(fz), XS[i]), send(wb_at(fz), wb_at(fz), XS[i]))
        for i in NEAR_FIRST
    ]
    weights += [send(wa_at(fz), wa_at(fz), KC), send(wb_at(fz), wb_at(fz), KC)]
    gz.wait_recv()
    gzy = {i: send(gs.at[4], gs.at[origin(1, i)], YS[i]) for i in NEAR_FIRST}
    for j, i in enumerate(NEAR_FIRST):
        for copy in wx[j]:
            copy.wait_recv()
        fs = lax.rem(xx + 4 - i, 4) * 2 + h
        weights += [send(wa_at(fs), wa_at(fs), KC), send(wb_at(fs), wb_at(fs), KC)]
    xyz = {}
    for i in NEAR_FIRST:
        xy[i].wait_recv()
        n = origin(0, i)
        xyz[i] = send(xs.at[n], xs.at[origin(1, i)], ZL)
    for j, i in enumerate(NEAR_FIRST):
        for copy in wxz[j]:
            copy.wait_recv()
        fs = lax.rem(xx + 4 - i, 4) * 2 + (1 - h)
        weights += [send(wa_at(fs), wa_at(fs), KC), send(wb_at(fs), wb_at(fs), KC)]
    for copy in own:
        copy.wait()
    for copy in weights:
        copy.wait_recv()
    keep(was.at[:, 0:384], waq_o)
    keep(wbs.at[0:128], wbo_o)
    sums_o[...] = jnp.zeros_like(sums_o)
    low = left_half((128, 128))
    early = (lanes((128, 128)) & 63) < 8
    packs = []

    def down(v):
        return jnp.sum(v, axis=0, keepdims=True)

    def block(n):
        rows = slice(n * 128, n * 128 + 128)
        x_hat, _ = normalised(xs[n].astype(F32))
        first_low = (x_hat * g1[...] + b1[...]).astype(BF)
        second_low = (x_hat * g2[...] + b2[...]).astype(BF)
        first[n] = first_low
        second[rows, :] = second_low
        grad = gs[n]
        cos, sin = cs[0:8, rows], cs[8:16, rows]
        one, zero = jnp.ones((48, 128), F32), jnp.zeros((48, 128), F32)
        tc = jnp.concatenate([cos, cos, one, cos, cos, one], axis=0).T
        ts = jnp.concatenate([-sin, sin, zero, -sin, sin, zero], axis=0).T

        def turn(v):
            return v * tc + jnp.where(early, roll(v, 120), roll(v, 8)) * ts

        triple = nn(first_low, was[:, 0:384]) + tb[...]
        query, key, value = turn(triple[:, 0:128]), turn(triple[:, 128:256]), triple[:, 256:384]
        dmix = nt(grad, wbs[0:128, :])
        pairs = (
            (jnp.where(low, query, roll(key, 64)), jnp.where(low, roll(query, 64), key)),
            (jnp.where(low, value, roll(dmix, 64)), jnp.where(low, roll(value, 64), dmix)),
        )
        for j, (head0, head1) in enumerate(pairs):
            at = slice(j * 128, j * 128 + 128)
            mine[n, :, at] = jnp.where(k == 0, head0, head1).astype(BF)
            theirs[n, :, at] = jnp.where(k == 0, head1, head0).astype(BF)
        keep(mine.at[n], pack_o.at[k, n])
        packs.append(send(theirs.at[n], pack_o.at[k, n], KC))
        u = nn(second_low, was[:, 384:896]) + eb[...]
        cdf = 0.5 * (1.0 + lax.erf(u * math.sqrt(0.5)))
        pdf = jnp.exp(-0.5 * u * u) * (1.0 / math.sqrt(2.0 * math.pi))
        hidden_low = (u * cdf).astype(BF)
        hidden[rows, :] = hidden_low
        dexp_low = (nt(grad, wbs[128:640, :]) * (cdf + u * pdf)).astype(BF)
        dexp[rows, :] = dexp_low
        p1[n] = nn(hidden_low, wbs[128:640, :]).astype(BF)
        d_second = nt(dexp_low, was[:, 384:896])
        p2[n] = (d_second * g2[...]).astype(BF)
        sums_o[2:3, :] += down(d_second * x_hat)
        sums_o[3:4, :] += down(d_second)
        sums_o[4:5, :] += down(grad.astype(F32))
        sums_o[5:6, 384:896] += down(dexp_low.astype(F32))
        for src, dst in ((xs, x_o), (gs, g_o), (first, first_o), (p1, p1_o), (p2, p2_o)):
            keep(src.at[n], dst.at[n])

    for n, (da, db) in enumerate(OFFS):
        i = (4 - db) % 4
        if (da, db) == (1, 0):
            xz.wait_recv()
        elif da:
            gzy[i].wait_recv()
            xyz[i].wait_recv()
        elif db:
            gy[i].wait_recv()
        block(n)
    ge[...] = tn(second[...], dexp[...])
    gsh[...] = tn(hidden[...], gs[...].reshape(1024, 1024))
    for kk in range(2):
        for ff in range(8):
            at = [(tt * 2 + kk) * 64 + ff * 8 for tt in range(8)]
            own_rows = slice((kk * 8 + ff) * 32, (kk * 8 + ff) * 32 + 32)
            grads_o[kk, ff, 0:64, :] = jnp.concatenate(
                [ge[r : r + 8, :] for r in at], axis=0
            ).astype(BF)
            grads_o[kk, ff, 64:96, :] = gsh[own_rows, 0:512].astype(BF)
            grads_o[kk, ff, 96:128, :] = gsh[own_rows, 512:1024].astype(BF)
    for copy in packs:
        copy.wait_recv()
    send.finish()
    for copy in local[4:]:
        copy.wait()


def gather(x, g, wa, wb, tb, eb, g1, b1, g2, b2, cs):
    tok = jax.ShapeDtypeStruct((8, 128, 1024), BF)
    big = pltpu.VMEM((8, 128, 1024), BF)
    return pl.pallas_call(
        gather_kernel,
        out_shape=(
            jax.ShapeDtypeStruct((2, 8, 128, 256), BF),
            tok,
            tok,
            tok,
            tok,
            tok,
            jax.ShapeDtypeStruct((1024, 384), BF),
            jax.ShapeDtypeStruct((128, 1024), BF),
            jax.ShapeDtypeStruct((2, 8, 128, 512), BF),
            jax.ShapeDtypeStruct((8, 1024), F32),
        ),
        in_specs=[ANY] * 4 + [VM] * 7,
        out_specs=(ANY,) * 8 + (VM,) * 2,
        scratch_shapes=[
            big,
            big,
            pltpu.VMEM((1024, 896), BF),
            pltpu.VMEM((640, 1024), BF),
            big,
            pltpu.VMEM((1024, 1024), BF),
            pltpu.VMEM((1024, 512), BF),
            pltpu.VMEM((1024, 512), BF),
            big,
            big,
            pltpu.VMEM((8, 128, 256), BF),
            pltpu.VMEM((8, 128, 256), BF),
            pltpu.VMEM((1024, 512), F32),
            pltpu.VMEM((512, 1024), F32),
            pltpu.SemaphoreType.DMA((GATHER_COPIES,)),
            pltpu.SemaphoreType.DMA((GATHER_COPIES,)),
            pltpu.SemaphoreType.DMA((KEEP,)),
        ],
        compiler_params=pltpu.CompilerParams(
            collective_id=0, has_side_effects=True, vmem_limit_bytes=56 * MIB
        ),
        name="gather",
    )(x, g, wa, wb, tb, eb, g1, b1, g2, b2, cs)


def normalised(x):
    mean = jnp.mean(x, axis=1, keepdims=True)
    centred = x - mean
    inv = lax.rsqrt(jnp.mean(centred * centred, axis=1, keepdims=True) + EPS)
    return centred * inv, inv


def lanes(shape):
    return lax.broadcasted_iota(jnp.int32, shape, 1)


def left_half(shape):
    return lanes(shape) < 64


def roll(v, shift):
    return pltpu.roll(v, shift, 1)


TILE = 256


def attention_kernel(
    order, pack, cs, out, t0, t1, t0r, t1r, qz, dz, t0t, t1t, sc, acc, left, right
):
    def place(n, _):
        at = pl.ds(pl.multiple_of(order[n] * 64, 64), 64)
        v0, v1 = pack[n, :, 0:128].astype(F32), pack[n, :, 128:256].astype(F32)
        low = left_half((64, 128))
        v0 = jnp.where(low, v0 * SCALE, v0)
        t0[at, :] = v0.astype(BF)
        t1[at, :] = v1.astype(BF)
        t0r[at, :] = roll(v0, 64).astype(BF)
        t1r[at, :] = roll(v1, 64).astype(BF)
        qz[at, :] = jnp.where(low, v0, 0.0).astype(BF)
        dz[at, :] = jnp.where(low, 0.0, v1).astype(BF)
        return 0

    lax.fori_loop(0, 32, place, 0)
    acc[...] = jnp.zeros_like(acc)
    for i in range(8):
        rows = pl.ds(i * TILE, TILE)
        t0t[:, rows] = t0[rows, :].astype(F32).T.astype(BF)
        t1t[:, rows] = t1[rows, :].astype(F32).T.astype(BF)

    key_row = lax.broadcasted_iota(jnp.int32, (TILE, TILE), 0)
    query_col = lax.broadcasted_iota(jnp.int32, (TILE, TILE), 1)
    seen = key_row <= query_col
    low = left_half((TILE, 128))

    def folded(v, op):
        parts = [v[j * 8 : j * 8 + 8] for j in range(TILE // 8)]
        while len(parts) > 1:
            parts = [op(parts[j], parts[j + 1]) for j in range(0, len(parts), 2)]
        return parts[0]

    for i in range(8):
        cols = pl.ds(i * TILE, TILE)
        q_i, d_i = qz[cols, :], dz[cols, :]

        def scores(j, peak):
            rows = pl.ds(j * TILE, TILE)
            s = nt(t0r[rows, :], q_i)
            sc[rows, :] = s
            return jnp.maximum(peak, folded(s, jnp.maximum))

        s = jnp.where(seen, nt(t0r[cols, :], q_i), -jnp.inf)
        sc[cols, :] = s
        peak = folded(s, jnp.maximum)
        for j in range(i):
            peak = scores(j, peak)
        peak = jnp.max(peak, axis=0, keepdims=True)

        def weigh(j, carry):
            total, mix = carry
            rows = pl.ds(j * TILE, TILE)
            e = jnp.exp(sc[rows, :] - peak)
            sc[rows, :] = e
            return total + folded(e, jnp.add), mix + nn(t1t[:, rows], e.astype(BF))

        carry = (jnp.zeros((8, TILE), F32), jnp.zeros((128, TILE), F32))
        for j in range(i + 1):
            carry = weigh(j, carry)
        total, mix = carry
        inv = 1.0 / jnp.sum(total, axis=0, keepdims=True)
        mix = mix[0:64] * inv
        inner = jnp.sum(mix * t1t[64:128, cols].astype(F32), axis=0, keepdims=True)

        def back(j, dq):
            rows = pl.ds(j * TILE, TILE)
            p = sc[rows, :] * inv
            ds = (p * (nt(t1r[rows, :], d_i) - inner)).astype(BF)
            acc[rows, :] += jnp.where(low, nn(ds, t0[cols, :]), nn(p.astype(BF), t1[cols, :]))
            return dq + nn(t0t[:, rows], ds)

        dq = jnp.zeros((128, TILE), F32)
        for j in range(i + 1):
            dq = back(j, dq)
        dq = dq[64:128] * SCALE
        cos, sin = cs[0:8, cols], cs[8:16, cols]
        f1, f2 = dq[0:8], dq[8:16]
        both = jnp.concatenate(
            [mix, f1 * cos + f2 * sin, f2 * cos - f1 * sin, dq[16:64]], axis=0
        )
        left[cols, :] = both.T.astype(BF)

    for i in range(8):
        cols = pl.ds(i * TILE, TILE)
        dk = acc[cols, :].T
        cos, sin = cs[0:8, cols], cs[8:16, cols]
        f1, f2 = dk[0:8], dk[8:16]
        both = jnp.concatenate([f1 * cos + f2 * sin, f2 * cos - f1 * sin, dk[16:128]], axis=0)
        right[cols, :] = both.T.astype(BF)

    def give(n, _):
        at = pl.ds(pl.multiple_of(order[n] * 64, 64), 64)
        out[n, :, 0:128] = left[at, :]
        out[n, :, 128:256] = right[at, :]
        return 0

    lax.fori_loop(0, 32, give, 0)


def attention(order, pack, cs):
    return pl.pallas_call(
        attention_kernel,
        out_shape=jax.ShapeDtypeStruct((32, 64, 256), BF),
        in_specs=[pl.BlockSpec(memory_space=pltpu.SMEM), VM, VM],
        out_specs=VM,
        scratch_shapes=[pltpu.VMEM((2048, 128), BF)] * 6
        + [pltpu.VMEM((128, 2048), BF)] * 2
        + [
            pltpu.VMEM((2048, TILE), F32),
            pltpu.VMEM((2048, 128), F32),
            pltpu.VMEM((2048, 128), BF),
            pltpu.VMEM((2048, 128), BF),
        ],
        compiler_params=pltpu.CompilerParams(vmem_limit_bytes=56 * MIB),
        name="attention",
    )(order, pack, cs)


SUM_COPIES = 4 + 1 + 4 + 6 + 3 + 3 + 1 + 7 + 1 + 3 + 1 + 7 + 1 + 3 + 1 + 7 + 1
AFTER = (4, 5, 6, 7, 1, 2, 3, 0)


def finish_kernel(
    mixed, xi, gi, firsti, p1i, p2i, waq, wbo, gradsi, sums_a, g1, bias,
    act_o, tok_o, gtw_o, gew_o, gow_o, gsw_o, small_o,
    em, eo, xs, gs, first, p1, p2, act, dhat, attn, dtr, ra, rd, ta, rta, w, rw,
    gm, rgm, um, rum, vm, rvm, finm, rfm,
    gt, go, ga, rga, ua, rua, va, rva, fina, rfa,
    sm, rsm, sk, rsx, sz, rsz, st, rst,
    ss, rs, ls,
):
    me = coords()
    a, b, k, xx, h = me
    t = a * 4 + b
    local = []

    def load(src, dst):
        copy = pltpu.make_async_copy(src, dst, ls.at[len(local)])
        copy.start()
        local.append(copy)

    load(mixed.at[k], em)
    for src, dst in ((p1i, p1), (p2i, p2), (xi, xs), (gi, gs), (firsti, first)):
        load(src, dst)
    load(gradsi.at[k], gm)
    barrier(me, [*(chips(n) for n in range(1, 8)), *XS.values(), ZH, KC])
    send = Sender(me, ss, rs)
    e_sent = {
        n: send(mixed.at[1 - k, pl.ds(n, 2)], eo.at[pl.ds(n, 2)], KC) for n in (4, 6, 0, 2)
    }
    gm_core = send(gradsi.at[1 - k], rgm, KC)
    low = left_half((128, 128))
    sm[...] = sums_a[...]
    for copy in local:
        copy.wait()
    act_z, dhat_y = {}, {}

    def down(v):
        return jnp.sum(v, axis=0, keepdims=True)

    def block(n):
        rows = slice(n * 128, n * 128 + 128)
        tiles = []
        for at in (slice(0, 128), slice(128, 256)):
            own, other = em[n, :, at].astype(F32), eo[n, :, at].astype(F32)
            tiles.append((jnp.where(k == 0, own, other), jnp.where(k == 0, other, own)))
        (p_0, p_1), (r_0, r_1) = tiles
        attn_low = jnp.where(low, p_0, roll(p_1, 64)).astype(BF)
        turned = jnp.concatenate(
            [
                jnp.where(low, roll(p_0, 64), p_1),
                jnp.where(low, r_0, roll(r_1, 64)),
                jnp.where(low, roll(r_0, 64), r_1),
            ],
            axis=1,
        )
        turned_low = turned.astype(BF)
        attn[rows, :] = attn_low
        dtr[rows, :] = turned_low
        act[n] = (p1[n].astype(F32) + nn(attn_low, wbo[...])).astype(BF)
        da, db = OFFS[n]
        if da:
            act_z[n - 4] = send(act.at[n], ra.at[n - 4], ZL)
        d_first = nt(turned_low, waq[...])
        dhat[n] = (p2[n].astype(F32) + d_first * g1[...]).astype(BF)
        if db:
            dhat_y[n] = send(dhat.at[n], rd.at[da, NEAR_FIRST.index(db)], YS[db])
        x_hat, _ = normalised(xs[n].astype(F32))
        sm[0:1, :] += down(d_first * x_hat)
        sm[1:2, :] += down(d_first)
        sm[5:6, 0:384] += down(turned)

    def to_x(src, dst):
        sent = []
        for j, i in enumerate(NEAR_FIRST):
            there = pl.ds(lax.rem(xx + i, 4) * 2, 2)
            sent.append(send(src.at[there], dst.at[j], XS[i]))
        return sent

    def core_sum(own, got, dst):
        def one(ff, _):
            dst[ff] = (own[ff].astype(F32) + got[ff].astype(F32)).astype(BF)
            return 0

        lax.fori_loop(0, 8, one, 0)

    def x_sum(own, got, dst):
        for hh in range(2):
            total = own[xx * 2 + hh].astype(F32)
            for j in range(3):
                total += got[j, hh].astype(F32)
            dst[hh] = total.astype(BF)

    def to_owners(fin, got):
        sent = []
        for n in range(1, 8):
            da, db = OFFS[n]
            there = lax.rem(a + da, 2) * 4 + lax.rem(b + db, 4)
            sent.append(send(fin.at[there], got.at[origin(da, db)], chips(n)))
        got[0] = fin[t]
        return sent

    def wait(copies):
        for copy in copies:
            copy.wait_recv()

    for n in AFTER:
        if n in (4, 6, 1, 2):
            e_sent[n & 6].wait_recv()
        block(n)
        if n == 5:
            gm_core.wait_recv()
            core_sum(gm, rgm, um)
            gm_x = to_x(um, rum)
    sm_core = send(sm, rsm, KC)
    gt[...] = tn(first[...].reshape(1024, 1024), dtr[...])
    go[...] = tn(attn[...], gs[...].reshape(1024, 1024))
    for kk in range(2):
        for ff in range(8):
            at = [(tt * 2 + kk) * 64 + ff * 8 for tt in range(8)]
            r = (kk * 8 + ff) * 8
            ga[kk, ff, :, 0:384] = jnp.concatenate([gt[q : q + 8, :] for q in at], axis=0).astype(BF)
            ga[kk, ff, :, 384:512] = jnp.concatenate(
                [go[r : r + 8, j * 128 : j * 128 + 128] for j in range(8)], axis=0
            ).astype(BF)
    ga_core = send(ga.at[1 - k], rga, KC)
    act_y = []
    for m in (1, 2, 3):
        act_z[m].wait_recv()
        ta[m] = (act[m].astype(F32) + ra[m].astype(F32)).astype(BF)
        db = OFFS[m][1]
        act_y.append(send(ta.at[m], rta.at[NEAR_FIRST.index(db)], YS[db]))
    ga_core.wait_recv()
    core_sum(ga.at[k], rga, ua)
    ga_x = to_x(ua, rua)
    sm_core.wait_recv()
    sk[...] = sm[...] + rsm[...]
    sm_x = [send(sk, rsx.at[j], XS[i]) for j, i in enumerate(NEAR_FIRST)]
    wait(gm_x)
    x_sum(um, rum, vm)
    gm_zh = send(vm.at[1 - h], rvm, ZH)
    for n in (5, 6, 7):
        dhat_y[n].wait_recv()
    total = dhat[4].astype(F32)
    for j in range(3):
        total += rd[1, j].astype(F32)
    w[...] = total.astype(BF)
    dhat_z = send(w, rw, ZL)
    wait(ga_x)
    x_sum(ua, rua, va)
    ga_zh = send(va.at[1 - h], rva, ZH)
    wait(sm_x)
    sz[...] = sk[...] + rsx[0] + rsx[1] + rsx[2]
    sm_zh = send(sz, rsz, ZH)
    gm_zh.wait_recv()
    total = vm[h].astype(F32) + rvm[...].astype(F32)
    for j in range(8):
        finm[j] = total[j * 8 : j * 8 + 8, :]
    gsw_o[:, 0:512] = total[64:96, :]
    gsw_o[:, 512:1024] = total[96:128, :]
    gm_own = to_owners(finm, rfm)
    ga_zh.wait_recv()
    total = va[h].astype(F32) + rva[...].astype(F32)
    for j in range(8):
        fina[j] = total[j * 8 : j * 8 + 8, 0:384]
        gow_o[:, j * 128 : j * 128 + 128] = total[j * 8 : j * 8 + 8, 384:512]
    ga_own = to_owners(fina, rfa)
    sm_zh.wait_recv()
    total = sz[...] + rsz[...]
    for j in range(8):
        st[j, 0:4, :] = total[0:4, j * 128 : j * 128 + 128]
        st[j, 4:5, :] = total[5:6, 0:128]
        st[j, 5:6, :] = total[5:6, 128:256]
        st[j, 6:7, :] = total[4:5, j * 128 : j * 128 + 128]
        st[j, 7:8, :] = total[5:6, 256:384]
    small_o[8:12, :] = jnp.concatenate(
        [total[5:6, 384 + j * 128 : 512 + j * 128] for j in range(4)], axis=0
    )
    small_o[12:16, :] = jnp.zeros((4, 128), F32)
    st_own = to_owners(st, rst)
    act_z[0].wait_recv()
    wait(act_y)
    total = xs[0].astype(F32) + bias[...] + act[0].astype(F32) + ra[0].astype(F32)
    for j in range(3):
        total += rta[j].astype(F32)
    act_o[...] = total.astype(BF)
    for n in (1, 2, 3):
        dhat_y[n].wait_recv()
    total = dhat[0].astype(F32)
    for j in range(3):
        total += rd[0, j].astype(F32)
    x_hat, inv = normalised(xs[0].astype(F32))
    dhat_z.wait_recv()
    d_hat = total + rw[...].astype(F32)
    tok_o[...] = gs[0].astype(F32) + inv * (
        d_hat
        - jnp.mean(d_hat, axis=1, keepdims=True)
        - x_hat * jnp.mean(d_hat * x_hat, axis=1, keepdims=True)
    )
    wait(gm_own)
    wait(ga_own)
    wait(st_own)
    for n, (da, db) in enumerate(OFFS):
        ts = lax.rem(a + da, 2) * 4 + lax.rem(b + db, 4)
        for o in range(3):
            at = pl.ds(pl.multiple_of(o * 1024 + ts * 128, 128), 128)
            gtw_o[:, at] = rfa[n, :, o * 128 : o * 128 + 128]
        gew_o[:, pl.ds(pl.multiple_of(ts * 512, 512), 512)] = rfm[n]
    total = rst[0]
    for n in range(1, 8):
        total += rst[n]
    small_o[0:4, :] = total[0:4, :]
    source = lax.rem(2 * t + k, 8)
    bias_rows = jnp.zeros((2, 128), F32)
    for n, (da, db) in enumerate(OFFS):
        ts = lax.rem(a + da, 2) * 4 + lax.rem(b + db, 4)
        bias_rows = jnp.where(ts == source, rst[n, 4:6, :], bias_rows)
    small_o[4:5, :] = jnp.where(a == 0, bias_rows[0:1], bias_rows[1:2])
    small_o[5:6, :] = st[t, 6:7, :]
    small_o[6:7, :] = st[t, 7:8, :]
    small_o[7:8, :] = jnp.zeros((1, 128), F32)
    send.finish()


def finish(mixed, xs, gs, first, p1, p2, waq, wbo, grads, sums_a, g1, bias):
    tok = ((8, 128, 1024), BF)
    shapes = [
        ((8, 128, 256), BF),
        ((8, 128, 256), BF),
        tok,
        tok,
        tok,
        tok,
        tok,
        tok,
        tok,
        ((1024, 128), BF),
        ((1024, 384), BF),
        ((4, 128, 1024), BF),
        ((2, 3, 128, 1024), BF),
        ((4, 128, 1024), BF),
        ((3, 128, 1024), BF),
        ((128, 1024), BF),
        ((128, 1024), BF),
        ((8, 128, 512), BF),
        ((8, 128, 512), BF),
        ((8, 128, 512), BF),
        ((3, 2, 128, 512), BF),
        ((2, 128, 512), BF),
        ((128, 512), BF),
        ((8, 8, 512), F32),
        ((8, 8, 512), F32),
        ((1024, 384), F32),
        ((128, 1024), F32),
        ((2, 8, 64, 512), BF),
        ((8, 64, 512), BF),
        ((8, 64, 512), BF),
        ((3, 2, 64, 512), BF),
        ((2, 64, 512), BF),
        ((64, 512), BF),
        ((8, 8, 384), F32),
        ((8, 8, 384), F32),
        ((8, 1024), F32),
        ((8, 1024), F32),
        ((8, 1024), F32),
        ((3, 8, 1024), F32),
        ((8, 1024), F32),
        ((8, 1024), F32),
        ((8, 8, 128), F32),
        ((8, 8, 128), F32),
    ]
    return pl.pallas_call(
        finish_kernel,
        out_shape=(
            jax.ShapeDtypeStruct((128, 1024), BF),
            jax.ShapeDtypeStruct((128, 1024), F32),
            jax.ShapeDtypeStruct((8, 3072), F32),
            jax.ShapeDtypeStruct((8, 4096), F32),
            jax.ShapeDtypeStruct((8, 1024), F32),
            jax.ShapeDtypeStruct((32, 1024), F32),
            jax.ShapeDtypeStruct((16, 128), F32),
        ),
        in_specs=[ANY] * 6 + [VM] * 2 + [ANY] + [VM] * 3,
        out_specs=(VM,) * 7,
        scratch_shapes=[pltpu.VMEM(shape, kind) for shape, kind in shapes]
        + [
            pltpu.SemaphoreType.DMA((SUM_COPIES,)),
            pltpu.SemaphoreType.DMA((SUM_COPIES,)),
            pltpu.SemaphoreType.DMA((7,)),
        ],
        compiler_params=pltpu.CompilerParams(
            collective_id=1, has_side_effects=True, vmem_limit_bytes=56 * MIB
        ),
        name="finish",
    )(mixed, xs, gs, first, p1, p2, waq, wbo, grads, sums_a, g1, bias)


def shards(
    tokens_in,
    positions,
    block_pairs,
    first_gain,
    first_bias,
    second_gain,
    second_bias,
    triple_weight,
    triple_bias,
    output_weight,
    output_bias,
    expand_weight,
    expand_bias,
    shrink_weight,
    shrink_bias,
    cotangent,
):
    c = lax.axis_index("ctx")
    t, k = c // 2, c % 2
    x, g = tokens_in.reshape(128, 1024), cotangent.reshape(128, 1024)

    def cut(v, at, size, dim):
        return lax.dynamic_slice_in_dim(v, at, size, dim)

    wa = jnp.concatenate(
        [cut(triple_weight, o * 1024 + t * 128, 128, 1) for o in range(3)]
        + [cut(expand_weight, t * 512, 512, 1)],
        axis=1,
    )
    wb = jnp.concatenate(
        [cut(output_weight, t * 128, 128, 0), cut(shrink_weight, t * 512, 512, 0)], axis=0
    )
    tb = cut(triple_bias.reshape(3, 1024), t * 128, 128, 1).reshape(1, 384)
    eb = cut(expand_bias, t * 512, 512, 0).reshape(1, 512)
    a, b = t // 4, t % 4
    chip = jnp.stack([((a + da) % 2) * 4 + (b + db) % 4 for da, db in OFFS])
    order = jnp.take(block_pairs.reshape(8, 2, 2), chip, axis=0).transpose(1, 0, 2)
    rates = 1.0 / BASE ** (jnp.arange(0, 16, 2, dtype=F32) / 16)

    def turns(pos):
        angles = rates[:, None] * pos.astype(F32)[None, :]
        return jnp.concatenate([jnp.cos(angles), jnp.sin(angles)], axis=0)

    own_blocks = lax.dynamic_index_in_dim(order, k, 0, keepdims=False).reshape(16)
    cs_own = turns(jnp.take(positions.reshape(32, 64), own_blocks, axis=0).reshape(1024))
    cs_all = turns(positions.reshape(2048))
    g1, b1 = first_gain.reshape(1, 1024), first_bias.reshape(1, 1024)
    g2, b2 = second_gain.reshape(1, 1024), second_bias.reshape(1, 1024)

    pack, xs, gs, first, p1, p2, waq, wbo, grads, sm = gather(
        x, g, wa, wb, tb, eb, g1, b1, g2, b2, cs_own
    )
    mixed = attention(order.reshape(32), pack.reshape(32, 64, 256), cs_all)
    bias = (output_bias + shrink_bias).reshape(1, 1024)
    act, tok, gtw, gew, gow, gsw, small = finish(
        mixed.reshape(2, 8, 128, 256), xs, gs, first, p1, p2, waq, wbo, grads, sm, g1, bias
    )
    f = lax.axis_index("fsdp")
    eight = cut(small, k * 64 + f * 8, 8, 1)
    sixteen = cut(small[4], f * 16, 16, 0)
    wide = cut(small[8:12].reshape(512), k * 256 + f * 32, 32, 0)
    return (
        act.reshape(tokens_in.shape),
        tok.reshape(tokens_in.shape),
        eight[0],
        eight[1],
        eight[2],
        eight[3],
        gtw,
        sixteen,
        eight[6],
        gow,
        eight[5],
        gew,
        wide,
        gsw,
        eight[5],
    )


def solution(mesh):
    return jax.shard_map(
        shards,
        mesh=mesh,
        in_specs=(
            P("fsdp", "ctx", None, None, None),
            P("fsdp", None),
            P(),
            P(),
            P(),
            P(),
            P(),
            P("fsdp", None),
            P(),
            P(None, "fsdp"),
            P(),
            P("fsdp", None),
            P(),
            P(None, "fsdp"),
            P(),
            P("fsdp", "ctx", None, None, None),
        ),
        out_specs=(
            P("fsdp", "ctx", None, None, None),
            P("fsdp", "ctx", None, None, None),
            P(("ctx", "fsdp")),
            P(("ctx", "fsdp")),
            P(("ctx", "fsdp")),
            P(("ctx", "fsdp")),
            P(("ctx", "fsdp"), None),
            P(("ctx", "fsdp")),
            P(("ctx", "fsdp")),
            P(("ctx", "fsdp"), None),
            P(("ctx", "fsdp")),
            P(("ctx", "fsdp"), None),
            P(("ctx", "fsdp")),
            P(("ctx", "fsdp"), None),
            P(("ctx", "fsdp")),
        ),
        check_vma=False,
    )
```

time: 217 us -> 152 us (0.70)
  Pallas kernels: 186 us -> 122 us
    pallas_call x6 -> x2, Pallas kernels: 152 us -> 106 us  [the longest x1 53.3 us: gather(): pl.pallas_call(gather_kernel, out_shape=(jax.ShapeDtypeStruct((2, 8, 128,...]
    pallas_call x1, Pallas kernels: 34.2 us -> 16.5 us  [attention(): pl.pallas_call(attention_kernel, out_shape=jax.ShapeDtypeStruct((32, 64,...]
    slice x6 -> x1, local copies, waits for them, and re-layouts: 4.24 us -> 0.68 us  [shards(): sixteen = cut(small[4], f * 16, 16, 0)]
    dynamic_slice x5 -> x7, local copies, waits for them, and re-layouts: 3.9 us -> 5 us  [cut(): return lax.dynamic_slice_in_dim(v, at, size, dim)]
    unnamed x26 -> x22, local copies, waits for them, and re-layouts: 10.6 us -> 10.3 us
where the time goes in v2:
time: 152 us; the launch traced here: 151 us
  Pallas kernels  122 us (80%)
  local copies, waits for them, and re-layouts  21.9 us (14%)
  other arithmetic  5.54 us (4%)
    pallas_call x1, Pallas kernels, gather(): pl.pallas_call(gather_kernel, out_shape=(jax.ShapeDtypeStruct((2, 8, 128,...  53.3 us
    pallas_call x1, Pallas kernels, finish(): pl.pallas_call(finish_kernel, out_shape=(jax.ShapeDtypeStruct((128, 1024)...  52.3 us
    pallas_call x1, Pallas kernels, attention(): pl.pallas_call(attention_kernel, out_shape=jax.ShapeDtypeStruct((32, 64,...  16.5 us
    unnamed x22, local copies, waits for them, and re-layouts  10.3 us
    dynamic_slice x7, local copies, waits for them, and re-layouts, cut(): return lax.dynamic_slice_in_dim(v, at, size, dim)  5 us

profile of v2, /device:TPU:0, one launch (start us, length us, event | category | flops | bytes accessed | tf_op | source)
XLA Modules:
  0.0 150.5 jit_solution(14551232618154145033)
XLA Ops:
  0.6 0.0 copy-start
  0.8 0.1 stack.53
  0.9 0.1 stack.62
  1.0 0.8 copy.36
  1.8 0.6 gather_fusion
  2.4 0.1 broadcast_select_fusion
  2.5 0.5 broadcast.123
  3.0 0.7 fusion.5
  3.6 0.1 reshape.512
  3.7 1.4 fusion.6
  5.2 0.1 reshape.511
  5.3 0.6 gather_fusion.1
  5.8 0.1 reshape.510
  5.9 0.1 select_convert_fusion
  6.0 0.1 convert_element_type.15
  6.1 0.2 multiply_cosine_fusion.1
  6.3 0.6 pad_maximum_fusion.3.cs
  6.9 0.8 constant_dynamic-slice_fusion.9
  7.7 0.7 pad_maximum_fusion.wa
  8.5 0.9 constant_dynamic-slice_fusion.4
  9.4 0.0 copy-start.3
  9.4 0.0 copy-start.4
  9.4 0.8 constant_dynamic-slice_fusion.5
  10.2 0.7 pad_maximum_fusion.1.wb
  10.9 0.0 copy-done.2
  10.9 0.6 copy.39
  11.4 1.3 dynamic_slice.44
  12.8 53.3 %gather.15 = (bf16[2,8,128,256]{3,2,1,0:T(8,128)(2,1)}, bf16[8,128,1024]{2,1,0:T(8,128)(2,1)}, bf16[8,128,1024]{2,1,0:T(8,128)(2,1)}, bf16[8,128,1024]{2,1,0:T(8...) custom-call(bf16[128,1024]{1,0:T(8,128)(2,1)} %bitcast.63, ...), custom_call_target="tpu_custom_call" | custom-call | tf_op jit(solution)/shard_map/gather/pallas_call | solution.py:246
  66.1 0.1 fusion.7
  66.2 0.6 reshape.500.order
  66.8 0.3 multiply_cosine_fusion
  67.1 0.7 pad_maximum_fusion.2.cs
  67.8 16.5 %attention.1 = bf16[32,64,256]{2,1,0:T(8,128)(2,1)} custom-call(s32[32]{0:T(128)} %reshape.500.order, bf16[32,64,256]{2,1,0:T(8,128)(2,1)} %bitcast.60, f32[16,2048]{1,0:T(8,128)} %pad_maximum_fusion.2.cs), custom_call_target="tpu_custom_call" | custom-call | tf_op jit(solution)/shard_map/attention/pallas_call | solution.py:412
  84.3 0.6 add.184
  84.9 52.3 %finish.1 = (bf16[128,1024]{1,0:T(8,128)(2,1)}, f32[128,1024]{1,0:T(8,128)}, f32[8,3072]{1,0:T(8,128)}, f32[8,4096]{1,0:T(8,128)}, f32[8,1024]{1,0:T(8,128)}, /*index=5*/f32[32,1024]{1,0:T(8,128)}, f32[16,128]{1,0:T(8,128)}) custom-call(bf16[2,8,128,256]{3,2,1,0:T(8,128)(2,1)} %bitcast.59, bf16[8,128,1024]{2,1,0:T(8,128)(2,1)} %get-tuple-element.33.xi, ...), custom_call_target="tpu_custom_call" | custom-call | tf_op jit(solution)/shard_map/finish/pallas_call | solution.py:703
  137.3 1.5 %dynamic-slice_bitcast_fusion = (f32[8]{0:T(128)S(1)}, f32[8]{0:T(128)}, f32[8]{0:T(128)}, f32[8]{0:T(128)}, f32[8]{0:T(128)}, /*index=5*/f32[8]{0:T(128)}) fusion(f32[16,128]{1,0:T(8,128)} %get-tuple-element.44, s32[]{:T(128)S(6)} %add.200, s32[]{:T(128)S(6)} %select_n.166, s32[]{:T(128)S(6)} %add.199, s32[]{:T(128)S(6)} %add.198, s32[]{:T(128)S(6)} %add.197, ...), kind=kLoop, calls=%fused_computation.37 | loop fusion | bytes 408 | tf_op jit(solution)/shard_map/squeeze | solution.py:802
  138.8 0.7 slice_bitcast_fusion
  139.5 0.6 dynamic_slice.48
  140.0 0.7 slice.29
  140.7 0.6 fusion.1
  141.3 0.5 copy.47
  141.8 1.7 %copy.48 = bf16[1,1,2,64,1024]{4,3,2,1,0:T(8,128)(2,1)} copy(bf16[1,1,2,64,1024]{4,3,2,1,0:T(8,128)(2,1)} %bitcast.62) | data formatting | bytes 524288
  143.5 1.9 %copy.49 = f32[1,1,2,64,1024]{4,3,2,1,0:T(8,128)} copy(f32[1,1,2,64,1024]{4,3,2,1,0:T(8,128)} %bitcast.61) | data formatting | bytes 1048576
  145.4 1.5 %copy.50 = f32[8,3072]{1,0:T(8,128)} copy(f32[8,3072]{1,0:T(8,128)} %get-tuple-element.117) | data formatting | bytes 196608
  146.9 1.4 copy.51
  148.3 1.6 %copy.52 = f32[8,4096]{1,0:T(8,128)} copy(f32[8,4096]{1,0:T(8,128)} %get-tuple-element.122) | data formatting | bytes 262144
  149.9 0.0 copy-done.1
  149.9 0.7 copy.53
  (18 shorter events, 0.1 us)
Async XLA Ops:
  0.6 7.1 %copy-start = (bf16[128,4096]{1,0:T(8,128)(2,1)S(1)}, bf16[128,4096]{1,0:T(8,128)(2,1)}, u32[]{:S(2)}) copy-start(bf16[128,4096]{1,0:T(8,128)(2,1)} %param.27) | copy-start | bytes 3145732
  0.7 10.2 %copy-start.2 = (f32[3072]{0:T(1024)S(1)}, f32[3072]{0:T(1024)}, u32[]{:S(2)}) copy-start(f32[3072]{0:T(1024)} %param.24) | copy-start | bytes 36868
  9.4 74.9 %copy-start.3 = (f32[1024]{0:T(1024)S(1)}, f32[1024]{0:T(1024)}, u32[]{:S(2)}) copy-start(f32[1024]{0:T(1024)} %param.26) | copy-start | bytes 12292
  9.4 74.9 %copy-start.4 = (f32[1024]{0:T(1024)S(1)}, f32[1024]{0:T(1024)}, u32[]{:S(2)}) copy-start(f32[1024]{0:T(1024)} %param.30) | copy-start | bytes 12292
  137.2 12.6 %copy-start.1 = (f32[32,1024]{1,0:T(8,128)S(1)}, f32[32,1024]{1,0:T(8,128)}, u32[]{:S(2)}) copy-start(f32[32,1024]{1,0:T(8,128)} %get-tuple-element.124) | copy-start | bytes 393220
  138.8 11.7 %copy-start.5 = (f32[8]{0:T(128)}, f32[8]{0:T(128)S(1)}, u32[]{:S(2)}) copy-start(f32[8]{0:T(128)S(1)} %get-tuple-element.121) | copy-start | bytes 100

commit v3 on v0

v3 whole, which is shorter than its diff:
```python
import math

import jax
import jax.numpy as jnp
import numpy as np
from jax import lax
from jax.experimental import pallas as pl
from jax.experimental.pallas import tpu as pltpu
from jax.sharding import PartitionSpec as P

MESH = pl.DeviceIdType.MESH
BF, F32 = jnp.bfloat16, jnp.float32
EPS = 1e-05
BASE = 10000.0
MIB = 1 << 20
SCALE = 0.125
TILE = 256
RATES = 1.0 / BASE ** (np.arange(0, 16, 2, dtype=np.float32) / 16)

ZL, KC, ZH = (1, 0, 0, 0, 0), (0, 0, 1, 0, 0), (0, 0, 0, 0, 1)
YS = {i: (0, i, 0, 0, 0) for i in (1, 2, 3)}
XS = {i: (0, 0, 0, i, 0) for i in (1, 2, 3)}
NEAR_FIRST = (1, 3, 2)
OFFS = ((0, 0), (0, 1), (0, 3), (0, 2), (1, 0), (1, 1), (1, 3), (1, 2))
SLOT = {off: n for n, off in enumerate(OFFS)}


def origin(da, i):
    return SLOT[(da, (4 - i) % 4)]


def chips(n):
    return (*OFFS[n], 0, 0, 0)


def coords():
    c, f = lax.axis_index("ctx"), lax.axis_index("fsdp")
    return lax.div(c, 8), lax.rem(lax.div(c, 2), 4), lax.rem(c, 2), lax.div(f, 2), lax.rem(f, 2)


def device_at(me, off):
    a, b, k, x, h = (lax.rem(p + o, n) for p, o, n in zip(me, off, (2, 4, 2, 4, 2)))
    return ((a * 4 + b) * 2 + k, x * 2 + h)


def barrier(me, offs):
    sem = pltpu.get_barrier_semaphore()
    for off in offs:
        pl.semaphore_signal(sem, inc=1, device_id=device_at(me, off), device_id_type=MESH)
    pl.semaphore_wait(sem, len(offs))


class Sender:
    def __init__(self, me, send_sems, recv_sems):
        self.me, self.send_sems, self.recv_sems, self.copies = me, send_sems, recv_sems, []

    def __call__(self, src, dst, off):
        i = len(self.copies)
        copy = pltpu.make_async_remote_copy(
            src_ref=src,
            dst_ref=dst,
            send_sem=self.send_sems.at[i],
            recv_sem=self.recv_sems.at[i],
            device_id=device_at(self.me, off),
            device_id_type=MESH,
        )
        copy.start()
        self.copies.append(copy)
        return copy

    def finish(self):
        for copy in self.copies:
            copy.wait_send()


def nt(left, right):
    return lax.dot_general(left, right, (((1,), (1,)), ((), ())), preferred_element_type=F32)


def tn(left, right):
    return lax.dot_general(left, right, (((0,), (0,)), ((), ())), preferred_element_type=F32)


def nn(left, right):
    return jnp.dot(left, right, preferred_element_type=F32)


def down(v):
    return jnp.sum(v, axis=0, keepdims=True)


def lanes(shape):
    return lax.broadcasted_iota(jnp.int32, shape, 1)


def roll(v, shift):
    return pltpu.roll(v, shift, 1)


ANY = pl.BlockSpec(memory_space=pl.ANY)
VM = pl.BlockSpec(memory_space=pltpu.VMEM)


COPIES = 45 + 22 + 16 + 10 + 5 + 21 + 28
LOADS = 8
TOK = (8, 128, 1024)
SCRATCH = (
    ("xs", TOK, BF),
    ("gs", TOK, BF),
    ("first", TOK, BF),
    ("second", (1024, 1024), BF),
    ("mus", (1024, 1), F32),
    ("invs", (1024, 1), F32),
    ("was", (1024, 896), BF),
    ("wos", (128, 1024), BF),
    ("wss", (512, 1024), BF),
    ("slope", (1024, 512), F32),
    ("hidden", (1024, 512), BF),
    ("dexp", (1024, 512), BF),
    ("cst", (16, 2048), F32),
    ("cs3", (32, 16, 128), F32),
    ("pk", (32, 64, 256), BF),
    ("th", (16, 64, 256), BF),
    ("pd", (32, 64, 128), BF),
    ("td", (16, 64, 128), BF),
    ("kq", (2048, 128), BF),
    ("qz", (2048, 128), BF),
    ("vz", (2048, 128), BF),
    ("vt", (64, 2048), BF),
    ("kt", (64, 2048), BF),
    ("dt", (64, 2048), BF),
    ("sc", (2048, TILE), F32),
    ("es", (36, TILE, TILE), BF),
    ("acc", (2048, 128), F32),
    ("mixs", (64, 2048), F32),
    ("rsum", (8, TILE), F32),
    ("ot", (32, 64, 128), BF),
    ("o_own", (16, 64, 128), BF),
    ("o_away", (16, 64, 128), BF),
    ("o_got", (16, 64, 128), BF),
    ("dd", (32, 64, 256), BF),
    ("d_own", (16, 64, 256), BF),
    ("d_away", (16, 64, 256), BF),
    ("d_got", (16, 64, 256), BF),
    ("attn", (1024, 128), BF),
    ("dtr", (1024, 384), BF),
    ("act", TOK, BF),
    ("act_rz", (4, 64, 1024), BF),
    ("act_ry", (2, 3, 64, 1024), BF),
    ("act_t", (4, 64, 1024), BF),
    ("act_rt", (3, 64, 1024), BF),
    ("act_w", (64, 1024), BF),
    ("act_rw", (64, 1024), BF),
    ("dhat", TOK, BF),
    ("dhat_rz", (4, 64, 1024), BF),
    ("dhat_ry", (2, 3, 64, 1024), BF),
    ("dhat_t", (4, 64, 1024), BF),
    ("dhat_rt", (3, 64, 1024), BF),
    ("dhat_w", (64, 1024), BF),
    ("dhat_rw", (64, 1024), BF),
    ("gsh", (512, 1024), F32),
    ("gm", (2, 8, 128, 512), BF),
    ("gm_r", (8, 128, 512), BF),
    ("gm_u", (8, 128, 512), BF),
    ("gm_ru", (3, 2, 128, 512), BF),
    ("gm_v", (2, 128, 512), BF),
    ("gm_rv", (128, 512), BF),
    ("gm_f", (8, 8, 512), F32),
    ("gm_rf", (8, 8, 512), F32),
    ("go", (128, 1024), F32),
    ("ga", (2, 8, 64, 512), BF),
    ("ga_r", (8, 64, 512), BF),
    ("ga_u", (8, 64, 512), BF),
    ("ga_ru", (3, 2, 64, 512), BF),
    ("ga_v", (2, 64, 512), BF),
    ("ga_rv", (64, 512), BF),
    ("ga_f", (8, 8, 384), F32),
    ("ga_rf", (8, 8, 384), F32),
    ("sm", (8, 1024), F32),
    ("sm_r", (8, 1024), F32),
    ("sm_u", (8, 1024), F32),
    ("sm_ru", (3, 8, 1024), F32),
    ("sm_v", (8, 1024), F32),
    ("sm_rv", (8, 1024), F32),
    ("sm_f", (8, 8, 128), F32),
    ("sm_rf", (8, 8, 128), F32),
)
ZR, YR = slice(0, 64), slice(64, 128)


class Refs:
    pass


class RowSum:
    def __init__(self, send, src, rz, ry, t, rt, w, rw):
        self.send, self.src = send, src
        self.rz, self.ry, self.t, self.rt, self.w, self.rw = rz, ry, t, rt, w, rw
        self.z, self.y, self.on = {}, {}, []

    def start(self, n):
        da, db = OFFS[n]
        if da:
            self.z[n - 4] = self.send(self.src.at[n, ZR], self.rz.at[n - 4], ZL)
        if db:
            j = NEAR_FIRST.index(db)
            self.y[n] = self.send(self.src.at[n, YR], self.ry.at[da, j], YS[db])

    def middle(self):
        for m in (1, 2, 3):
            self.z[m].wait_recv()
            self.t[m] = (self.src[m, ZR].astype(F32) + self.rz[m].astype(F32)).astype(BF)
            db = OFFS[m][1]
            j = NEAR_FIRST.index(db)
            self.on.append(self.send(self.t.at[m], self.rt.at[j], YS[db]))
        for n in (5, 6, 7):
            self.y[n].wait_recv()
        total = self.src[4, YR].astype(F32)
        for j in range(3):
            total += self.ry[1, j].astype(F32)
        self.w[...] = total.astype(BF)
        self.on.append(self.send(self.w, self.rw, ZL))

    def end(self):
        self.z[0].wait_recv()
        for n in (1, 2, 3):
            self.y[n].wait_recv()
        for copy in self.on:
            copy.wait_recv()
        upper = self.src[0, ZR].astype(F32) + self.rz[0].astype(F32)
        lower = self.src[0, YR].astype(F32) + self.rw[...].astype(F32)
        for j in range(3):
            upper += self.rt[j].astype(F32)
            lower += self.ry[0, j].astype(F32)
        return jnp.concatenate([upper, lower], axis=0)


class WeightSum:
    def __init__(self, send, me, kind, r, u, ru, v, rv, f, rf):
        self.send, self.me, self.kind = send, me, kind
        self.r, self.u, self.ru, self.v, self.rv, self.f, self.rf = r, u, ru, v, rv, f, rf

    def core(self, src):
        self.src = src
        self.sent = [self.send(src.at[1 - self.me[2]], self.r, KC)]

    def wait(self):
        for copy in self.sent:
            copy.wait_recv()

    def along_x(self):
        k, x = self.me[2], self.me[3]
        self.wait()

        def one(f, _):
            self.u[f] = (self.src[k, f].astype(F32) + self.r[f].astype(F32)).astype(self.kind)
            return 0

        lax.fori_loop(0, 8, one, 0)
        self.sent = []
        for j, i in enumerate(NEAR_FIRST):
            there = pl.ds(lax.rem(x + i, 4) * 2, 2)
            self.sent.append(self.send(self.u.at[there], self.ru.at[j], XS[i]))

    def along_z(self):
        x, h = self.me[3], self.me[4]
        self.wait()
        for hh in range(2):
            total = self.u[x * 2 + hh].astype(F32)
            for j in range(3):
                total += self.ru[j, hh].astype(F32)
            self.v[hh] = total.astype(self.kind)
        self.sent = [self.send(self.v.at[1 - h], self.rv, ZH)]

    def total(self):
        self.wait()
        return self.v[self.me[4]].astype(F32) + self.rv[...].astype(F32)

    def to_owners(self):
        a, b = self.me[0], self.me[1]
        self.sent = []
        for n in range(1, 8):
            da, db = OFFS[n]
            there = lax.rem(a + da, 2) * 4 + lax.rem(b + db, 4)
            self.sent.append(self.send(self.f.at[there], self.rf.at[origin(da, db)], chips(n)))
        self.rf[0] = self.f[a * 4 + b]


def block_kernel(
    pairs, pos, x, g, tw, ow, ew, sw, tb, eb, g1, b1, g2, b2, bias,
    act_o, tok_o, gtw_o, gew_o, gow_o, gsw_o, small_o, *scratch,
):
    s = Refs()
    for (name, _, _), ref in zip(SCRATCH, scratch):
        setattr(s, name, ref)
    ss, rs, ls, inv_slot = scratch[len(SCRATCH) :]
    me = coords()
    a, b, k, xx, h = me
    t, f = a * 4 + b, xx * 2 + h
    local = []

    def load(src, dst):
        copy = pltpu.make_async_copy(src, dst, ls.at[len(local)])
        copy.start()
        local.append(copy)

    def cols_at(ff):
        return pl.ds(pl.multiple_of(ff * 128, 128), 128)

    def pieces(ff):
        rows = pl.ds(pl.multiple_of(ff * 128 + k * 64, 64), 64)
        return (
            s.was.at[rows],
            s.wos.at[pl.ds(pl.multiple_of(k * 64, 64), 64), cols_at(ff)],
            s.wss.at[pl.ds(pl.multiple_of(k * 256, 256), 256), cols_at(ff)],
        )

    half = pl.ds(pl.multiple_of(k * 64, 64), 64)
    mine = pl.ds(pl.multiple_of(f * 128 + k * 64, 64), 64)
    for o in range(3):
        load(
            tw.at[half, pl.ds(pl.multiple_of(o * 1024 + t * 128, 128), 128)],
            s.was.at[mine, pl.ds(o * 128, 128)],
        )
    load(ew.at[half, pl.ds(pl.multiple_of(t * 512, 512), 512)], s.was.at[mine, pl.ds(384, 512)])
    load(ow.at[pl.ds(pl.multiple_of(t * 128 + k * 64, 64), 64)], pieces(f)[1])
    load(sw.at[pl.ds(pl.multiple_of(t * 512 + k * 256, 256), 256)], pieces(f)[2])
    load(x, s.xs.at[0])
    load(g, s.gs.at[0])
    barrier(me, [*(chips(n) for n in range(1, 8)), *XS.values(), ZH, KC])
    send = Sender(me, ss, rs)

    def send_pieces(ff, off):
        return [send(ref, ref, off) for ref in pieces(ff)]

    def wait(copies):
        for copy in copies:
            copy.wait_recv()

    def tokens_out(src, dst):
        z = [send(src.at[rows], dst.at[4, rows], ZL) for rows in (ZR, YR)]
        y = {i: send(src, dst.at[origin(0, i)], YS[i]) for i in NEAR_FIRST}
        return z, y

    def tokens_on_y(z, dst):
        z[0].wait_recv()
        return {i: send(dst.at[4, ZR], dst.at[origin(1, i), ZR], YS[i]) for i in NEAR_FIRST}

    def tokens_on_z(y, dst):
        on = {}
        for i in NEAR_FIRST:
            y[i].wait_recv()
            on[i] = send(dst.at[origin(0, i), YR], dst.at[origin(1, i), YR], ZL)
        return on

    for copy in local:
        copy.wait()
    wz = send_pieces(f, ZH)
    wx = {i: send_pieces(f, XS[i]) for i in NEAR_FIRST}
    x_z, x_y = tokens_out(x, s.xs)
    weights = send_pieces(f, KC)

    def chip_at(n):
        da, db = OFFS[n]
        return lax.rem(a + da, 2) * 4 + lax.rem(b + db, 4)

    def block_of(kk, n, j):
        return pairs[j, chip_at(n) * 2 + kk]

    held = [block_of(kk, n, j) for kk in range(2) for n in range(8) for j in range(2)]

    def find(j, _):
        at = jnp.int32(0)
        for q, block in enumerate(held):
            at = jnp.where(block == j, q, at)
        inv_slot[j] = at
        return 0

    lax.fori_loop(0, 32, find, 0)
    row = lax.broadcasted_iota(jnp.int32, (8, 1), 0)
    rates = jnp.zeros((8, 1), F32)
    for j in range(8):
        rates = jnp.where(row == j, float(RATES[j]), rates)
    angles = rates * pos[...].astype(F32)
    s.cst[0:8, :] = jnp.cos(angles)
    s.cst[8:16, :] = jnp.sin(angles)
    low16 = lanes((16, 128)) < 64
    for j in range(16):
        both = s.cst[:, j * 128 : j * 128 + 128]
        turned = roll(both, 64)
        s.cs3[2 * j] = jnp.where(low16, both, turned)
        s.cs3[2 * j + 1] = jnp.where(low16, turned, both)
    s.sm[...] = jnp.zeros_like(s.sm)

    def norm(n):
        rows = slice(n * 128, n * 128 + 128)
        v = s.xs[n].astype(F32)
        mean = jnp.mean(v, axis=1, keepdims=True)
        centred = v - mean
        inv = lax.rsqrt(jnp.mean(centred * centred, axis=1, keepdims=True) + EPS)
        s.mus[rows, :] = mean
        s.invs[rows, :] = inv
        x_hat = centred * inv
        s.first[n] = (x_hat * g1[...] + b1[...]).astype(BF)
        s.second[rows, :] = (x_hat * g2[...] + b2[...]).astype(BF)

    norm(0)
    fz = xx * 2 + (1 - h)
    wait(wz)
    wxz = {i: send_pieces(fz, XS[i]) for i in NEAR_FIRST}
    weights += send_pieces(fz, KC)
    x_yz = tokens_on_y(x_z, s.xs)
    x_zy = tokens_on_z(x_y, s.xs)
    g_z, g_y = tokens_out(g, s.gs)
    for n in (1, 2, 3):
        norm(n)
    for i in NEAR_FIRST:
        wait(wx[i])
        weights += send_pieces(lax.rem(xx + 4 - i, 4) * 2 + h, KC)
    x_z[1].wait_recv()
    norm(4)
    for i in NEAR_FIRST:
        wait(wxz[i])
        weights += send_pieces(lax.rem(xx + 4 - i, 4) * 2 + (1 - h), KC)
    for i, n in ((3, 5), (1, 6), (2, 7)):
        x_yz[i].wait_recv()
        x_zy[i].wait_recv()
        norm(n)
    g_yz = tokens_on_y(g_z, s.gs)
    wait(weights)

    low = lanes((256, 128)) < 64
    low128 = lanes((16, 128)) < 64
    early = (lanes((256, 128)) & 63) < 8
    bias_at = [tb[0:1, pl.ds(pl.multiple_of(o * 1024 + t * 128, 128), 128)] for o in range(3)]
    triple_bias = jnp.concatenate(bias_at, axis=1)
    expand_bias = eb[0:1, pl.ds(pl.multiple_of(t * 512, 512), 512)]

    def deal(tiles, own, away, to, m):
        quads = pl.ds(4 * m, 4)
        for j, (head0, head1) in enumerate(tiles):
            at = slice(j * 128, j * 128 + 128)
            keep = jnp.where(k == 0, head0, head1).astype(BF).reshape(4, 64, 128)
            give = jnp.where(k == 0, head1, head0).astype(BF).reshape(4, 64, 128)
            own[pl.ds(k * 16 + 4 * m, 4), :, at] = keep
            away[quads, :, at] = give
        return send(away.at[quads], to.at[pl.ds(k * 16 + 4 * m, 4)], KC)

    def attend_in(m):
        rows = slice(m * 256, m * 256 + 256)
        tables = []
        for n in (2 * m, 2 * m + 1):
            tables.append(
                jnp.where(low128, s.cs3[block_of(k, n, 0)], s.cs3[block_of(k, n, 1)])
            )
        cs = jnp.concatenate(tables, axis=1)
        cos, sin = cs[0:8], cs[8:16]
        one, zero = jnp.ones((48, 256), F32), jnp.zeros((48, 256), F32)
        tc = jnp.concatenate([cos, cos, one, cos, cos, one], axis=0).T
        ts = jnp.concatenate([-sin, sin, zero, -sin, sin, zero], axis=0).T

        def turn(v):
            return v * tc + jnp.where(early, roll(v, 120), roll(v, 8)) * ts

        left = s.first[2 * m : 2 * m + 2].reshape(256, 1024)
        triple = nn(left, s.was[:, 0:384]) + triple_bias
        query, key, value = turn(triple[:, 0:128]), turn(triple[:, 128:256]), triple[:, 256:384]
        zeros = jnp.zeros_like(value)
        return deal(
            (
                (jnp.where(low, query, roll(key, 64)), jnp.where(low, roll(query, 64), key)),
                (jnp.where(low, value, zeros), jnp.where(low, roll(value, 64), zeros)),
            ),
            s.pk,
            s.th,
            s.pk,
            m,
        )

    heads_in = [attend_in(m) for m in range(4)]
    g_zy = tokens_on_z(g_y, s.gs)

    for m in range(4):
        rows = slice(m * 256, m * 256 + 256)
        u = nn(s.second[rows, :], s.was[:, 384:896]) + expand_bias
        cdf = 0.5 * (1.0 + lax.erf(u * math.sqrt(0.5)))
        pdf = jnp.exp(-0.5 * u * u) * (1.0 / math.sqrt(2.0 * math.pi))
        s.hidden[rows, :] = (u * cdf).astype(BF)
        s.slope[rows, :] = cdf + u * pdf

    wait(heads_in)
    low64 = lanes((64, 128)) < 64

    def place(j, _):
        at = pl.ds(pl.multiple_of(j * 64, 64), 64)
        both = s.pk[inv_slot[j], :, 0:128].astype(F32)
        value = s.pk[inv_slot[j], :, 128:256].astype(F32)
        s.kq[at, :] = roll(both, 64).astype(BF)
        s.qz[at, :] = jnp.where(low64, both * SCALE, 0.0).astype(BF)
        s.vz[at, :] = roll(value, 64).astype(BF)
        return 0

    lax.fori_loop(0, 32, place, 0)
    for i in range(8):
        cols = slice(i * TILE, i * TILE + TILE)
        s.kt[:, cols] = s.kq[cols, :].astype(F32).T[0:64].astype(BF)
        s.vt[:, cols] = s.vz[cols, :].astype(F32).T[64:128].astype(BF)
    seen = lax.broadcasted_iota(jnp.int32, (TILE, TILE), 0) <= lanes((TILE, TILE))

    def folded(v, op):
        parts = [v[j * 8 : j * 8 + 8] for j in range(TILE // 8)]
        while len(parts) > 1:
            parts = [op(parts[j], parts[j + 1]) for j in range(0, len(parts), 2)]
        return parts[0]

    def tile(i, j):
        return i * (i + 1) // 2 + j

    def at_tile(i):
        return slice(i * TILE, i * TILE + TILE)

    for i in range(8):
        cols = at_tile(i)
        q_i = s.qz[cols, :]
        peak = None
        for j in range(i + 1):
            score = nt(s.kq[at_tile(j), :], q_i)
            if j == i:
                score = jnp.where(seen, score, -jnp.inf)
            s.sc[at_tile(j), :] = score
            high = folded(score, jnp.maximum)
            peak = high if peak is None else jnp.maximum(peak, high)
        peak = jnp.max(peak, axis=0, keepdims=True)
        total, mix = jnp.zeros((8, TILE), F32), jnp.zeros((64, TILE), F32)
        for j in range(i + 1):
            e = jnp.exp(s.sc[at_tile(j), :] - peak)
            total += folded(e, jnp.add)
            e_low = e.astype(BF)
            s.es[tile(i, j)] = e_low
            mix += nn(s.vt[:, at_tile(j)], e_low)
        inv = 1.0 / jnp.sum(total, axis=0, keepdims=True)
        mix *= inv
        s.rsum[i : i + 1, :] = inv
        s.mixs[:, cols] = mix
        out = jnp.concatenate([mix, jnp.zeros_like(mix)], axis=0).T
        s.ot[4 * i : 4 * i + 4] = out.astype(BF).reshape(4, 64, 128)
    for n in range(8):
        for j in range(2):
            s.o_own[2 * n + j] = s.ot[block_of(k, n, j)]
            s.o_away[2 * n + j] = s.ot[block_of(1 - k, n, j)]
    o_sent = send(s.o_away, s.o_got, KC)

    act = RowSum(send, s.act, s.act_rz, s.act_ry, s.act_t, s.act_rt, s.act_w, s.act_rw)
    o_sent.wait_recv()
    for m in (2, 3, 1, 0):
        rows = slice(m * 256, m * 256 + 256)
        own = s.o_own[4 * m : 4 * m + 4].reshape(256, 128).astype(F32)
        got = s.o_got[4 * m : 4 * m + 4].reshape(256, 128).astype(F32)
        head0, head1 = jnp.where(k == 0, own, got), jnp.where(k == 0, got, own)
        attn_low = jnp.where(low, head0, roll(head1, 64)).astype(BF)
        s.attn[rows, :] = attn_low
        out = nn(attn_low, s.wos[...]) + nn(s.hidden[rows, :], s.wss[...])
        s.act[2 * m : 2 * m + 2] = out.astype(BF).reshape(2, 128, 1024)
        act.start(2 * m)
        act.start(2 * m + 1)

    g_z[1].wait_recv()
    wait(g_yz.values())
    wait(g_zy.values())
    grads_in = []
    for m in range(4):
        dmix = nt(s.gs[2 * m : 2 * m + 2].reshape(256, 1024), s.wos[...])
        grads_in.append(deal(((dmix, roll(dmix, 64)),), s.pd, s.td, s.pd, m))

    def x_hat_of(m):
        rows = slice(m * 256, m * 256 + 256)
        v = s.xs[2 * m : 2 * m + 2].reshape(256, 1024).astype(F32)
        return (v - s.mus[rows, :]) * s.invs[rows, :]

    for m in range(4):
        rows = slice(m * 256, m * 256 + 256)
        grad = s.gs[2 * m : 2 * m + 2].reshape(256, 1024)
        dexp_low = (nt(grad, s.wss[...]) * s.slope[rows, :]).astype(BF)
        s.dexp[rows, :] = dexp_low
        d_second = nt(dexp_low, s.was[:, 384:896])
        s.dhat[2 * m : 2 * m + 2] = (d_second * g2[...]).astype(BF).reshape(2, 128, 1024)
        s.sm[2:3, :] += down(d_second * x_hat_of(m))
        s.sm[3:4, :] += down(d_second)
        s.sm[4:5, :] += down(grad.astype(F32))
        s.sm[5:6, 384:896] += down(dexp_low.astype(F32))

    gm = WeightSum(send, me, BF, s.gm_r, s.gm_u, s.gm_ru, s.gm_v, s.gm_rv, s.gm_f, s.gm_rf)
    ga = WeightSum(send, me, BF, s.ga_r, s.ga_u, s.ga_ru, s.ga_v, s.ga_rv, s.ga_f, s.ga_rf)
    s.slope[...] = tn(s.second[...], s.dexp[...])
    s.gsh[...] = tn(s.hidden[...], s.gs[...].reshape(1024, 1024))
    for kk in range(2):
        for ff in range(8):
            at = [(tt * 2 + kk) * 64 + ff * 8 for tt in range(8)]
            own = slice((kk * 8 + ff) * 32, (kk * 8 + ff) * 32 + 32)
            s.gm[kk, ff, 0:64, :] = jnp.concatenate(
                [s.slope[r : r + 8, :] for r in at], axis=0
            ).astype(BF)
            s.gm[kk, ff, 64:96, :] = s.gsh[own, 0:512].astype(BF)
            s.gm[kk, ff, 96:128, :] = s.gsh[own, 512:1024].astype(BF)
    gm.core(s.gm)

    wait(grads_in)

    def place_back(j, _):
        at = pl.ds(pl.multiple_of(j * 64, 64), 64)
        s.vz[at, :] = jnp.where(
            low64, s.pd[inv_slot[j]].astype(F32), s.vz[at, :].astype(F32)
        ).astype(BF)
        return 0

    lax.fori_loop(0, 32, place_back, 0)
    for i in range(8):
        cols = at_tile(i)
        s.dt[:, cols] = s.vz[cols, :].astype(F32).T[0:64].astype(BF)
    for i in range(8):
        cols = at_tile(i)
        scaled = (s.dt[:, cols].astype(F32) * s.rsum[i : i + 1, :]).astype(BF).astype(F32)
        inner = jnp.sum(s.mixs[:, cols] * scaled, axis=0, keepdims=True)
        d_i = jnp.concatenate([jnp.zeros_like(scaled), scaled], axis=0).T.astype(BF)
        right = jnp.concatenate([s.qz[cols, :], d_i], axis=0)
        dq = jnp.zeros((64, TILE), F32)
        for j in range(i + 1):
            rows = at_tile(j)
            e_low = s.es[tile(i, j)]
            ds = (e_low.astype(F32) * (nt(s.vz[rows, :], d_i) - inner)).astype(BF)
            both = nn(jnp.concatenate([ds, e_low], axis=1), right)
            s.acc[rows, :] = both if i == j else s.acc[rows, :] + both
            dq += nn(s.kt[:, rows], ds)
        s.mixs[:, cols] = dq * SCALE
        if i == 3:
            gm.along_x()
        if i == 6:
            act.middle()

    def turned_back(v, cols):
        cos, sin = s.cst[0:8, cols], s.cst[8:16, cols]
        f1, f2 = v[0:8], v[8:16]
        return [f1 * cos + f2 * sin, f2 * cos - f1 * sin, v[16:64]]

    for i in range(8):
        cols = at_tile(i)
        tail = s.acc[cols, :]
        both = turned_back(s.mixs[:, cols], cols) + turned_back(tail.T[0:64], cols)
        s.dd[4 * i : 4 * i + 4, :, 0:128] = (
            jnp.concatenate(both, axis=0).T.astype(BF).reshape(4, 64, 128)
        )
        s.dd[4 * i : 4 * i + 4, :, 128:256] = tail.astype(BF).reshape(4, 64, 128)
    for n in range(8):
        for j in range(2):
            s.d_own[2 * n + j] = s.dd[block_of(k, n, j)]
            s.d_away[2 * n + j] = s.dd[block_of(1 - k, n, j)]
    d_sent = send(s.d_away, s.d_got, KC)

    dhat = RowSum(
        send, s.dhat, s.dhat_rz, s.dhat_ry, s.dhat_t, s.dhat_rt, s.dhat_w, s.dhat_rw
    )
    d_sent.wait_recv()
    for m in (2, 3, 1, 0):
        rows = slice(m * 256, m * 256 + 256)
        quads = slice(4 * m, 4 * m + 4)
        tiles = []
        for at in (slice(0, 128), slice(128, 256)):
            own = s.d_own[quads, :, at].reshape(256, 128).astype(F32)
            got = s.d_got[quads, :, at].reshape(256, 128).astype(F32)
            tiles.append((jnp.where(k == 0, own, got), jnp.where(k == 0, got, own)))
        (p_0, p_1), (r_0, r_1) = tiles
        turned = jnp.concatenate(
            [
                jnp.where(low, p_0, roll(p_1, 64)),
                jnp.where(low, roll(p_0, 64), p_1),
                jnp.where(low, roll(r_0, 64), r_1),
            ],
            axis=1,
        )
        turned_low = turned.astype(BF)
        s.dtr[rows, :] = turned_low
        d_first = nt(turned_low, s.was[:, 0:384])
        before = s.dhat[2 * m : 2 * m + 2].reshape(256, 1024).astype(F32)
        s.dhat[2 * m : 2 * m + 2] = (
            (before + d_first * g1[...]).astype(BF).reshape(2, 128, 1024)
        )
        dhat.start(2 * m)
        dhat.start(2 * m + 1)
        s.sm[0:1, :] += down(d_first * x_hat_of(m))
        s.sm[1:2, :] += down(d_first)
        s.sm[5:6, 0:384] += down(turned)

    sm_core = send(s.sm, s.sm_r, KC)
    s.slope[:, 0:384] = tn(s.first[...].reshape(1024, 1024), s.dtr[...])
    s.go[...] = tn(s.attn[...], s.gs[...].reshape(1024, 1024))
    for kk in range(2):
        for ff in range(8):
            at = [(tt * 2 + kk) * 64 + ff * 8 for tt in range(8)]
            r = (kk * 8 + ff) * 8
            s.ga[kk, ff, :, 0:384] = jnp.concatenate(
                [s.slope[q : q + 8, 0:384] for q in at], axis=0
            ).astype(BF)
            s.ga[kk, ff, :, 384:512] = jnp.concatenate(
                [s.go[r : r + 8, j * 128 : j * 128 + 128] for j in range(8)], axis=0
            ).astype(BF)
    ga.core(s.ga)
    gm.along_z()
    sm_core.wait_recv()
    s.sm_u[...] = s.sm[...] + s.sm_r[...]
    sm_x = [send(s.sm_u, s.sm_ru.at[j], XS[i]) for j, i in enumerate(NEAR_FIRST)]
    ga.along_x()
    total = gm.total()
    for j in range(8):
        s.gm_f[j] = total[j * 8 : j * 8 + 8, :]
    gsw_o[:, 0:512] = total[64:96, :]
    gsw_o[:, 512:1024] = total[96:128, :]
    gm.to_owners()
    wait(sm_x)
    s.sm_v[...] = s.sm_u[...] + s.sm_ru[0] + s.sm_ru[1] + s.sm_ru[2]
    sm_zh = send(s.sm_v, s.sm_rv, ZH)
    act_o[...] = (s.xs[0].astype(F32) + bias[...] + act.end()).astype(BF)
    dhat.middle()
    ga.along_z()
    sm_zh.wait_recv()
    total = s.sm_v[...] + s.sm_rv[...]
    for j in range(8):
        s.sm_f[j, 0:4, :] = total[0:4, j * 128 : j * 128 + 128]
        s.sm_f[j, 4:5, :] = total[5:6, 0:128]
        s.sm_f[j, 5:6, :] = total[5:6, 128:256]
        s.sm_f[j, 6:7, :] = total[4:5, j * 128 : j * 128 + 128]
        s.sm_f[j, 7:8, :] = total[5:6, 256:384]
    small_o[8:12, :] = jnp.concatenate(
        [total[5:6, 384 + j * 128 : 512 + j * 128] for j in range(4)], axis=0
    )
    small_o[12:16, :] = jnp.zeros((4, 128), F32)
    sm = WeightSum(send, me, F32, None, None, None, None, None, s.sm_f, s.sm_rf)
    sm.to_owners()
    total = ga.total()
    for j in range(8):
        s.ga_f[j] = total[j * 8 : j * 8 + 8, 0:384]
        gow_o[:, j * 128 : j * 128 + 128] = total[j * 8 : j * 8 + 8, 384:512]
    ga.to_owners()
    d_hat = dhat.end()
    inv = s.invs[0:128, :]
    x_hat = (s.xs[0].astype(F32) - s.mus[0:128, :]) * inv
    tok_o[...] = s.gs[0].astype(F32) + inv * (
        d_hat
        - jnp.mean(d_hat, axis=1, keepdims=True)
        - x_hat * jnp.mean(d_hat * x_hat, axis=1, keepdims=True)
    )
    gm.wait()
    for n in range(8):
        gew_o[:, pl.ds(pl.multiple_of(chip_at(n) * 512, 512), 512)] = s.gm_rf[n]
    sm.wait()
    total = s.sm_rf[0]
    for n in range(1, 8):
        total += s.sm_rf[n]
    small_o[0:4, :] = total[0:4, :]
    source = lax.rem(2 * t + k, 8)
    bias_rows = jnp.zeros((2, 128), F32)
    for n in range(8):
        bias_rows = jnp.where(chip_at(n) == source, s.sm_rf[n, 4:6, :], bias_rows)
    small_o[4:5, :] = jnp.where(a == 0, bias_rows[0:1], bias_rows[1:2])
    small_o[5:6, :] = s.sm_f[t, 6:7, :]
    small_o[6:7, :] = s.sm_f[t, 7:8, :]
    small_o[7:8, :] = jnp.zeros((1, 128), F32)
    ga.wait()
    for n in range(8):
        for o in range(3):
            at = pl.ds(pl.multiple_of(o * 1024 + chip_at(n) * 128, 128), 128)
            gtw_o[:, at] = s.ga_rf[n, :, o * 128 : o * 128 + 128]
    send.finish()


def block(pairs, pos, x, g, tw, ow, ew, sw, tb, eb, g1, b1, g2, b2, bias):
    return pl.pallas_call(
        block_kernel,
        out_shape=(
            jax.ShapeDtypeStruct((128, 1024), BF),
            jax.ShapeDtypeStruct((128, 1024), F32),
            jax.ShapeDtypeStruct((8, 3072), F32),
            jax.ShapeDtypeStruct((8, 4096), F32),
            jax.ShapeDtypeStruct((8, 1024), F32),
            jax.ShapeDtypeStruct((32, 1024), F32),
            jax.ShapeDtypeStruct((16, 128), F32),
        ),
        in_specs=[pl.BlockSpec(memory_space=pltpu.SMEM), VM] + [ANY] * 6 + [VM] * 7,
        out_specs=(VM,) * 7,
        scratch_shapes=[pltpu.VMEM(shape, kind) for _, shape, kind in SCRATCH]
        + [
            pltpu.SemaphoreType.DMA((COPIES,)),
            pltpu.SemaphoreType.DMA((COPIES,)),
            pltpu.SemaphoreType.DMA((LOADS,)),
            pltpu.SMEM((32,), jnp.int32),
        ],
        compiler_params=pltpu.CompilerParams(
            collective_id=0, has_side_effects=True, vmem_limit_bytes=62 * MIB
        ),
        name="block",
    )(pairs, pos, x, g, tw, ow, ew, sw, tb, eb, g1, b1, g2, b2, bias)


def shards(
    tokens_in,
    positions,
    block_pairs,
    first_gain,
    first_bias,
    second_gain,
    second_bias,
    triple_weight,
    triple_bias,
    output_weight,
    output_bias,
    expand_weight,
    expand_bias,
    shrink_weight,
    shrink_bias,
    cotangent,
):
    c = lax.axis_index("ctx")
    k = c % 2
    x, g = tokens_in.reshape(128, 1024), cotangent.reshape(128, 1024)

    def cut(v, at, size, dim):
        return lax.dynamic_slice_in_dim(v, at, size, dim)

    def line(v):
        return v.reshape(1, -1)

    act, tok, gtw, gew, gow, gsw, small = block(
        block_pairs.T,
        positions,
        x,
        g,
        triple_weight,
        output_weight,
        expand_weight,
        shrink_weight,
        line(triple_bias),
        line(expand_bias),
        line(first_gain),
        line(first_bias),
        line(second_gain),
        line(second_bias),
        line(output_bias + shrink_bias),
    )
    f = lax.axis_index("fsdp")
    eight = cut(small, k * 64 + f * 8, 8, 1)
    sixteen = cut(small[4], f * 16, 16, 0)
    wide = cut(small[8:12].reshape(512), k * 256 + f * 32, 32, 0)
    return (
        act.reshape(tokens_in.shape),
        tok.reshape(tokens_in.shape),
        eight[0],
        eight[1],
        eight[2],
        eight[3],
        gtw,
        sixteen,
        eight[6],
        gow,
        eight[5],
        gew,
        wide,
        gsw,
        eight[5],
    )


def solution(mesh):
    return jax.shard_map(
        shards,
        mesh=mesh,
        in_specs=(
            P("fsdp", "ctx", None, None, None),
            P("fsdp", None),
            P(),
            P(),
            P(),
            P(),
            P(),
            P("fsdp", None),
            P(),
            P(None, "fsdp"),
            P(),
            P("fsdp", None),
            P(),
            P(None, "fsdp"),
            P(),
            P("fsdp", "ctx", None, None, None),
        ),
        out_specs=(
            P("fsdp", "ctx", None, None, None),
            P("fsdp", "ctx", None, None, None),
            P(("ctx", "fsdp")),
            P(("ctx", "fsdp")),
            P(("ctx", "fsdp")),
            P(("ctx", "fsdp")),
            P(("ctx", "fsdp"), None),
            P(("ctx", "fsdp")),
            P(("ctx", "fsdp")),
            P(("ctx", "fsdp"), None),
            P(("ctx", "fsdp")),
            P(("ctx", "fsdp"), None),
            P(("ctx", "fsdp")),
            P(("ctx", "fsdp"), None),
            P(("ctx", "fsdp")),
        ),
        check_vma=False,
    )
```

time: 2040 us -> 116 us (0.06)
  waiting for transfers between devices: 1660 us -> 0 us
  matrix products: 109 us -> 0 us
  local copies, waits for them, and re-layouts: 115 us -> 10.8 us
  Pallas kernels: 0 us -> 104 us
  blocking collectives: 80.5 us -> 0 us
  other arithmetic: 43.5 us -> 0.59 us
    reduce_scatter x4 -> x0, waiting for transfers between devices: 1350 us -> none  [the longest x1 727 us: scatter_lines(): own = lax.psum_scatter(lines, axis, scatter_dimension=0, tiled=True)]
    all_gather x5 -> x0, waiting for transfers between devices: 316 us -> none  [the longest x1 133 us: in_one_piece(): lax.all_gather(both, axis, axis=dim, tiled=True)]
    dot_general x18 -> x0, matrix products: 109 us -> none  [the longest x4 24 us: times_t(): lax.dot_general(left, right, (((1,), (1,)), ((), ())), preferred_element_...]
    pallas_call x0 -> x1, Pallas kernels: none -> 104 us  [block(): pl.pallas_call(block_kernel, out_shape=(jax.ShapeDtypeStruct((128, 1024),...]
    unnamed x1 -> x0, blocking collectives: 80.5 us -> none
    reshape x3 -> x1, local copies, waits for them, and re-layouts: 42.3 us -> 0.68 us  [shards(): wide = cut(small[8:12].reshape(512), k * 256 + f * 32, 32, 0)]
  transfers between devices with their start and end apart: 9 -> 0, of which waited for: 8 -> 0; matrix products, arithmetic and copies ran while one was open for 13% -> 0% of each run, Pallas kernels for 0% -> 0%
where the time goes in v3:
time: 116 us
  Pallas kernels  104 us (90%)
  local copies, waits for them, and re-layouts  10.8 us (9%)
    pallas_call x1, Pallas kernels, block(): pl.pallas_call(block_kernel, out_shape=(jax.ShapeDtypeStruct((128, 1024),...  104 us
    unnamed x23, local copies, waits for them, and re-layouts  6.81 us

profile of v3, /device:TPU:0, one launch (start us, length us, event | category | flops | bytes accessed | tf_op | source)
XLA Modules:
  0.0 115.7 jit_solution(3514023583973147467)
XLA Ops:
  0.7 0.0 copy-start.6
  0.7 0.0 copy-start.5
  0.7 0.7 copy-done.6
  1.3 0.0 copy-done.5
  1.4 0.6 add.22
  2.0 103.5 %block.1 = (bf16[128,1024]{1,0:T(8,128)(2,1)}, f32[128,1024]{1,0:T(8,128)}, f32[8,3072]{1,0:T(8,128)}, f32[8,4096]{1,0:T(8,128)}, f32[8,1024]{1,0:T(8,128)}, /*index=5*/f32[32,1024]{1,0:T(8,128)}, f32[16,128]{1,0:T(8,128)}) custom-call(s32[2,16]{1,0:T(2,128)} %bitcast.39, s32[1,2048]{1,0:T(1,128)} %pos.1, bf16[128,1024]{1,0:T(8,128)(2,1)} %bitcast.29, ...), custom_call_target="tpu_custom_call" | custom-call | tf_op jit(solution)/shard_map/block/pallas_call | solution.py:776
  105.5 0.0 copy-start
  105.5 1.5 %dynamic-slice_bitcast_fusion = (f32[8]{0:T(128)S(1)}, f32[8]{0:T(128)}, f32[8]{0:T(128)}, f32[8]{0:T(128)}, f32[8]{0:T(128)}, /*index=5*/f32[8]{0:T(128)}) fusion(f32[16,128]{1,0:T(8,128)} %get-tuple-element.24, s32[]{:T(128)S(6)} %add.33, s32[]{:T(128)S(6)} %select_n.17, s32[]{:T(128)S(6)} %add.32, s32[]{:T(128)S(6)} %add.31, s32[]{:T(128)S(6)} %add.30, ...), kind=kLoop, calls=%fused_computation.1 | loop fusion | bytes 408 | tf_op jit(solution)/shard_map/squeeze | solution.py:863
  107.0 0.0 copy-start.7
  107.0 0.7 slice_bitcast_fusion
  107.7 0.6 dynamic_slice.14
  108.3 0.7 slice.29
  109.0 0.6 dynamic-slice_bitcast_fusion.6
  109.5 0.0 copy-done.7
  109.6 0.5 copy.38
  110.1 1.7 %copy.39 = bf16[1,1,2,64,1024]{4,3,2,1,0:T(8,128)(2,1)} copy(bf16[1,1,2,64,1024]{4,3,2,1,0:T(8,128)(2,1)} %bitcast.31) | data formatting | bytes 524288
  111.7 0.0 copy-done
  111.7 0.0 copy-start.3
  111.7 0.8 copy.40
  112.5 0.2 copy-done.3
  112.7 0.0 copy-start.4
  112.7 0.0 copy-start.2
  112.7 0.6 copy.41
  113.3 0.1 copy-done.4
  113.5 0.6 copy.42
  114.1 0.0 copy-done.2
  114.1 0.0 copy-start.1
  114.1 0.7 copy.43
  114.7 0.3 copy-done.1
  115.0 0.7 copy.44
Async XLA Ops:
  0.7 0.7 copy-start.6
  0.7 0.7 copy-start.5
  105.5 6.2 %copy-start = (f32[128,1024]{1,0:T(8,128)S(1)}, f32[128,1024]{1,0:T(8,128)}, u32[]{:S(2)}) copy-start(f32[128,1024]{1,0:T(8,128)} %get-tuple-element.23) | copy-start | bytes 1572868
  107.0 2.5 %copy-start.7 = (f32[8]{0:T(128)}, f32[8]{0:T(128)S(1)}, u32[]{:S(2)}) copy-start(f32[8]{0:T(128)S(1)} %get-tuple-element.90) | copy-start | bytes 100
  111.7 1.0 copy-start.3
  112.7 0.8 copy-start.4
  112.7 1.4 %copy-start.2 = (f32[8,4096]{1,0:T(8,128)S(1)}, f32[8,4096]{1,0:T(8,128)}, u32[]{:S(2)}) copy-start(f32[8,4096]{1,0:T(8,128)} %get-tuple-element.91) | copy-start | bytes 393220
  114.1 1.0 copy-start.1

commit v4 on v3

--- a/solution.py
+++ b/solution.py
@@ -101,8 +101,9 @@
 VM = pl.BlockSpec(memory_space=pltpu.VMEM)
 
 
-COPIES = 45 + 22 + 16 + 10 + 5 + 21 + 28
+COPIES = 60 + 28 + 10 + 28 + 10 + 5 + 21
 LOADS = 8
+SPLIT = 32
 TOK = (8, 128, 1024)
 SCRATCH = (
     ("xs", TOK, BF),
@@ -123,11 +124,9 @@
     ("th", (16, 64, 256), BF),
     ("pd", (32, 64, 128), BF),
     ("td", (16, 64, 128), BF),
-    ("kq", (2048, 128), BF),
+    ("kv", (2048, 128), BF),
     ("qz", (2048, 128), BF),
-    ("vz", (2048, 128), BF),
-    ("vt", (64, 2048), BF),
-    ("kt", (64, 2048), BF),
+    ("kvt", (128, 2048), BF),
     ("dt", (64, 2048), BF),
     ("sc", (2048, TILE), F32),
     ("es", (36, TILE, TILE), BF),
@@ -152,12 +151,12 @@
     ("act_w", (64, 1024), BF),
     ("act_rw", (64, 1024), BF),
     ("dhat", TOK, BF),
-    ("dhat_rz", (4, 64, 1024), BF),
-    ("dhat_ry", (2, 3, 64, 1024), BF),
-    ("dhat_t", (4, 64, 1024), BF),
-    ("dhat_rt", (3, 64, 1024), BF),
-    ("dhat_w", (64, 1024), BF),
-    ("dhat_rw", (64, 1024), BF),
+    ("dhat_rz", (4, SPLIT, 1024), BF),
+    ("dhat_ry", (2, 3, 128 - SPLIT, 1024), BF),
+    ("dhat_t", (4, SPLIT, 1024), BF),
+    ("dhat_rt", (3, SPLIT, 1024), BF),
+    ("dhat_w", (128 - SPLIT, 1024), BF),
+    ("dhat_rw", (128 - SPLIT, 1024), BF),
     ("gsh", (512, 1024), F32),
     ("gm", (2, 8, 128, 512), BF),
     ("gm_r", (8, 128, 512), BF),
@@ -195,27 +194,28 @@
 class RowSum:
     def __init__(self, send, src, rz, ry, t, rt, w, rw):
         self.send, self.src = send, src
+        self.zr, self.yr = slice(0, rz.shape[1]), slice(rz.shape[1], 128)
         self.rz, self.ry, self.t, self.rt, self.w, self.rw = rz, ry, t, rt, w, rw
         self.z, self.y, self.on = {}, {}, []
 
     def start(self, n):
         da, db = OFFS[n]
         if da:
-            self.z[n - 4] = self.send(self.src.at[n, ZR], self.rz.at[n - 4], ZL)
+            self.z[n - 4] = self.send(self.src.at[n, self.zr], self.rz.at[n - 4], ZL)
         if db:
             j = NEAR_FIRST.index(db)
-            self.y[n] = self.send(self.src.at[n, YR], self.ry.at[da, j], YS[db])
+            self.y[n] = self.send(self.src.at[n, self.yr], self.ry.at[da, j], YS[db])
 
     def middle(self):
         for m in (1, 2, 3):
             self.z[m].wait_recv()
-            self.t[m] = (self.src[m, ZR].astype(F32) + self.rz[m].astype(F32)).astype(BF)
+            self.t[m] = (self.src[m, self.zr].astype(F32) + self.rz[m].astype(F32)).astype(BF)
             db = OFFS[m][1]
             j = NEAR_FIRST.index(db)
             self.on.append(self.send(self.t.at[m], self.rt.at[j], YS[db]))
         for n in (5, 6, 7):
             self.y[n].wait_recv()
-        total = self.src[4, YR].astype(F32)
+        total = self.src[4, self.yr].astype(F32)
         for j in range(3):
             total += self.ry[1, j].astype(F32)
         self.w[...] = total.astype(BF)
@@ -227,8 +227,8 @@
             self.y[n].wait_recv()
         for copy in self.on:
             copy.wait_recv()
-        upper = self.src[0, ZR].astype(F32) + self.rz[0].astype(F32)
-        lower = self.src[0, YR].astype(F32) + self.rw[...].astype(F32)
+        upper = self.src[0, self.zr].astype(F32) + self.rz[0].astype(F32)
+        lower = self.src[0, self.yr].astype(F32) + self.rw[...].astype(F32)
         for j in range(3):
             upper += self.rt[j].astype(F32)
             lower += self.ry[0, j].astype(F32)
@@ -287,7 +287,7 @@
 
 
 def block_kernel(
-    pairs, pos, x, g, tw, ow, ew, sw, tb, eb, g1, b1, g2, b2, bias,
+    pairs, pos, x, g, tw, ow, ew, sw, tb, eb, g1, b1, g2, b2, ob, sb,
     act_o, tok_o, gtw_o, gew_o, gow_o, gsw_o, small_o, *scratch,
 ):
     s = Refs()
@@ -310,7 +310,8 @@
     def pieces(ff):
         rows = pl.ds(pl.multiple_of(ff * 128 + k * 64, 64), 64)
         return (
-            s.was.at[rows],
+            s.was.at[rows, 0:384],
+            s.was.at[rows, 384:896],
             s.wos.at[pl.ds(pl.multiple_of(k * 64, 64), 64), cols_at(ff)],
             s.wss.at[pl.ds(pl.multiple_of(k * 256, 256), 256), cols_at(ff)],
         )
@@ -323,8 +324,8 @@
             s.was.at[mine, pl.ds(o * 128, 128)],
         )
     load(ew.at[half, pl.ds(pl.multiple_of(t * 512, 512), 512)], s.was.at[mine, pl.ds(384, 512)])
-    load(ow.at[pl.ds(pl.multiple_of(t * 128 + k * 64, 64), 64)], pieces(f)[1])
-    load(sw.at[pl.ds(pl.multiple_of(t * 512 + k * 256, 256), 256)], pieces(f)[2])
+    load(ow.at[pl.ds(pl.multiple_of(t * 128 + k * 64, 64), 64)], pieces(f)[2])
+    load(sw.at[pl.ds(pl.multiple_of(t * 512 + k * 256, 256), 256)], pieces(f)[3])
     load(x, s.xs.at[0])
     load(g, s.gs.at[0])
     barrier(me, [*(chips(n) for n in range(1, 8)), *XS.values(), ZH, KC])
@@ -338,8 +339,11 @@
             copy.wait_recv()
 
     def tokens_out(src, dst):
-        z = [send(src.at[rows], dst.at[4, rows], ZL) for rows in (ZR, YR)]
-        y = {i: send(src, dst.at[origin(0, i)], YS[i]) for i in NEAR_FIRST}
+        z = [send(src.at[ZR], dst.at[4, ZR], ZL)]
+        y = {i: [send(src.at[YR], dst.at[origin(0, i), YR], YS[i])] for i in NEAR_FIRST}
+        z.append(send(src.at[YR], dst.at[4, YR], ZL))
+        for i in NEAR_FIRST:
+            y[i].append(send(src.at[ZR], dst.at[origin(0, i), ZR], YS[i]))
         return z, y
 
     def tokens_on_y(z, dst):
@@ -349,16 +353,19 @@
     def tokens_on_z(y, dst):
         on = {}
         for i in NEAR_FIRST:
-            y[i].wait_recv()
+            y[i][0].wait_recv()
             on[i] = send(dst.at[origin(0, i), YR], dst.at[origin(1, i), YR], ZL)
         return on
 
     for copy in local:
         copy.wait()
-    wz = send_pieces(f, ZH)
-    wx = {i: send_pieces(f, XS[i]) for i in NEAR_FIRST}
+    ways = {0: ZH, **XS}
+    w_own = {i: [send(pieces(f)[0], pieces(f)[0], ways[i])] for i in (0, *NEAR_FIRST)}
     x_z, x_y = tokens_out(x, s.xs)
-    weights = send_pieces(f, KC)
+    for i in (0, *NEAR_FIRST):
+        w_own[i] += [send(ref, ref, ways[i]) for ref in pieces(f)[1:]]
+    wz, wx = w_own[0], w_own
+    weights = [send_pieces(f, KC)]
 
     def chip_at(n):
         da, db = OFFS[n]
@@ -406,28 +413,15 @@
 
     norm(0)
     fz = xx * 2 + (1 - h)
-    wait(wz)
-    wxz = {i: send_pieces(fz, XS[i]) for i in NEAR_FIRST}
-    weights += send_pieces(fz, KC)
+    wz[0].wait_recv()
+    wxz = {i: [send(pieces(fz)[0], pieces(fz)[0], XS[i])] for i in NEAR_FIRST}
     x_yz = tokens_on_y(x_z, s.xs)
     x_zy = tokens_on_z(x_y, s.xs)
+    wait(wz[1:])
+    for i in NEAR_FIRST:
+        wxz[i] += [send(ref, ref, XS[i]) for ref in pieces(fz)[1:]]
+    weights.append(send_pieces(fz, KC))
     g_z, g_y = tokens_out(g, s.gs)
-    for n in (1, 2, 3):
-        norm(n)
-    for i in NEAR_FIRST:
-        wait(wx[i])
-        weights += send_pieces(lax.rem(xx + 4 - i, 4) * 2 + h, KC)
-    x_z[1].wait_recv()
-    norm(4)
-    for i in NEAR_FIRST:
-        wait(wxz[i])
-        weights += send_pieces(lax.rem(xx + 4 - i, 4) * 2 + (1 - h), KC)
-    for i, n in ((3, 5), (1, 6), (2, 7)):
-        x_yz[i].wait_recv()
-        x_zy[i].wait_recv()
-        norm(n)
-    g_yz = tokens_on_y(g_z, s.gs)
-    wait(weights)
 
     low = lanes((256, 128)) < 64
     low128 = lanes((16, 128)) < 64
@@ -465,11 +459,12 @@
         left = s.first[2 * m : 2 * m + 2].reshape(256, 1024)
         triple = nn(left, s.was[:, 0:384]) + triple_bias
         query, key, value = turn(triple[:, 0:128]), turn(triple[:, 128:256]), triple[:, 256:384]
+        query *= SCALE
         zeros = jnp.zeros_like(value)
         return deal(
             (
-                (jnp.where(low, query, roll(key, 64)), jnp.where(low, roll(query, 64), key)),
-                (jnp.where(low, value, zeros), jnp.where(low, roll(value, 64), zeros)),
+                (jnp.where(low, key, roll(value, 64)), jnp.where(low, roll(key, 64), value)),
+                (jnp.where(low, query, zeros), jnp.where(low, roll(query, 64), zeros)),
             ),
             s.pk,
             s.th,
@@ -477,10 +472,7 @@
             m,
         )
 
-    heads_in = [attend_in(m) for m in range(4)]
-    g_zy = tokens_on_z(g_y, s.gs)
-
-    for m in range(4):
+    def forward_in(m):
         rows = slice(m * 256, m * 256 + 256)
         u = nn(s.second[rows, :], s.was[:, 384:896]) + expand_bias
         cdf = 0.5 * (1.0 + lax.erf(u * math.sqrt(0.5)))
@@ -488,23 +480,46 @@
         s.hidden[rows, :] = (u * cdf).astype(BF)
         s.slope[rows, :] = cdf + u * pdf
 
+    def weights_on(i, which, hh):
+        wait(which[i])
+        weights.append(send_pieces(lax.rem(xx + 4 - i, 4) * 2 + hh, KC))
+
+    for i, n in ((3, 1), (1, 2), (2, 3)):
+        x_y[i][1].wait_recv()
+        norm(n)
+    for i in NEAR_FIRST:
+        weights_on(i, wx, h)
+    x_z[1].wait_recv()
+    norm(4)
+    for i in NEAR_FIRST:
+        weights_on(i, wxz, 1 - h)
+    for copies in weights:
+        copies[0].wait_recv()
+    heads_in = [attend_in(0), attend_in(1)]
+    for copies in weights:
+        wait(copies[1:])
+    forward_in(0)
+    forward_in(1)
+    g_yz = tokens_on_y(g_z, s.gs)
+    for i, n in ((3, 5), (1, 6), (2, 7)):
+        x_yz[i].wait_recv()
+        x_zy[i].wait_recv()
+        norm(n)
+    heads_in += [attend_in(2), attend_in(3)]
+    forward_in(2)
+    forward_in(3)
+
     wait(heads_in)
-    low64 = lanes((64, 128)) < 64
-
     def place(j, _):
         at = pl.ds(pl.multiple_of(j * 64, 64), 64)
-        both = s.pk[inv_slot[j], :, 0:128].astype(F32)
-        value = s.pk[inv_slot[j], :, 128:256].astype(F32)
-        s.kq[at, :] = roll(both, 64).astype(BF)
-        s.qz[at, :] = jnp.where(low64, both * SCALE, 0.0).astype(BF)
-        s.vz[at, :] = roll(value, 64).astype(BF)
+        s.kv[at, :] = s.pk[inv_slot[j], :, 0:128]
+        s.qz[at, :] = s.pk[inv_slot[j], :, 128:256]
         return 0
 
-    lax.fori_loop(0, 32, place, 0)
+    lax.fori_loop(0, 32, place, 0, unroll=4)
     for i in range(8):
         cols = slice(i * TILE, i * TILE + TILE)
-        s.kt[:, cols] = s.kq[cols, :].astype(F32).T[0:64].astype(BF)
-        s.vt[:, cols] = s.vz[cols, :].astype(F32).T[64:128].astype(BF)
+        s.kvt[:, cols] = s.kv[cols, :].astype(F32).T.astype(BF)
     seen = lax.broadcasted_iota(jnp.int32, (TILE, TILE), 0) <= lanes((TILE, TILE))
 
     def folded(v, op):
@@ -524,7 +539,7 @@
         q_i = s.qz[cols, :]
         peak = None
         for j in range(i + 1):
-            score = nt(s.kq[at_tile(j), :], q_i)
+            score = nt(s.kv[at_tile(j), :], q_i)
             if j == i:
                 score = jnp.where(seen, score, -jnp.inf)
             s.sc[at_tile(j), :] = score
@@ -537,13 +552,15 @@
             total += folded(e, jnp.add)
             e_low = e.astype(BF)
             s.es[tile(i, j)] = e_low
-            mix += nn(s.vt[:, at_tile(j)], e_low)
+            mix += nn(s.kvt[64:128, at_tile(j)], e_low)
         inv = 1.0 / jnp.sum(total, axis=0, keepdims=True)
         mix *= inv
         s.rsum[i : i + 1, :] = inv
         s.mixs[:, cols] = mix
         out = jnp.concatenate([mix, jnp.zeros_like(mix)], axis=0).T
         s.ot[4 * i : 4 * i + 4] = out.astype(BF).reshape(4, 64, 128)
+        if i == 3:
+            g_zy = tokens_on_z(g_y, s.gs)
     for n in range(8):
         for j in range(2):
             s.o_own[2 * n + j] = s.ot[block_of(k, n, j)]
@@ -564,30 +581,41 @@
         act.start(2 * m)
         act.start(2 * m + 1)
 
-    g_z[1].wait_recv()
-    wait(g_yz.values())
-    wait(g_zy.values())
-    grads_in = []
-    for m in range(4):
-        dmix = nt(s.gs[2 * m : 2 * m + 2].reshape(256, 1024), s.wos[...])
-        grads_in.append(deal(((dmix, roll(dmix, 64)),), s.pd, s.td, s.pd, m))
+    def back_to_heads(p):
+        dmix = nt(s.gs[4 * p : 4 * p + 4].reshape(512, 1024), s.wos[...])
+        for m in (2 * p, 2 * p + 1):
+            part = dmix[(m - 2 * p) * 256 : (m - 2 * p) * 256 + 256]
+            grads_in.append(deal(((part, roll(part, 64)),), s.pd, s.td, s.pd, m))
 
     def x_hat_of(m):
         rows = slice(m * 256, m * 256 + 256)
         v = s.xs[2 * m : 2 * m + 2].reshape(256, 1024).astype(F32)
         return (v - s.mus[rows, :]) * s.invs[rows, :]
 
-    for m in range(4):
-        rows = slice(m * 256, m * 256 + 256)
-        grad = s.gs[2 * m : 2 * m + 2].reshape(256, 1024)
-        dexp_low = (nt(grad, s.wss[...]) * s.slope[rows, :]).astype(BF)
-        s.dexp[rows, :] = dexp_low
-        d_second = nt(dexp_low, s.was[:, 384:896])
-        s.dhat[2 * m : 2 * m + 2] = (d_second * g2[...]).astype(BF).reshape(2, 128, 1024)
-        s.sm[2:3, :] += down(d_second * x_hat_of(m))
-        s.sm[3:4, :] += down(d_second)
-        s.sm[4:5, :] += down(grad.astype(F32))
-        s.sm[5:6, 384:896] += down(dexp_low.astype(F32))
+    def forward_back(p):
+        half = slice(p * 512, p * 512 + 512)
+        d_hidden = nt(s.gs[4 * p : 4 * p + 4].reshape(512, 1024), s.wss[...])
+        s.dexp[half, :] = (d_hidden * s.slope[half, :]).astype(BF)
+        d_second = nt(s.dexp[half, :], s.was[:, 384:896])
+        for m in (2 * p, 2 * p + 1):
+            rows = slice(m * 256, m * 256 + 256)
+            part = d_second[(m - 2 * p) * 256 : (m - 2 * p) * 256 + 256]
+            s.dhat[2 * m : 2 * m + 2] = (part * g2[...]).astype(BF).reshape(2, 128, 1024)
+            s.sm[2:3, :] += down(part * x_hat_of(m))
+            s.sm[3:4, :] += down(part)
+            s.sm[4:5, :] += down(s.gs[2 * m : 2 * m + 2].reshape(256, 1024).astype(F32))
+            s.sm[5:6, 384:896] += down(s.dexp[rows, :].astype(F32))
+
+    grads_in = []
+    for i in NEAR_FIRST:
+        g_y[i][1].wait_recv()
+    back_to_heads(0)
+    forward_back(0)
+    g_z[1].wait_recv()
+    wait(g_yz.values())
+    wait(g_zy.values())
+    back_to_heads(1)
+    forward_back(1)
 
     gm = WeightSum(send, me, BF, s.gm_r, s.gm_u, s.gm_ru, s.gm_v, s.gm_rv, s.gm_f, s.gm_rf)
     ga = WeightSum(send, me, BF, s.ga_r, s.ga_u, s.ga_ru, s.ga_v, s.ga_rv, s.ga_f, s.ga_rf)
@@ -606,17 +634,9 @@
 
     wait(grads_in)
 
-    def place_back(j, _):
-        at = pl.ds(pl.multiple_of(j * 64, 64), 64)
-        s.vz[at, :] = jnp.where(
-            low64, s.pd[inv_slot[j]].astype(F32), s.vz[at, :].astype(F32)
-        ).astype(BF)
-        return 0
-
-    lax.fori_loop(0, 32, place_back, 0)
     for i in range(8):
-        cols = at_tile(i)
-        s.dt[:, cols] = s.vz[cols, :].astype(F32).T[0:64].astype(BF)
+        quad = [s.pd[inv_slot[4 * i + q]].astype(F32) for q in range(4)]
+        s.dt[:, at_tile(i)] = jnp.concatenate(quad, axis=0).T[0:64].astype(BF)
     for i in range(8):
         cols = at_tile(i)
         scaled = (s.dt[:, cols].astype(F32) * s.rsum[i : i + 1, :]).astype(BF).astype(F32)
@@ -627,14 +647,14 @@
         for j in range(i + 1):
             rows = at_tile(j)
             e_low = s.es[tile(i, j)]
-            ds = (e_low.astype(F32) * (nt(s.vz[rows, :], d_i) - inner)).astype(BF)
+            ds = (e_low.astype(F32) * (nt(s.kv[rows, :], d_i) - inner)).astype(BF)
             both = nn(jnp.concatenate([ds, e_low], axis=1), right)
             s.acc[rows, :] = both if i == j else s.acc[rows, :] + both
-            dq += nn(s.kt[:, rows], ds)
+            dq += nn(s.kvt[0:64, rows], ds)
         s.mixs[:, cols] = dq * SCALE
-        if i == 3:
+        if i == 4:
             gm.along_x()
-        if i == 6:
+        if i == 5:
             act.middle()
 
     def turned_back(v, cols):
@@ -659,6 +679,7 @@
     dhat = RowSum(
         send, s.dhat, s.dhat_rz, s.dhat_ry, s.dhat_t, s.dhat_rt, s.dhat_w, s.dhat_rw
     )
+    s.go[...] = tn(s.attn[...], s.gs[...].reshape(1024, 1024))
     d_sent.wait_recv()
     for m in (2, 3, 1, 0):
         rows = slice(m * 256, m * 256 + 256)
@@ -692,7 +713,6 @@
 
     sm_core = send(s.sm, s.sm_r, KC)
     s.slope[:, 0:384] = tn(s.first[...].reshape(1024, 1024), s.dtr[...])
-    s.go[...] = tn(s.attn[...], s.gs[...].reshape(1024, 1024))
     for kk in range(2):
         for ff in range(8):
             at = [(tt * 2 + kk) * 64 + ff * 8 for tt in range(8)]
@@ -709,18 +729,18 @@
     s.sm_u[...] = s.sm[...] + s.sm_r[...]
     sm_x = [send(s.sm_u, s.sm_ru.at[j], XS[i]) for j, i in enumerate(NEAR_FIRST)]
     ga.along_x()
+    act_o[...] = (s.xs[0].astype(F32) + (ob[...] + sb[...]) + act.end()).astype(BF)
+    wait(sm_x)
+    s.sm_v[...] = s.sm_u[...] + s.sm_ru[0] + s.sm_ru[1] + s.sm_ru[2]
+    sm_zh = send(s.sm_v, s.sm_rv, ZH)
+    dhat.middle()
+    ga.along_z()
     total = gm.total()
     for j in range(8):
         s.gm_f[j] = total[j * 8 : j * 8 + 8, :]
     gsw_o[:, 0:512] = total[64:96, :]
     gsw_o[:, 512:1024] = total[96:128, :]
     gm.to_owners()
-    wait(sm_x)
-    s.sm_v[...] = s.sm_u[...] + s.sm_ru[0] + s.sm_ru[1] + s.sm_ru[2]
-    sm_zh = send(s.sm_v, s.sm_rv, ZH)
-    act_o[...] = (s.xs[0].astype(F32) + bias[...] + act.end()).astype(BF)
-    dhat.middle()
-    ga.along_z()
     sm_zh.wait_recv()
     total = s.sm_v[...] + s.sm_rv[...]
     for j in range(8):
@@ -772,7 +792,7 @@
     send.finish()
 
 
-def block(pairs, pos, x, g, tw, ow, ew, sw, tb, eb, g1, b1, g2, b2, bias):
+def block(pairs, pos, x, g, tw, ow, ew, sw, tb, eb, g1, b1, g2, b2, ob, sb):
     return pl.pallas_call(
         block_kernel,
         out_shape=(
@@ -784,7 +804,7 @@
             jax.ShapeDtypeStruct((32, 1024), F32),
             jax.ShapeDtypeStruct((16, 128), F32),
         ),
-        in_specs=[pl.BlockSpec(memory_space=pltpu.SMEM), VM] + [ANY] * 6 + [VM] * 7,
+        in_specs=[pl.BlockSpec(memory_space=pltpu.SMEM), VM] + [ANY] * 6 + [VM] * 8,
         out_specs=(VM,) * 7,
         scratch_shapes=[pltpu.VMEM(shape, kind) for _, shape, kind in SCRATCH]
         + [
@@ -797,7 +817,41 @@
             collective_id=0, has_side_effects=True, vmem_limit_bytes=62 * MIB
         ),
         name="block",
-    )(pairs, pos, x, g, tw, ow, ew, sw, tb, eb, g1, b1, g2, b2, bias)
+    )(pairs, pos, x, g, tw, ow, ew, sw, tb, eb, g1, b1, g2, b2, ob, sb)
+
+
+def results_kernel(
+    act, tok, gtw, gew, gow, gsw, small,
+    act_o, tok_o, gtw_o, gew_o, gow_o, gsw_o,
+    fg_o, fb_o, sg_o, sb_o, tb_o, vb_o, ob_o, eb_o, hb_o,
+):
+    for src, dst in (
+        (act, act_o), (tok, tok_o), (gtw, gtw_o), (gew, gew_o), (gow, gow_o), (gsw, gsw_o)
+    ):
+        dst[...] = src[...]
+    k, f = lax.rem(lax.axis_index("ctx"), 2), lax.axis_index("fsdp")
+    rows = small[0:8, :]
+    eights = pltpu.roll(rows, lax.rem(128 - (k * 64 + f * 8), 128), 1)
+    for j, dst in enumerate((fg_o, fb_o, sg_o, sb_o)):
+        dst[...] = eights[j : j + 1, 0:8]
+    vb_o[...] = eights[6:7, 0:8]
+    ob_o[...] = eights[5:6, 0:8]
+    hb_o[...] = eights[5:6, 0:8]
+    tb_o[...] = pltpu.roll(rows, lax.rem(128 - f * 16, 128), 1)[4:5, 0:16]
+    wide = small[pl.ds(8 + k * 2 + lax.div(f, 4), 1), :]
+    wide = jnp.broadcast_to(wide, (8, 128))
+    eb_o[...] = pltpu.roll(wide, lax.rem(128 - lax.rem(f, 4) * 32, 128), 1)[0:1, 0:32]
+
+
+def results(*arrays):
+    vectors = (8, 8, 8, 8, 16, 8, 8, 32, 8)
+    return pl.pallas_call(
+        results_kernel,
+        out_shape=tuple(jax.ShapeDtypeStruct(v.shape, v.dtype) for v in arrays[:6])
+        + tuple(jax.ShapeDtypeStruct((1, n), F32) for n in vectors),
+        compiler_params=pltpu.CompilerParams(vmem_limit_bytes=62 * MIB),
+        name="results",
+    )(*arrays)
 
 
 def shards(
@@ -818,17 +872,12 @@
     shrink_bias,
     cotangent,
 ):
-    c = lax.axis_index("ctx")
-    k = c % 2
     x, g = tokens_in.reshape(128, 1024), cotangent.reshape(128, 1024)
-
-    def cut(v, at, size, dim):
-        return lax.dynamic_slice_in_dim(v, at, size, dim)
 
     def line(v):
         return v.reshape(1, -1)
 
-    act, tok, gtw, gew, gow, gsw, small = block(
+    found = block(
         block_pairs.T,
         positions,
         x,
@@ -843,28 +892,26 @@
         line(first_bias),
         line(second_gain),
         line(second_bias),
-        line(output_bias + shrink_bias),
+        line(output_bias),
+        line(shrink_bias),
     )
-    f = lax.axis_index("fsdp")
-    eight = cut(small, k * 64 + f * 8, 8, 1)
-    sixteen = cut(small[4], f * 16, 16, 0)
-    wide = cut(small[8:12].reshape(512), k * 256 + f * 32, 32, 0)
+    act, tok, gtw, gew, gow, gsw, fg, fb, sg, sb, tb, vb, ob, eb, hb = results(*found)
     return (
         act.reshape(tokens_in.shape),
         tok.reshape(tokens_in.shape),
-        eight[0],
-        eight[1],
-        eight[2],
-        eight[3],
+        fg.reshape(8),
+        fb.reshape(8),
+        sg.reshape(8),
+        sb.reshape(8),
         gtw,
-        sixteen,
-        eight[6],
+        tb.reshape(16),
+        vb.reshape(8),
         gow,
-        eight[5],
+        ob.reshape(8),
         gew,
-        wide,
+        eb.reshape(32),
         gsw,
-        eight[5],
+        hb.reshape(8),
     )
 
 

time: 116 us -> 98.4 us (0.85)
  local copies, waits for them, and re-layouts: 10.8 us -> 0 us
  Pallas kernels: 104 us -> 96.3 us
    pallas_call x1, Pallas kernels: 104 us -> 94 us  [block(): pl.pallas_call(block_kernel, out_shape=(jax.ShapeDtypeStruct((128, 1024),...]
    unnamed x23 -> x0, local copies, waits for them, and re-layouts: 6.81 us -> none
    pallas_call x0 -> x1, Pallas kernels: none -> 2.28 us  [results(): pl.pallas_call(results_kernel, out_shape=tuple((jax.ShapeDtypeStruct(v.sh...]
    squeeze x1 -> x0, local copies, waits for them, and re-layouts: 1.51 us -> none  [shards(): eight[5]]
    dynamic_slice x2 -> x0, local copies, waits for them, and re-layouts: 1.17 us -> none  [cut(): return lax.dynamic_slice_in_dim(v, at, size, dim)]
where the time goes in v4:
time: 98.4 us; the launch traced here: 97.2 us
  Pallas kernels  96.3 us (98%)
    pallas_call x1, Pallas kernels, block(): pl.pallas_call(block_kernel, out_shape=(jax.ShapeDtypeStruct((128, 1024),...  94 us
    pallas_call x1, Pallas kernels, results(): pl.pallas_call(results_kernel, out_shape=tuple((jax.ShapeDtypeStruct(v.sh...  2.28 us

profile of v4, /device:TPU:0, one launch (start us, length us, event | category | flops | bytes accessed | tf_op | source)
XLA Modules:
  0.0 97.2 jit_solution(13703145459781511444)
XLA Ops:
  0.7 94.0 %block.1 = (bf16[128,1024]{1,0:T(8,128)(2,1)}, f32[128,1024]{1,0:T(8,128)}, f32[8,3072]{1,0:T(8,128)}, f32[8,4096]{1,0:T(8,128)}, f32[8,1024]{1,0:T(8,128)}, /*index=5*/f32[32,1024]{1,0:T(8,128)}, f32[16,128]{1,0:T(8,128)}) custom-call(s32[2,16]{1,0:T(2,128)} %bitcast.32, s32[1,2048]{1,0:T(1,128)} %pos.1, bf16[128,1024]{1,0:T(8,128)(2,1)} %bitcast.22, ...), custom_call_target="tpu_custom_call" | custom-call | tf_op jit(solution)/shard_map/block/pallas_call | solution.py:796
  94.7 2.3 %results.1 = (bf16[128,1024]{1,0:T(8,128)(2,1)}, f32[128,1024]{1,0:T(8,128)}, f32[8,3072]{1,0:T(8,128)}, f32[8,4096]{1,0:T(8,128)}, f32[8,1024]{1,0:T(8,128)}, /...) custom-call(bf16[128,1024]{1,0:T(8,128)(2,1)} %get-tuple-element.37., ...), custom_call_target="tpu_custom_call" | custom-call | tf_op jit(solution)/shard_map/results/pallas_call | solution.py:848

commit v5 on v4

--- a/solution.py
+++ b/solution.py
@@ -101,9 +101,23 @@
 VM = pl.BlockSpec(memory_space=pltpu.VMEM)
 
 
-COPIES = 60 + 28 + 10 + 28 + 10 + 5 + 21
+def row_sum_scratch(name, rows):
+    low = 128 - rows
+    return (
+        (name + "_rz", (4, rows, 1024), BF),
+        (name + "_t", (4, rows, 1024), BF),
+        (name + "_tr", (2, rows // 2, 1024), BF),
+        (name + "_rt", (2, rows, 1024), BF),
+        (name + "_yr", (2, 2, low // 2, 1024), BF),
+        (name + "_u", (2, 2, low, 1024), BF),
+        (name + "_ry", (2, 2, low, 1024), BF),
+        (name + "_w", (low, 1024), BF),
+        (name + "_rw", (low, 1024), BF),
+    )
+
+
+COPIES = 60 + 2 * 17 + 10 + 2 * 17 + 5 + 5 + 5 + 21
 LOADS = 8
-SPLIT = 32
 TOK = (8, 128, 1024)
 SCRATCH = (
     ("xs", TOK, BF),
@@ -144,35 +158,25 @@
     ("attn", (1024, 128), BF),
     ("dtr", (1024, 384), BF),
     ("act", TOK, BF),
-    ("act_rz", (4, 64, 1024), BF),
-    ("act_ry", (2, 3, 64, 1024), BF),
-    ("act_t", (4, 64, 1024), BF),
-    ("act_rt", (3, 64, 1024), BF),
-    ("act_w", (64, 1024), BF),
-    ("act_rw", (64, 1024), BF),
+    *row_sum_scratch("act", 64),
     ("dhat", TOK, BF),
-    ("dhat_rz", (4, SPLIT, 1024), BF),
-    ("dhat_ry", (2, 3, 128 - SPLIT, 1024), BF),
-    ("dhat_t", (4, SPLIT, 1024), BF),
-    ("dhat_rt", (3, SPLIT, 1024), BF),
-    ("dhat_w", (128 - SPLIT, 1024), BF),
-    ("dhat_rw", (128 - SPLIT, 1024), BF),
+    *row_sum_scratch("dhat", 32),
     ("gsh", (512, 1024), F32),
-    ("gm", (2, 8, 128, 512), BF),
-    ("gm_r", (8, 128, 512), BF),
-    ("gm_u", (8, 128, 512), BF),
-    ("gm_ru", (3, 2, 128, 512), BF),
-    ("gm_v", (2, 128, 512), BF),
-    ("gm_rv", (128, 512), BF),
+    ("gm", (2, 8, 144, 512), BF),
+    ("gm_r", (8, 144, 512), BF),
+    ("gm_u", (8, 144, 512), BF),
+    ("gm_ru", (3, 2, 144, 512), BF),
+    ("gm_v", (2, 144, 512), BF),
+    ("gm_rv", (144, 512), BF),
     ("gm_f", (8, 8, 512), F32),
     ("gm_rf", (8, 8, 512), F32),
     ("go", (128, 1024), F32),
-    ("ga", (2, 8, 64, 512), BF),
-    ("ga_r", (8, 64, 512), BF),
-    ("ga_u", (8, 64, 512), BF),
-    ("ga_ru", (3, 2, 64, 512), BF),
-    ("ga_v", (2, 64, 512), BF),
-    ("ga_rv", (64, 512), BF),
+    ("ga", (2, 8, 64, 384), BF),
+    ("ga_r", (8, 64, 384), BF),
+    ("ga_u", (8, 64, 384), BF),
+    ("ga_ru", (3, 2, 64, 384), BF),
+    ("ga_v", (2, 64, 384), BF),
+    ("ga_rv", (64, 384), BF),
     ("ga_f", (8, 8, 384), F32),
     ("ga_rf", (8, 8, 384), F32),
     ("sm", (8, 1024), F32),
@@ -191,47 +195,131 @@
     pass
 
 
+def halves(rows):
+    middle = (rows.start + rows.stop) // 2
+    return {1: slice(rows.start, middle), 3: slice(middle, rows.stop)}
+
+
+class TokenGather:
+    def __init__(self, send, dst):
+        self.send, self.dst = send, dst
+        self.zy, self.far_y, self.far_z = [], [], []
+
+    def first(self):
+        send, d = self.send, self.dst
+        self.y = {i: send(d.at[0, YR], d.at[origin(0, i), YR], YS[i]) for i in (1, 3)}
+        self.z = send(d.at[0, ZR], d.at[4, ZR], ZL)
+
+    def rest(self):
+        send, d = self.send, self.dst
+        self.own_z = send(d.at[0, YR], d.at[4, YR], ZL)
+        self.own_y = {i: send(d.at[0, ZR], d.at[origin(0, i), ZR], YS[i]) for i in (1, 3)}
+
+    def relay(self, i, da, rows):
+        part, src, dst = halves(rows)[i], origin(da, i), SLOT[(da, 2)]
+        return self.send(self.dst.at[src, part], self.dst.at[dst, part], YS[i])
+
+    def second(self):
+        send, d = self.send, self.dst
+        self.far = []
+        for i in (1, 3):
+            self.y[i].wait_recv()
+            self.far.append(self.relay(i, 0, YR))
+            self.zy.append(send(d.at[origin(0, i), YR], d.at[origin(1, i), YR], ZL))
+        self.z.wait_recv()
+        self.yz = {i: send(d.at[4, ZR], d.at[origin(1, i), ZR], YS[i]) for i in (1, 3)}
+
+    def third(self):
+        send, d = self.send, self.dst
+        for copy in self.far:
+            copy.wait_recv()
+        self.zy.append(send(d.at[3, YR], d.at[7, YR], ZL))
+        for i in (1, 3):
+            self.own_y[i].wait_recv()
+            self.far_y.append(self.relay(i, 0, ZR))
+
+    def fourth(self):
+        for i in (1, 3):
+            self.yz[i].wait_recv()
+            self.far_z.append(self.relay(i, 1, ZR))
+
+    def near(self):
+        for copy in self.far_y:
+            copy.wait_recv()
+
+    def beside(self):
+        self.own_z.wait_recv()
+
+    def end(self):
+        for copy in self.zy + self.far_z:
+            copy.wait_recv()
+
+
 class RowSum:
-    def __init__(self, send, src, rz, ry, t, rt, w, rw):
-        self.send, self.src = send, src
-        self.zr, self.yr = slice(0, rz.shape[1]), slice(rz.shape[1], 128)
-        self.rz, self.ry, self.t, self.rt, self.w, self.rw = rz, ry, t, rt, w, rw
-        self.z, self.y, self.on = {}, {}, []
+    def __init__(self, send, src, rz, t, tr, rt, yr, u, ry, w, rw):
+        self.send, self.src, self.rz, self.t, self.tr, self.rt = send, src, rz, t, tr, rt
+        self.yr, self.u, self.ry, self.w, self.rw = yr, u, ry, w, rw
+        self.top, self.low = slice(0, rz.shape[1]), slice(rz.shape[1], 128)
+        self.z, self.far, self.on = {}, {}, []
 
     def start(self, n):
+        self.start_z(n)
+        self.start_far(n)
+
+    def start_z(self, n):
+        if n > 3:
+            self.z[n - 4] = self.send(self.src.at[n, self.top], self.rz.at[n - 4], ZL)
+
+    def start_far(self, n):
         da, db = OFFS[n]
-        if da:
-            self.z[n - 4] = self.send(self.src.at[n, self.zr], self.rz.at[n - 4], ZL)
-        if db:
-            j = NEAR_FIRST.index(db)
-            self.y[n] = self.send(self.src.at[n, self.yr], self.ry.at[da, j], YS[db])
-
-    def middle(self):
-        for m in (1, 2, 3):
-            self.z[m].wait_recv()
-            self.t[m] = (self.src[m, self.zr].astype(F32) + self.rz[m].astype(F32)).astype(BF)
-            db = OFFS[m][1]
-            j = NEAR_FIRST.index(db)
-            self.on.append(self.send(self.t.at[m], self.rt.at[j], YS[db]))
-        for n in (5, 6, 7):
-            self.y[n].wait_recv()
-        total = self.src[4, self.yr].astype(F32)
-        for j in range(3):
-            total += self.ry[1, j].astype(F32)
+        if db == 2:
+            for i, part in halves(self.low).items():
+                self.far[da, i] = self.send(self.src.at[n, part], self.yr.at[da, i // 2], YS[i])
+
+    def along_y(self):
+        split = halves(self.low)
+        own = halves(slice(0, self.low.stop - self.low.start))
+        for da in (1, 0):
+            for i in (1, 3):
+                n, j = SLOT[(da, i)], i // 2
+                self.far[da, i].wait_recv()
+                self.u[da, j, own[i]] = (
+                    self.src[n, split[i]].astype(F32) + self.yr[da, j].astype(F32)
+                ).astype(BF)
+                self.u[da, j, own[4 - i]] = self.src[n, split[4 - i]]
+                self.far[da, i] = self.send(self.u.at[da, j], self.ry.at[da, j], YS[i])
+
+    def after_z(self, m):
+        self.z[m].wait_recv()
+        total = self.src[m, self.top].astype(F32) + self.rz[m].astype(F32)
+        self.t[m] = total.astype(BF)
+        if m == 3:
+            self.far_t = {
+                i: self.send(self.t.at[3, part], self.tr.at[i // 2], YS[i])
+                for i, part in halves(self.top).items()
+            }
+
+    def after_y(self):
+        for i in (1, 3):
+            self.far[1, i].wait_recv()
+        total = self.src[4, self.low].astype(F32)
+        total += self.ry[1, 0].astype(F32) + self.ry[1, 1].astype(F32)
         self.w[...] = total.astype(BF)
         self.on.append(self.send(self.w, self.rw, ZL))
 
+    def last_y(self):
+        for i, part in halves(self.top).items():
+            m, j = SLOT[(0, i)], i // 2
+            self.far_t[i].wait_recv()
+            self.t[m, part] = (self.t[m, part].astype(F32) + self.tr[j].astype(F32)).astype(BF)
+            self.on.append(self.send(self.t.at[m], self.rt.at[j], YS[i]))
+
     def end(self):
-        self.z[0].wait_recv()
-        for n in (1, 2, 3):
-            self.y[n].wait_recv()
-        for copy in self.on:
+        for copy in [self.far[0, 1], self.far[0, 3], *self.on]:
             copy.wait_recv()
-        upper = self.src[0, self.zr].astype(F32) + self.rz[0].astype(F32)
-        lower = self.src[0, self.yr].astype(F32) + self.rw[...].astype(F32)
-        for j in range(3):
-            upper += self.rt[j].astype(F32)
-            lower += self.ry[0, j].astype(F32)
+        upper = self.t[0].astype(F32) + self.rt[0].astype(F32) + self.rt[1].astype(F32)
+        lower = self.src[0, self.low].astype(F32) + self.rw[...].astype(F32)
+        lower += self.ry[0, 0].astype(F32) + self.ry[0, 1].astype(F32)
         return jnp.concatenate([upper, lower], axis=0)
 
 
@@ -249,14 +337,8 @@
             copy.wait_recv()
 
     def along_x(self):
-        k, x = self.me[2], self.me[3]
-        self.wait()
-
-        def one(f, _):
-            self.u[f] = (self.src[k, f].astype(F32) + self.r[f].astype(F32)).astype(self.kind)
-            return 0
-
-        lax.fori_loop(0, 8, one, 0)
+        x = self.me[3]
+        self.core_sum()
         self.sent = []
         for j, i in enumerate(NEAR_FIRST):
             there = pl.ds(lax.rem(x + i, 4) * 2, 2)
@@ -271,6 +353,16 @@
                 total += self.ru[j, hh].astype(F32)
             self.v[hh] = total.astype(self.kind)
         self.sent = [self.send(self.v.at[1 - h], self.rv, ZH)]
+
+    def core_sum(self):
+        self.wait()
+        k = self.me[2]
+
+        def one(f, _):
+            self.u[f] = (self.src[k, f].astype(F32) + self.r[f].astype(F32)).astype(self.kind)
+            return 0
+
+        lax.fori_loop(0, 8, one, 0)
 
     def total(self):
         self.wait()
@@ -331,41 +423,30 @@
     barrier(me, [*(chips(n) for n in range(1, 8)), *XS.values(), ZH, KC])
     send = Sender(me, ss, rs)
 
-    def send_pieces(ff, off):
-        return [send(ref, ref, off) for ref in pieces(ff)]
-
     def wait(copies):
         for copy in copies:
             copy.wait_recv()
 
-    def tokens_out(src, dst):
-        z = [send(src.at[ZR], dst.at[4, ZR], ZL)]
-        y = {i: [send(src.at[YR], dst.at[origin(0, i), YR], YS[i])] for i in NEAR_FIRST}
-        z.append(send(src.at[YR], dst.at[4, YR], ZL))
-        for i in NEAR_FIRST:
-            y[i].append(send(src.at[ZR], dst.at[origin(0, i), ZR], YS[i]))
-        return z, y
-
-    def tokens_on_y(z, dst):
-        z[0].wait_recv()
-        return {i: send(dst.at[4, ZR], dst.at[origin(1, i), ZR], YS[i]) for i in NEAR_FIRST}
-
-    def tokens_on_z(y, dst):
-        on = {}
-        for i in NEAR_FIRST:
-            y[i][0].wait_recv()
-            on[i] = send(dst.at[origin(0, i), YR], dst.at[origin(1, i), YR], ZL)
-        return on
-
     for copy in local:
         copy.wait()
     ways = {0: ZH, **XS}
-    w_own = {i: [send(pieces(f)[0], pieces(f)[0], ways[i])] for i in (0, *NEAR_FIRST)}
-    x_z, x_y = tokens_out(x, s.xs)
-    for i in (0, *NEAR_FIRST):
-        w_own[i] += [send(ref, ref, ways[i]) for ref in pieces(f)[1:]]
-    wz, wx = w_own[0], w_own
-    weights = [send_pieces(f, KC)]
+    weights = {0: [], 1: []}
+
+    def weights_out(ff, part, ways):
+        refs = pieces(ff)[:1] if part == 0 else pieces(ff)[1:]
+        sent = {i: [send(ref, ref, way) for ref in refs] for i, way in ways.items()}
+        weights[part] += [send(ref, ref, KC) for ref in refs]
+        return sent
+
+    def weights_on(came, part, hh):
+        for i in NEAR_FIRST:
+            wait(came[i])
+            weights_out(lax.rem(xx + 4 - i, 4) * 2 + hh, part, {})
+
+    w_own = {0: weights_out(f, 0, ways)}
+    xt, gt = TokenGather(send, s.xs), TokenGather(send, s.gs)
+    xt.first()
+    xt.rest()
 
     def chip_at(n):
         da, db = OFFS[n]
@@ -413,15 +494,20 @@
 
     norm(0)
     fz = xx * 2 + (1 - h)
-    wz[0].wait_recv()
-    wxz = {i: [send(pieces(fz)[0], pieces(fz)[0], XS[i])] for i in NEAR_FIRST}
-    x_yz = tokens_on_y(x_z, s.xs)
-    x_zy = tokens_on_z(x_y, s.xs)
-    wait(wz[1:])
-    for i in NEAR_FIRST:
-        wxz[i] += [send(ref, ref, XS[i]) for ref in pieces(fz)[1:]]
-    weights.append(send_pieces(fz, KC))
-    g_z, g_y = tokens_out(g, s.gs)
+    wait(w_own[0][0])
+    w_z = {0: weights_out(fz, 0, XS)}
+    xt.second()
+    xt.third()
+    norm(1)
+    norm(2)
+    xt.fourth()
+    w_own[1] = weights_out(f, 1, ways)
+    gt.first()
+    gt.rest()
+    weights_on(w_own[0], 0, h)
+    weights_on(w_z[0], 0, 1 - h)
+    xt.near()
+    norm(3)
 
     low = lanes((256, 128)) < 64
     low128 = lanes((16, 128)) < 64
@@ -480,34 +566,17 @@
         s.hidden[rows, :] = (u * cdf).astype(BF)
         s.slope[rows, :] = cdf + u * pdf
 
-    def weights_on(i, which, hh):
-        wait(which[i])
-        weights.append(send_pieces(lax.rem(xx + 4 - i, 4) * 2 + hh, KC))
-
-    for i, n in ((3, 1), (1, 2), (2, 3)):
-        x_y[i][1].wait_recv()
-        norm(n)
-    for i in NEAR_FIRST:
-        weights_on(i, wx, h)
-    x_z[1].wait_recv()
+    wait(weights[0])
+    heads_in = [attend_in(0), attend_in(1)]
+    xt.beside()
     norm(4)
-    for i in NEAR_FIRST:
-        weights_on(i, wxz, 1 - h)
-    for copies in weights:
-        copies[0].wait_recv()
-    heads_in = [attend_in(0), attend_in(1)]
-    for copies in weights:
-        wait(copies[1:])
-    forward_in(0)
-    forward_in(1)
-    g_yz = tokens_on_y(g_z, s.gs)
-    for i, n in ((3, 5), (1, 6), (2, 7)):
-        x_yz[i].wait_recv()
-        x_zy[i].wait_recv()
+    xt.end()
+    for n in (5, 6, 7):
         norm(n)
     heads_in += [attend_in(2), attend_in(3)]
-    forward_in(2)
-    forward_in(3)
+    wait(w_own[1][0])
+    w_z[1] = weights_out(fz, 1, XS)
+    gt.second()
 
     wait(heads_in)
     def place(j, _):
@@ -560,16 +629,24 @@
         out = jnp.concatenate([mix, jnp.zeros_like(mix)], axis=0).T
         s.ot[4 * i : 4 * i + 4] = out.astype(BF).reshape(4, 64, 128)
         if i == 3:
-            g_zy = tokens_on_z(g_y, s.gs)
+            weights_on(w_own[1], 1, h)
+        if i == 5:
+            gt.third()
+        if i == 6:
+            weights_on(w_z[1], 1, 1 - h)
     for n in range(8):
         for j in range(2):
             s.o_own[2 * n + j] = s.ot[block_of(k, n, j)]
             s.o_away[2 * n + j] = s.ot[block_of(1 - k, n, j)]
     o_sent = send(s.o_away, s.o_got, KC)
-
-    act = RowSum(send, s.act, s.act_rz, s.act_ry, s.act_t, s.act_rt, s.act_w, s.act_rw)
+    wait(weights[1])
+    for m in range(4):
+        forward_in(m)
+    gt.fourth()
+
+    act = RowSum(send, s.act, *(getattr(s, n) for n, _, _ in row_sum_scratch("act", 64)))
     o_sent.wait_recv()
-    for m in (2, 3, 1, 0):
+    for m in (3, 1, 2, 0):
         rows = slice(m * 256, m * 256 + 256)
         own = s.o_own[4 * m : 4 * m + 4].reshape(256, 128).astype(F32)
         got = s.o_got[4 * m : 4 * m + 4].reshape(256, 128).astype(F32)
@@ -578,8 +655,8 @@
         s.attn[rows, :] = attn_low
         out = nn(attn_low, s.wos[...]) + nn(s.hidden[rows, :], s.wss[...])
         s.act[2 * m : 2 * m + 2] = out.astype(BF).reshape(2, 128, 1024)
+        act.start(2 * m + 1)
         act.start(2 * m)
-        act.start(2 * m + 1)
 
     def back_to_heads(p):
         dmix = nt(s.gs[4 * p : 4 * p + 4].reshape(512, 1024), s.wos[...])
@@ -607,13 +684,13 @@
             s.sm[5:6, 384:896] += down(s.dexp[rows, :].astype(F32))
 
     grads_in = []
-    for i in NEAR_FIRST:
-        g_y[i][1].wait_recv()
+    gt.near()
     back_to_heads(0)
     forward_back(0)
-    g_z[1].wait_recv()
-    wait(g_yz.values())
-    wait(g_zy.values())
+    act.along_y()
+    act.after_z(3)
+    gt.beside()
+    gt.end()
     back_to_heads(1)
     forward_back(1)
 
@@ -621,6 +698,7 @@
     ga = WeightSum(send, me, BF, s.ga_r, s.ga_u, s.ga_ru, s.ga_v, s.ga_rv, s.ga_f, s.ga_rf)
     s.slope[...] = tn(s.second[...], s.dexp[...])
     s.gsh[...] = tn(s.hidden[...], s.gs[...].reshape(1024, 1024))
+    s.go[...] = tn(s.attn[...], s.gs[...].reshape(1024, 1024))
     for kk in range(2):
         for ff in range(8):
             at = [(tt * 2 + kk) * 64 + ff * 8 for tt in range(8)]
@@ -630,6 +708,10 @@
             ).astype(BF)
             s.gm[kk, ff, 64:96, :] = s.gsh[own, 0:512].astype(BF)
             s.gm[kk, ff, 96:128, :] = s.gsh[own, 512:1024].astype(BF)
+            r = (kk * 8 + ff) * 8
+            s.gm[kk, ff, 128:144, :] = jnp.concatenate(
+                [s.go[r : r + 8, 0:512], s.go[r : r + 8, 512:1024]], axis=0
+            ).astype(BF)
     gm.core(s.gm)
 
     wait(grads_in)
@@ -652,10 +734,14 @@
             s.acc[rows, :] = both if i == j else s.acc[rows, :] + both
             dq += nn(s.kvt[0:64, rows], ds)
         s.mixs[:, cols] = dq * SCALE
-        if i == 4:
+        if i == 2:
             gm.along_x()
         if i == 5:
-            act.middle()
+            act.after_y()
+            act.after_z(1)
+            act.after_z(2)
+            act.last_y()
+            act.after_z(0)
 
     def turned_back(v, cols):
         cos, sin = s.cst[0:8, cols], s.cst[8:16, cols]
@@ -676,12 +762,9 @@
             s.d_away[2 * n + j] = s.dd[block_of(1 - k, n, j)]
     d_sent = send(s.d_away, s.d_got, KC)
 
-    dhat = RowSum(
-        send, s.dhat, s.dhat_rz, s.dhat_ry, s.dhat_t, s.dhat_rt, s.dhat_w, s.dhat_rw
-    )
-    s.go[...] = tn(s.attn[...], s.gs[...].reshape(1024, 1024))
+    dhat = RowSum(send, s.dhat, *(getattr(s, n) for n, _, _ in row_sum_scratch("dhat", 32)))
     d_sent.wait_recv()
-    for m in (2, 3, 1, 0):
+    for m in (3, 1, 2, 0):
         rows = slice(m * 256, m * 256 + 256)
         quads = slice(4 * m, 4 * m + 4)
         tiles = []
@@ -705,23 +788,21 @@
         s.dhat[2 * m : 2 * m + 2] = (
             (before + d_first * g1[...]).astype(BF).reshape(2, 128, 1024)
         )
+        dhat.start(2 * m + 1)
         dhat.start(2 * m)
-        dhat.start(2 * m + 1)
         s.sm[0:1, :] += down(d_first * x_hat_of(m))
         s.sm[1:2, :] += down(d_first)
         s.sm[5:6, 0:384] += down(turned)
 
     sm_core = send(s.sm, s.sm_r, KC)
     s.slope[:, 0:384] = tn(s.first[...].reshape(1024, 1024), s.dtr[...])
+    dhat.after_z(3)
+    dhat.along_y()
     for kk in range(2):
         for ff in range(8):
             at = [(tt * 2 + kk) * 64 + ff * 8 for tt in range(8)]
-            r = (kk * 8 + ff) * 8
-            s.ga[kk, ff, :, 0:384] = jnp.concatenate(
+            s.ga[kk, ff] = jnp.concatenate(
                 [s.slope[q : q + 8, 0:384] for q in at], axis=0
-            ).astype(BF)
-            s.ga[kk, ff, :, 384:512] = jnp.concatenate(
-                [s.go[r : r + 8, j * 128 : j * 128 + 128] for j in range(8)], axis=0
             ).astype(BF)
     ga.core(s.ga)
     gm.along_z()
@@ -730,17 +811,23 @@
     sm_x = [send(s.sm_u, s.sm_ru.at[j], XS[i]) for j, i in enumerate(NEAR_FIRST)]
     ga.along_x()
     act_o[...] = (s.xs[0].astype(F32) + (ob[...] + sb[...]) + act.end()).astype(BF)
-    wait(sm_x)
-    s.sm_v[...] = s.sm_u[...] + s.sm_ru[0] + s.sm_ru[1] + s.sm_ru[2]
-    sm_zh = send(s.sm_v, s.sm_rv, ZH)
-    dhat.middle()
-    ga.along_z()
+    dhat.after_z(1)
+    dhat.after_z(2)
+    dhat.last_y()
+    dhat.after_y()
     total = gm.total()
     for j in range(8):
         s.gm_f[j] = total[j * 8 : j * 8 + 8, :]
     gsw_o[:, 0:512] = total[64:96, :]
     gsw_o[:, 512:1024] = total[96:128, :]
+    gow_o[:, 0:512] = total[128:136, :]
+    gow_o[:, 512:1024] = total[136:144, :]
     gm.to_owners()
+    wait(sm_x)
+    s.sm_v[...] = s.sm_u[...] + s.sm_ru[0] + s.sm_ru[1] + s.sm_ru[2]
+    sm_zh = send(s.sm_v, s.sm_rv, ZH)
+    ga.along_z()
+    dhat.after_z(0)
     sm_zh.wait_recv()
     total = s.sm_v[...] + s.sm_rv[...]
     for j in range(8):
@@ -757,8 +844,7 @@
     sm.to_owners()
     total = ga.total()
     for j in range(8):
-        s.ga_f[j] = total[j * 8 : j * 8 + 8, 0:384]
-        gow_o[:, j * 128 : j * 128 + 128] = total[j * 8 : j * 8 + 8, 384:512]
+        s.ga_f[j] = total[j * 8 : j * 8 + 8, :]
     ga.to_owners()
     d_hat = dhat.end()
     inv = s.invs[0:128, :]

time: 98.4 us -> 96.4 us (0.980); the launches traced: 97.2 us -> 96.2 us
  no operation moved by 1% of the time
where the time goes in v5:
time: 96.4 us; the launch traced here: 96.2 us
  Pallas kernels  95.4 us (99%)
    pallas_call x1, Pallas kernels, block(): pl.pallas_call(block_kernel, out_shape=(jax.ShapeDtypeStruct((128, 1024),...  93.1 us
    pallas_call x1, Pallas kernels, results(): pl.pallas_call(results_kernel, out_shape=tuple((jax.ShapeDtypeStruct(v.sh...  2.28 us

profile of v5, /device:TPU:0, one launch (start us, length us, event | category | flops | bytes accessed | tf_op | source)
XLA Modules:
  0.0 96.2 jit_solution(13237963244191915900)
XLA Ops:
  0.7 93.1 %block.1 = (bf16[128,1024]{1,0:T(8,128)(2,1)}, f32[128,1024]{1,0:T(8,128)}, f32[8,3072]{1,0:T(8,128)}, f32[8,4096]{1,0:T(8,128)}, f32[8,1024]{1,0:T(8,128)}, /*index=5*/f32[32,1024]{1,0:T(8,128)}, f32[16,128]{1,0:T(8,128)}) custom-call(s32[2,16]{1,0:T(2,128)} %bitcast.32, s32[1,2048]{1,0:T(1,128)} %pos.1, bf16[128,1024]{1,0:T(8,128)(2,1)} %bitcast.22, ...), custom_call_target="tpu_custom_call" | custom-call | tf_op jit(solution)/shard_map/block/pallas_call | solution.py:882
  93.8 2.3 %results.1 = (bf16[128,1024]{1,0:T(8,128)(2,1)}, f32[128,1024]{1,0:T(8,128)}, f32[8,3072]{1,0:T(8,128)}, f32[8,4096]{1,0:T(8,128)}, f32[8,1024]{1,0:T(8,128)}, /...) custom-call(bf16[128,1024]{1,0:T(8,128)(2,1)} %get-tuple-element.37., ...), custom_call_target="tpu_custom_call" | custom-call | tf_op jit(solution)/shard_map/results/pallas_call | solution.py:934

commit v6 on v5

--- a/solution.py
+++ b/solution.py
@@ -188,7 +188,6 @@
     ("sm_f", (8, 8, 128), F32),
     ("sm_rf", (8, 8, 128), F32),
 )
-ZR, YR = slice(0, 64), slice(64, 128)
 
 
 class Refs:
@@ -201,19 +200,20 @@
 
 
 class TokenGather:
-    def __init__(self, send, dst):
+    def __init__(self, send, dst, rows):
         self.send, self.dst = send, dst
+        self.top, self.low = slice(0, rows), slice(rows, 128)
         self.zy, self.far_y, self.far_z = [], [], []
 
     def first(self):
         send, d = self.send, self.dst
-        self.y = {i: send(d.at[0, YR], d.at[origin(0, i), YR], YS[i]) for i in (1, 3)}
-        self.z = send(d.at[0, ZR], d.at[4, ZR], ZL)
+        self.y = {i: send(d.at[0, self.low], d.at[origin(0, i), self.low], YS[i]) for i in (1, 3)}
+        self.z = send(d.at[0, self.top], d.at[4, self.top], ZL)
 
     def rest(self):
         send, d = self.send, self.dst
-        self.own_z = send(d.at[0, YR], d.at[4, YR], ZL)
-        self.own_y = {i: send(d.at[0, ZR], d.at[origin(0, i), ZR], YS[i]) for i in (1, 3)}
+        self.own_z = send(d.at[0, self.low], d.at[4, self.low], ZL)
+        self.own_y = {i: send(d.at[0, self.top], d.at[origin(0, i), self.top], YS[i]) for i in (1, 3)}
 
     def relay(self, i, da, rows):
         part, src, dst = halves(rows)[i], origin(da, i), SLOT[(da, 2)]
@@ -224,24 +224,24 @@
         self.far = []
         for i in (1, 3):
             self.y[i].wait_recv()
-            self.far.append(self.relay(i, 0, YR))
-            self.zy.append(send(d.at[origin(0, i), YR], d.at[origin(1, i), YR], ZL))
+            self.far.append(self.relay(i, 0, self.low))
+            self.zy.append(send(d.at[origin(0, i), self.low], d.at[origin(1, i), self.low], ZL))
         self.z.wait_recv()
-        self.yz = {i: send(d.at[4, ZR], d.at[origin(1, i), ZR], YS[i]) for i in (1, 3)}
+        self.yz = {i: send(d.at[4, self.top], d.at[origin(1, i), self.top], YS[i]) for i in (1, 3)}
 
     def third(self):
         send, d = self.send, self.dst
         for copy in self.far:
             copy.wait_recv()
-        self.zy.append(send(d.at[3, YR], d.at[7, YR], ZL))
+        self.zy.append(send(d.at[3, self.low], d.at[7, self.low], ZL))
         for i in (1, 3):
             self.own_y[i].wait_recv()
-            self.far_y.append(self.relay(i, 0, ZR))
+            self.far_y.append(self.relay(i, 0, self.top))
 
     def fourth(self):
         for i in (1, 3):
             self.yz[i].wait_recv()
-            self.far_z.append(self.relay(i, 1, ZR))
+            self.far_z.append(self.relay(i, 1, self.top))
 
     def near(self):
         for copy in self.far_y:
@@ -385,7 +385,8 @@
     s = Refs()
     for (name, _, _), ref in zip(SCRATCH, scratch):
         setattr(s, name, ref)
-    ss, rs, ls, inv_slot = scratch[len(SCRATCH) :]
+    ss, rs, ls, inv_slot, os, *values = scratch[len(SCRATCH) :]
+    act_v, tok_v, gtw_v, gew_v, gow_v, gsw_v, small_v = values
     me = coords()
     a, b, k, xx, h = me
     t, f = a * 4 + b, xx * 2 + h
@@ -395,6 +396,13 @@
         copy = pltpu.make_async_copy(src, dst, ls.at[len(local)])
         copy.start()
         local.append(copy)
+
+    stored = []
+
+    def store(src, dst):
+        copy = pltpu.make_async_copy(src, dst, os.at[len(stored)])
+        copy.start()
+        stored.append(copy)
 
     def cols_at(ff):
         return pl.ds(pl.multiple_of(ff * 128, 128), 128)
@@ -444,7 +452,7 @@
             weights_out(lax.rem(xx + 4 - i, 4) * 2 + hh, part, {})
 
     w_own = {0: weights_out(f, 0, ways)}
-    xt, gt = TokenGather(send, s.xs), TokenGather(send, s.gs)
+    xt, gt = TokenGather(send, s.xs, 96), TokenGather(send, s.gs, 96)
     xt.first()
     xt.rest()
 
@@ -496,18 +504,20 @@
     fz = xx * 2 + (1 - h)
     wait(w_own[0][0])
     w_z = {0: weights_out(fz, 0, XS)}
+    w_own[1] = weights_out(f, 1, ways)
     xt.second()
     xt.third()
     norm(1)
     norm(2)
     xt.fourth()
-    w_own[1] = weights_out(f, 1, ways)
     gt.first()
     gt.rest()
     weights_on(w_own[0], 0, h)
     weights_on(w_z[0], 0, 1 - h)
     xt.near()
     norm(3)
+    wait(w_own[1][0])
+    w_z[1] = weights_out(fz, 1, XS)
 
     low = lanes((256, 128)) < 64
     low128 = lanes((16, 128)) < 64
@@ -574,9 +584,6 @@
     for n in (5, 6, 7):
         norm(n)
     heads_in += [attend_in(2), attend_in(3)]
-    wait(w_own[1][0])
-    w_z[1] = weights_out(fz, 1, XS)
-    gt.second()
 
     wait(heads_in)
     def place(j, _):
@@ -628,7 +635,9 @@
         s.mixs[:, cols] = mix
         out = jnp.concatenate([mix, jnp.zeros_like(mix)], axis=0).T
         s.ot[4 * i : 4 * i + 4] = out.astype(BF).reshape(4, 64, 128)
-        if i == 3:
+        if i == 1:
+            gt.second()
+        if i == 0:
             weights_on(w_own[1], 1, h)
         if i == 5:
             gt.third()
@@ -687,12 +696,12 @@
     gt.near()
     back_to_heads(0)
     forward_back(0)
-    act.along_y()
-    act.after_z(3)
     gt.beside()
     gt.end()
     back_to_heads(1)
     forward_back(1)
+    act.along_y()
+    act.after_z(3)
 
     gm = WeightSum(send, me, BF, s.gm_r, s.gm_u, s.gm_ru, s.gm_v, s.gm_rv, s.gm_f, s.gm_rf)
     ga = WeightSum(send, me, BF, s.ga_r, s.ga_u, s.ga_ru, s.ga_v, s.ga_rv, s.ga_f, s.ga_rf)
@@ -734,9 +743,9 @@
             s.acc[rows, :] = both if i == j else s.acc[rows, :] + both
             dq += nn(s.kvt[0:64, rows], ds)
         s.mixs[:, cols] = dq * SCALE
-        if i == 2:
+        if i == 3:
             gm.along_x()
-        if i == 5:
+        if i == 6:
             act.after_y()
             act.after_z(1)
             act.after_z(2)
@@ -796,8 +805,6 @@
 
     sm_core = send(s.sm, s.sm_r, KC)
     s.slope[:, 0:384] = tn(s.first[...].reshape(1024, 1024), s.dtr[...])
-    dhat.after_z(3)
-    dhat.along_y()
     for kk in range(2):
         for ff in range(8):
             at = [(tt * 2 + kk) * 64 + ff * 8 for tt in range(8)]
@@ -805,12 +812,15 @@
                 [s.slope[q : q + 8, 0:384] for q in at], axis=0
             ).astype(BF)
     ga.core(s.ga)
+    dhat.after_z(3)
+    dhat.along_y()
     gm.along_z()
     sm_core.wait_recv()
     s.sm_u[...] = s.sm[...] + s.sm_r[...]
     sm_x = [send(s.sm_u, s.sm_ru.at[j], XS[i]) for j, i in enumerate(NEAR_FIRST)]
     ga.along_x()
-    act_o[...] = (s.xs[0].astype(F32) + (ob[...] + sb[...]) + act.end()).astype(BF)
+    act_v[...] = (s.xs[0].astype(F32) + (ob[...] + sb[...]) + act.end()).astype(BF)
+    store(act_v, act_o)
     dhat.after_z(1)
     dhat.after_z(2)
     dhat.last_y()
@@ -818,15 +828,17 @@
     total = gm.total()
     for j in range(8):
         s.gm_f[j] = total[j * 8 : j * 8 + 8, :]
-    gsw_o[:, 0:512] = total[64:96, :]
-    gsw_o[:, 512:1024] = total[96:128, :]
-    gow_o[:, 0:512] = total[128:136, :]
-    gow_o[:, 512:1024] = total[136:144, :]
-    gm.to_owners()
+    gsw_v[:, 0:512] = total[64:96, :]
+    gsw_v[:, 512:1024] = total[96:128, :]
+    gow_v[:, 0:512] = total[128:136, :]
+    gow_v[:, 512:1024] = total[136:144, :]
+    store(gsw_v, gsw_o)
+    store(gow_v, gow_o)
     wait(sm_x)
     s.sm_v[...] = s.sm_u[...] + s.sm_ru[0] + s.sm_ru[1] + s.sm_ru[2]
     sm_zh = send(s.sm_v, s.sm_rv, ZH)
     ga.along_z()
+    gm.to_owners()
     dhat.after_z(0)
     sm_zh.wait_recv()
     total = s.sm_v[...] + s.sm_rv[...]
@@ -836,10 +848,10 @@
         s.sm_f[j, 5:6, :] = total[5:6, 128:256]
         s.sm_f[j, 6:7, :] = total[4:5, j * 128 : j * 128 + 128]
         s.sm_f[j, 7:8, :] = total[5:6, 256:384]
-    small_o[8:12, :] = jnp.concatenate(
+    small_v[8:12, :] = jnp.concatenate(
         [total[5:6, 384 + j * 128 : 512 + j * 128] for j in range(4)], axis=0
     )
-    small_o[12:16, :] = jnp.zeros((4, 128), F32)
+    small_v[12:16, :] = jnp.zeros((4, 128), F32)
     sm = WeightSum(send, me, F32, None, None, None, None, None, s.sm_f, s.sm_rf)
     sm.to_owners()
     total = ga.total()
@@ -849,56 +861,67 @@
     d_hat = dhat.end()
     inv = s.invs[0:128, :]
     x_hat = (s.xs[0].astype(F32) - s.mus[0:128, :]) * inv
-    tok_o[...] = s.gs[0].astype(F32) + inv * (
+    tok_v[...] = s.gs[0].astype(F32) + inv * (
         d_hat
         - jnp.mean(d_hat, axis=1, keepdims=True)
         - x_hat * jnp.mean(d_hat * x_hat, axis=1, keepdims=True)
     )
+    store(tok_v, tok_o)
     gm.wait()
     for n in range(8):
-        gew_o[:, pl.ds(pl.multiple_of(chip_at(n) * 512, 512), 512)] = s.gm_rf[n]
+        gew_v[:, pl.ds(pl.multiple_of(chip_at(n) * 512, 512), 512)] = s.gm_rf[n]
+    store(gew_v, gew_o)
     sm.wait()
     total = s.sm_rf[0]
     for n in range(1, 8):
         total += s.sm_rf[n]
-    small_o[0:4, :] = total[0:4, :]
+    small_v[0:4, :] = total[0:4, :]
     source = lax.rem(2 * t + k, 8)
     bias_rows = jnp.zeros((2, 128), F32)
     for n in range(8):
         bias_rows = jnp.where(chip_at(n) == source, s.sm_rf[n, 4:6, :], bias_rows)
-    small_o[4:5, :] = jnp.where(a == 0, bias_rows[0:1], bias_rows[1:2])
-    small_o[5:6, :] = s.sm_f[t, 6:7, :]
-    small_o[6:7, :] = s.sm_f[t, 7:8, :]
-    small_o[7:8, :] = jnp.zeros((1, 128), F32)
+    small_v[4:5, :] = jnp.where(a == 0, bias_rows[0:1], bias_rows[1:2])
+    small_v[5:6, :] = s.sm_f[t, 6:7, :]
+    small_v[6:7, :] = s.sm_f[t, 7:8, :]
+    small_v[7:8, :] = jnp.zeros((1, 128), F32)
+    store(small_v, small_o)
     ga.wait()
     for n in range(8):
         for o in range(3):
             at = pl.ds(pl.multiple_of(o * 1024 + chip_at(n) * 128, 128), 128)
-            gtw_o[:, at] = s.ga_rf[n, :, o * 128 : o * 128 + 128]
+            gtw_v[:, at] = s.ga_rf[n, :, o * 128 : o * 128 + 128]
+    store(gtw_v, gtw_o)
+    for copy in stored:
+        copy.wait()
     send.finish()
+
+
+RESULTS = (
+    ((128, 1024), BF),
+    ((128, 1024), F32),
+    ((8, 3072), F32),
+    ((8, 4096), F32),
+    ((8, 1024), F32),
+    ((32, 1024), F32),
+    ((16, 128), F32),
+)
 
 
 def block(pairs, pos, x, g, tw, ow, ew, sw, tb, eb, g1, b1, g2, b2, ob, sb):
     return pl.pallas_call(
         block_kernel,
-        out_shape=(
-            jax.ShapeDtypeStruct((128, 1024), BF),
-            jax.ShapeDtypeStruct((128, 1024), F32),
-            jax.ShapeDtypeStruct((8, 3072), F32),
-            jax.ShapeDtypeStruct((8, 4096), F32),
-            jax.ShapeDtypeStruct((8, 1024), F32),
-            jax.ShapeDtypeStruct((32, 1024), F32),
-            jax.ShapeDtypeStruct((16, 128), F32),
-        ),
+        out_shape=tuple(jax.ShapeDtypeStruct(*result) for result in RESULTS),
         in_specs=[pl.BlockSpec(memory_space=pltpu.SMEM), VM] + [ANY] * 6 + [VM] * 8,
-        out_specs=(VM,) * 7,
+        out_specs=(ANY,) * 7,
         scratch_shapes=[pltpu.VMEM(shape, kind) for _, shape, kind in SCRATCH]
         + [
             pltpu.SemaphoreType.DMA((COPIES,)),
             pltpu.SemaphoreType.DMA((COPIES,)),
             pltpu.SemaphoreType.DMA((LOADS,)),
             pltpu.SMEM((32,), jnp.int32),
-        ],
+            pltpu.SemaphoreType.DMA((7,)),
+        ]
+        + [pltpu.VMEM(*result) for result in RESULTS],
         compiler_params=pltpu.CompilerParams(
             collective_id=0, has_side_effects=True, vmem_limit_bytes=62 * MIB
         ),

time: 96.4 us -> 95.5 us (level)
  no operation moved by 1% of the time
where the time goes in v6:
time: 95.5 us; the launch traced here: 95.3 us
  Pallas kernels  94.5 us (99%)
    pallas_call x1, Pallas kernels, block(): pl.pallas_call(block_kernel, out_shape=tuple((jax.ShapeDtypeStruct(*resul...  92.2 us
    pallas_call x1, Pallas kernels, results(): pl.pallas_call(results_kernel, out_shape=tuple((jax.ShapeDtypeStruct(v.sh...  2.28 us

profile of v6, /device:TPU:0, one launch (start us, length us, event | category | flops | bytes accessed | tf_op | source)
XLA Modules:
  0.0 95.3 jit_solution(8186738587390840439)
XLA Ops:
  0.7 92.2 %block.1 = (bf16[128,1024]{1,0:T(8,128)(2,1)}, f32[128,1024]{1,0:T(8,128)}, f32[8,3072]{1,0:T(8,128)}, f32[8,4096]{1,0:T(8,128)}, f32[8,1024]{1,0:T(8,128)}, /*index=5*/f32[32,1024]{1,0:T(8,128)}, f32[16,128]{1,0:T(8,128)}) custom-call(s32[2,16]{1,0:T(2,128)} %bitcast.32, s32[1,2048]{1,0:T(1,128)} %pos.1, bf16[128,1024]{1,0:T(8,128)(2,1)} %bitcast.22, ...), custom_call_target="tpu_custom_call" | custom-call | tf_op jit(solution)/shard_map/block/pallas_call | solution.py:911
  92.8 2.3 %results.1 = (bf16[128,1024]{1,0:T(8,128)(2,1)}, f32[128,1024]{1,0:T(8,128)}, f32[8,3072]{1,0:T(8,128)}, f32[8,4096]{1,0:T(8,128)}, f32[8,1024]{1,0:T(8,128)}, /...) custom-call(bf16[128,1024]{1,0:T(8,128)(2,1)} %get-tuple-element.37., ...), custom_call_target="tpu_custom_call" | custom-call | tf_op jit(solution)/shard_map/results/pallas_call | solution.py:957

commit v7 on v6

--- a/solution.py
+++ b/solution.py
@@ -655,17 +655,18 @@
 
     act = RowSum(send, s.act, *(getattr(s, n) for n, _, _ in row_sum_scratch("act", 64)))
     o_sent.wait_recv()
-    for m in (3, 1, 2, 0):
-        rows = slice(m * 256, m * 256 + 256)
-        own = s.o_own[4 * m : 4 * m + 4].reshape(256, 128).astype(F32)
-        got = s.o_got[4 * m : 4 * m + 4].reshape(256, 128).astype(F32)
-        head0, head1 = jnp.where(k == 0, own, got), jnp.where(k == 0, got, own)
-        attn_low = jnp.where(low, head0, roll(head1, 64)).astype(BF)
-        s.attn[rows, :] = attn_low
-        out = nn(attn_low, s.wos[...]) + nn(s.hidden[rows, :], s.wss[...])
-        s.act[2 * m : 2 * m + 2] = out.astype(BF).reshape(2, 128, 1024)
-        act.start(2 * m + 1)
-        act.start(2 * m)
+    for p in (1, 0):
+        for m in (2 * p + 1, 2 * p):
+            rows = slice(m * 256, m * 256 + 256)
+            own = s.o_own[4 * m : 4 * m + 4].reshape(256, 128).astype(F32)
+            got = s.o_got[4 * m : 4 * m + 4].reshape(256, 128).astype(F32)
+            head0, head1 = jnp.where(k == 0, own, got), jnp.where(k == 0, got, own)
+            s.attn[rows, :] = jnp.where(low, head0, roll(head1, 64)).astype(BF)
+        half = slice(p * 512, p * 512 + 512)
+        out = nn(s.attn[half, :], s.wos[...]) + nn(s.hidden[half, :], s.wss[...])
+        s.act[4 * p : 4 * p + 4] = out.astype(BF).reshape(4, 128, 1024)
+        for n in (4 * p + 3, 4 * p + 2, 4 * p + 1, 4 * p):
+            act.start(n)
 
     def back_to_heads(p):
         dmix = nt(s.gs[4 * p : 4 * p + 4].reshape(512, 1024), s.wos[...])

time: 95.5 us -> 94.7 us (level)
  no operation moved by 1% of the time
where the time goes in v7:
time: 94.7 us; the launch traced here: 94.5 us
  Pallas kernels  93.7 us (99%)
    pallas_call x1, Pallas kernels, block(): pl.pallas_call(block_kernel, out_shape=tuple((jax.ShapeDtypeStruct(*resul...  91.4 us
    pallas_call x1, Pallas kernels, results(): pl.pallas_call(results_kernel, out_shape=tuple((jax.ShapeDtypeStruct(v.sh...  2.28 us

profile of v7, /device:TPU:0, one launch (start us, length us, event | category | flops | bytes accessed | tf_op | source)
XLA Modules:
  0.0 94.5 jit_solution(5137293675706280889)
XLA Ops:
  0.7 91.4 %block.1 = (bf16[128,1024]{1,0:T(8,128)(2,1)}, f32[128,1024]{1,0:T(8,128)}, f32[8,3072]{1,0:T(8,128)}, f32[8,4096]{1,0:T(8,128)}, f32[8,1024]{1,0:T(8,128)}, /*index=5*/f32[32,1024]{1,0:T(8,128)}, f32[16,128]{1,0:T(8,128)}) custom-call(s32[2,16]{1,0:T(2,128)} %bitcast.32, s32[1,2048]{1,0:T(1,128)} %pos.1, bf16[128,1024]{1,0:T(8,128)(2,1)} %bitcast.22, ...), custom_call_target="tpu_custom_call" | custom-call | tf_op jit(solution)/shard_map/block/pallas_call | solution.py:912
  92.1 2.3 %results.1 = (bf16[128,1024]{1,0:T(8,128)(2,1)}, f32[128,1024]{1,0:T(8,128)}, f32[8,3072]{1,0:T(8,128)}, f32[8,4096]{1,0:T(8,128)}, f32[8,1024]{1,0:T(8,128)}, /...) custom-call(bf16[128,1024]{1,0:T(8,128)(2,1)} %get-tuple-element.37., ...), custom_call_target="tpu_custom_call" | custom-call | tf_op jit(solution)/shard_map/results/pallas_call | solution.py:958
